TPU v7x, 128 devices: a whole 4x4x4 slice. The times are simulated.
128 devices in a mesh: fsdp: 8 (over x_hi, z), context: 8 (over x_lo, y), tensor: 2 (over core).
Axes of the slice: x: 4 (x_hi: 2, x_lo: 2; x = x_hi * 2 + x_lo), y: 4, z: 4, core: 2. Of those that a mesh axis runs over, the one named last changes fastest.
Arguments:
- stream: bfloat16 [1024, 16, 1024], P('context', 'fsdp'), may hold values from -6 to 6
- lengths: int32 [16], P('fsdp'), may hold values from 256 to 1024, as said below
- query_weight: bfloat16 [1024, 1024], P(('fsdp', 'context'), 'tensor'), may hold values from -0.1875 to 0.1875
- query_bias: bfloat16 [1024], P('tensor'), may hold values from -1.75 to 1.75
- key_weight: bfloat16 [1024, 1024], P(('fsdp', 'context'), 'tensor'), may hold values from -0.1875 to 0.1875
- value_weight: bfloat16 [1024, 1024], P(('fsdp', 'context'), 'tensor'), may hold values from -0.1875 to 0.1875
- value_bias: bfloat16 [1024], P('tensor'), may hold values from -0.1875 to 0.1875
- output_weight: bfloat16 [1024, 1024], P('tensor', ('fsdp', 'context')), may hold values from -3 to 3
- output_bias: bfloat16 [1024], P(('fsdp', 'context')), may hold values from -1.75 to 1.75
- first_gain: bfloat16 [1024], P(('fsdp', 'context')), may hold values from 0.5 to 1.5
- first_shift: bfloat16 [1024], P(('fsdp', 'context')), may hold values from -1.75 to 1.75
- inner_weight: bfloat16 [1024, 4096], P(('fsdp', 'context'), 'tensor'), may hold values from -0.1875 to 0.1875
- inner_bias: bfloat16 [4096], P('tensor'), may hold values from -1.75 to 1.75
- outer_weight: bfloat16 [4096, 1024], P('tensor', ('fsdp', 'context')), may hold values from -0.09375 to 0.09375
- outer_bias: bfloat16 [1024], P(('fsdp', 'context')), may hold values from -1.75 to 1.75
- second_gain: bfloat16 [1024], P(('fsdp', 'context')), may hold values from 0.5 to 1.5
- second_shift: bfloat16 [1024], P(('fsdp', 'context')), may hold values from -1.75 to 1.75
- cotangent: bfloat16 [1024, 16, 1024], P('context', 'fsdp'), may hold values from -6 to 6
Outputs:
- result: bfloat16 [1024, 16, 1024], P('context', 'fsdp')
- stream_grad: float32 [1024, 16, 1024], P('context', 'fsdp')
- grad_query_weight: float32 [1024, 1024], P(('fsdp', 'context'), 'tensor')
- grad_query_bias: float32 [1024], P('tensor')
- grad_key_weight: float32 [1024, 1024], P(('fsdp', 'context'), 'tensor')
- grad_value_weight: float32 [1024, 1024], P(('fsdp', 'context'), 'tensor')
- grad_value_bias: float32 [1024], P('tensor')
- grad_output_weight: float32 [1024, 1024], P('tensor', ('fsdp', 'context'))
- grad_output_bias: float32 [1024], P(('fsdp', 'context'))
- grad_first_gain: float32 [1024], P(('fsdp', 'context'))
- grad_first_shift: float32 [1024], P(('fsdp', 'context'))
- grad_inner_weight: float32 [1024, 4096], P(('fsdp', 'context'), 'tensor')
- grad_inner_bias: float32 [4096], P('tensor')
- grad_outer_weight: float32 [4096, 1024], P('tensor', ('fsdp', 'context'))
- grad_outer_bias: float32 [1024], P(('fsdp', 'context'))
- grad_second_gain: float32 [1024], P(('fsdp', 'context'))
- grad_second_shift: float32 [1024], P(('fsdp', 'context'))
- root_squares: float32 [2, 3], replicated
Inputs may be any that keep to these rules, and one draw needn't show every extreme that they name: `lengths`: among the 2 sequences of each index of fsdp, one, drawn from the seed, has more than 896 valid slots.
All inputs are finite; a program needn't handle non-finite values.
Results may differ from a plain program's by a relative error of at most 0.03.
Values may be sent and summed in bfloat16 or wider, within the bound.
A program may use at most 192 MiB of HBM per device.

v0:
```python
import jax
import jax.numpy as jnp
from jax import lax
from jax.experimental import pallas as pl
from jax.experimental.pallas import tpu as pltpu
from jax.sharding import PartitionSpec as P

HEAD = 64
LAYERS = 2
LANES = 128
MESH = pl.DeviceIdType.MESH

F32 = jnp.float32
BF16 = jnp.bfloat16
ROWS = 128
LIMIT = 60 * 2**20
WIDTH = 6272
QUERY, KEY, VALUE, OUT, INNER, OUTER, EXTRA = 0, 512, 1024, 1536, 2048, 4096, 6144
GROUPS = ((QUERY, OUT), (OUT, WIDTH))
ORDERS = ("zyx", "yxz", "xzy")
SHARDS = (2, 4, 2, 4)


def spec(space):
    return pl.BlockSpec(memory_space=space)


def place():
    f = lax.axis_index("fsdp")
    c = lax.axis_index("context")
    t = lax.axis_index("tensor")
    return {"x": 2 * (f // 4) + c // 4, "y": c % 4, "z": f % 4, "t": t}


def device(at):
    x = at["x"]
    return ((x // 2) * 4 + at["z"], (x % 2) * 4 + at["y"], at["t"])


def shifted(at, axis, step):
    moved = dict(at)
    moved[axis] = lax.rem(at[axis] + step + 4, 4)
    return moved


def greet(devices):
    barrier = pltpu.get_barrier_semaphore()
    for device_id in devices:
        pl.semaphore_signal(barrier, inc=1, device_id=device_id, device_id_type=MESH)
    pl.semaphore_wait(barrier, len(devices))


def neighbours(at, steps):
    return [device(shifted(at, axis, step)) for axis in "xyz" for step in steps]


def context_peers():
    f = lax.axis_index("fsdp")
    c = lax.axis_index("context")
    t = lax.axis_index("tensor")
    return [(f, lax.rem(c + d, 8), t) for d in range(1, 8)]


def remote(src, dst, send_sem, recv_sem, device_id):
    return pltpu.make_async_remote_copy(
        src_ref=src,
        dst_ref=dst,
        send_sem=send_sem,
        recv_sem=recv_sem,
        device_id=device_id,
        device_id_type=MESH,
    )


def shards(ref, at, whole, cols):
    x = at["x"]
    xh = slice(None) if "x" in whole else x // 2
    xl = slice(None) if "x" in whole else x % 2
    z = slice(None) if "z" in whole else at["z"]
    y = slice(None) if "y" in whole else at["y"]
    return ref.at[xh, z, xl, y, :, pl.ds(cols[0], cols[1])]


def thirds(group):
    start, end = GROUPS[group]
    tiles = (end - start) // LANES
    cuts = [start + tiles * i // 6 * LANES for i in range(7)]
    return [
        ((cuts[2 * i], cuts[2 * i + 1] - cuts[2 * i]), (cuts[2 * i + 1], cuts[2 * i + 2] - cuts[2 * i + 1]))
        for i in range(3)
    ]


def across(left, right):
    return lax.dot_general(left, right, (((1,), (1,)), ((), ())), preferred_element_type=F32)


def straight(left, right):
    return jnp.dot(left, right, preferred_element_type=F32)


def rows_of(block):
    return pl.ds(pl.multiple_of(block * ROWS, ROWS), ROWS)


def by_head(block):
    first = lax.broadcasted_iota(jnp.int32, block.shape, 1) < HEAD
    zero = jnp.zeros_like(block)
    return jnp.concatenate([jnp.where(first, block, zero), jnp.where(first, zero, block)], 0)


def key_mask(length, first, count):
    position = first + lax.broadcasted_iota(jnp.int32, (count, 1), 0)
    return jnp.where(position < length, 0.0, -1e30)


def columns_of(weights, start, width):
    return weights[:, :, :, :, :, pl.ds(start, width)].reshape(1024, width)


def quarter_of(weights, quarter, start, width):
    z = 2 * (quarter % 2)
    return weights[quarter // 2, z : z + 2, :, :, :, start : start + width].reshape(256, width)


def part(ref, peer):
    return ref.at[rows_of(peer // 4), rows_of(peer % 4)]


def parts_of(width):
    tiles = width//LANES
    cuts = [tiles*i//6*LANES for i in range(7)]
    return [((cuts[2*i], cuts[2*i+1]-cuts[2*i]), (cuts[2*i+1], cuts[2*i+2]-cuts[2*i+1])) for i in range(3)]

def scatter_kernel(all_ref, small_ref, own_ref, total_ref, work, small_land, load_sem, send_sem, recv_sem, small_send, small_recv, *landings):
    at = place()
    parts = parts_of(all_ref.shape[-1])
    loads=[]
    for part in range(3):
        lo,hi=parts[part]; both=pl.ds(lo[0],lo[1]+hi[1])
        cp=pltpu.make_async_copy(all_ref.at[:,:,:,:,:,both], work.at[:,:,:,:,:,both], load_sem.at[part]); cp.start(); loads.append(cp)
    greet(neighbours(at, (1, 2, 3)))
    for cp in loads: cp.wait()

    def push(part,phase,kind,origin,whole,cols,axis,step):
        land=landings[phase*3+part]
        src=shards(work,origin,whole,cols)
        return pltpu.make_async_remote_copy(src_ref=src,dst_ref=land.at[kind] if cols[1]==land.shape[-1] else land.at[kind,...,pl.ds(0,cols[1])],send_sem=send_sem.at[part,phase,kind],recv_sem=recv_sem.at[part,phase,kind],device_id=device(shifted(at,axis,step)),device_id_type=MESH)

    def add(origin,whole,cols,land_list):
        x=origin["x"]
        xs=[(a,b) for a in range(2) for b in range(2)] if "x" in whole else [(x//2,x%2)]
        zs=list(range(4)) if "z" in whole else [origin["z"]]
        ys=list(range(4)) if "y" in whole else [origin["y"]]
        sx="x" in whole; sz="z" in whole; sy="y" in whole
        def one(ix,iz,iy):
            xh,xl=(ix//2,ix%2) if sx else (x//2,x%2)
            z=iz if sz else origin["z"]; y=iy if sy else origin["y"]
            index=(xh,z,xl,y,slice(None),pl.ds(cols[0],cols[1]))
            total=work[index].astype(jnp.float32)
            for land,kind in land_list:
                li=(kind,)
                if sx: li+=(xh,)
                if sz: li+=(z,)
                if sx: li+=(xl,)
                if sy: li+=(y,)
                li+=(slice(None),pl.ds(0,cols[1]))
                total=total+land[li].astype(jnp.float32)
            work[index]=total.astype(work.dtype)
        nx=4 if sx else 1; nz=4 if sz else 1; ny=4 if sy else 1
        n=nx*nz*ny
        def body(i,_):
            one(i//(nz*ny), (i//ny)%nz, i%ny); return 0
        if n==1: one(0,0,0)
        else: lax.fori_loop(0,n,body,0)

    total_ref[...]=small_ref[...]
    for phase in range(3):
        early=[]
        small=[]
        for step in (1,2,3):
            cp=pltpu.make_async_remote_copy(src_ref=total_ref,dst_ref=small_land.at[phase,step-1],send_sem=small_send.at[phase,step-1],recv_sem=small_recv.at[phase,step-1],device_id=device(shifted(at,"xyz"[phase],step)),device_id_type=MESH)
            cp.start(); small.append(cp)
        for part in range(3):
            order=ORDERS[part][::-1]; axis=order[phase]; whole=order[phase+1:]
            lo,hi=parts[part]
            far=shifted(at,axis,2); up=shifted(at,axis,1); down=shifted(at,axis,-1)
            a=push(part,phase,0,far,whole,lo,axis,1); a.start()
            b=push(part,phase,1,far,whole,hi,axis,-1); b.start()
            c=push(part,phase,2,up,whole,hi,axis,1); c.start()
            d=push(part,phase,3,down,whole,lo,axis,-1); d.start()
            early.append((a,b,c,d))
        late=[]
        for part in range(3):
            order=ORDERS[part][::-1]; axis=order[phase]; whole=order[phase+1:]
            lo,hi=parts[part]; land=landings[phase*3+part]
            up=shifted(at,axis,1); down=shifted(at,axis,-1)
            a,b,c,d=early[part]
            a.wait_recv(); add(up,whole,lo,[(land,0)])
            e=push(part,phase,4,up,whole,lo,axis,1); e.start()
            b.wait_recv(); add(down,whole,hi,[(land,1)])
            f=push(part,phase,5,down,whole,hi,axis,-1); f.start()
            late.append((e,f))
        for part in range(3):
            order=ORDERS[part][::-1]; axis=order[phase]; whole=order[phase+1:]
            lo,hi=parts[part]; land=landings[phase*3+part]
            a,b,c,d=early[part]; e,f=late[part]
            c.wait_recv(); f.wait_recv()
            add(at,whole,hi,[(land,2),(land,5)])
            d.wait_recv(); e.wait_recv()
            add(at,whole,lo,[(land,3),(land,4)])
        for part in range(3):
            for cp in early[part]+late[part]: cp.wait_send()
        for cp in small: cp.wait_recv()
        for cp in small: cp.wait_send()
        total_ref[...]=total_ref[...]+small_land[phase,0]+small_land[phase,1]+small_land[phase,2]
    x=at["x"]
    own_ref[...]=work[x//2,at["z"],x%2,at["y"]].astype(jnp.float32)

def scatter_all(whole, small):
    rows,width=whole.shape[-2:]
    parts=parts_of(width)
    landings=[]
    for phase in range(3):
        for part in range(3):
            order=ORDERS[part][::-1]; w=order[phase+1:]
            shape=[6]
            if "x" in w: shape.append(2)
            if "z" in w: shape.append(4)
            if "x" in w: shape.append(2)
            if "y" in w: shape.append(4)
            shape+= [rows, max(parts[part][0][1],parts[part][1][1])]
            landings.append(pltpu.VMEM(tuple(shape), whole.dtype))
    return pl.pallas_call(scatter_kernel,
        out_shape=(jax.ShapeDtypeStruct((rows,width), jnp.float32),jax.ShapeDtypeStruct(small.shape, jnp.float32)),
        in_specs=[pl.BlockSpec(memory_space=pl.ANY),pl.BlockSpec(memory_space=pltpu.VMEM)], out_specs=(pl.BlockSpec(memory_space=pltpu.VMEM),pl.BlockSpec(memory_space=pltpu.VMEM)),
        scratch_shapes=[pltpu.VMEM(whole.shape, whole.dtype), pltpu.VMEM((3,3)+small.shape,jnp.float32), pltpu.SemaphoreType.DMA((3,)), pltpu.SemaphoreType.DMA((3,3,6)), pltpu.SemaphoreType.DMA((3,3,6)), pltpu.SemaphoreType.DMA((3,3)), pltpu.SemaphoreType.DMA((3,3))]+landings,
        compiler_params=pltpu.CompilerParams(collective_id=2, has_side_effects=True, vmem_limit_bytes=60*2**20),
        name="scatter_grads")(whole, small)


class Gather:
    def __init__(self, weights, group, send_sem, recv_sem):
        self.at = place()
        self.weights, self.group = weights, group
        self.send_sem, self.recv_sem = send_sem, recv_sem
        self.parts = thirds(group)
        self.sent = {}

    def send(self, third, phase, kind, origin, cols, step):
        order = ORDERS[third]
        block = shards(self.weights, origin, order[:phase], cols)
        index = (self.group, third, phase, kind)
        copy = remote(
            block, block, self.send_sem.at[index], self.recv_sem.at[index],
            device(shifted(self.at, order[phase], step)),
        )
        copy.start()
        self.sent[third, phase, kind] = copy

    def first(self, phase):
        for third in range(3):
            low, high = self.parts[third]
            both = (low[0], low[1] + high[1])
            self.send(third, phase, 0, self.at, both, 1)
            self.send(third, phase, 1, self.at, both, -1)

    def onward(self, phase):
        for third in range(3):
            axis = ORDERS[third][phase]
            low, high = self.parts[third]
            self.sent[third, phase, 0].wait_recv()
            self.send(third, phase, 2, shifted(self.at, axis, -1), low, 1)
            self.sent[third, phase, 1].wait_recv()
            self.send(third, phase, 3, shifted(self.at, axis, 1), high, -1)

    def settle(self, phase):
        for third in range(3):
            self.sent[third, phase, 2].wait_recv()
            self.sent[third, phase, 3].wait_recv()

    def close(self):
        for copy in self.sent.values():
            copy.wait_send()


class Heads:
    def __init__(self, own, unit, outcome, mixed, local_sem, send_sem, recv_sem, back_send, back_recv):
        self.f = lax.axis_index("fsdp")
        self.c = lax.axis_index("context")
        self.t = lax.axis_index("tensor")
        self.own, self.unit, self.outcome, self.mixed = own, unit, outcome, mixed
        self.local_sem, self.send_sem, self.recv_sem = local_sem, send_sem, recv_sem
        self.back_send, self.back_recv = back_send, back_recv

    def push(self, j, d):
        peer = lax.rem(self.c + d, 8)
        return remote(
            part(self.own.at[j], peer), self.unit.at[j, rows_of(self.c)],
            self.send_sem.at[j, d - 1], self.recv_sem.at[j, d - 1], (self.f, peer, self.t),
        )

    def keep(self, j):
        return pltpu.make_async_copy(
            part(self.own.at[j], self.c), self.unit.at[j, rows_of(self.c)], self.local_sem.at[j]
        )

    def answer(self, d):
        peer = lax.rem(self.c + d, 8)
        return remote(
            self.outcome.at[rows_of(peer)], part(self.mixed, self.c),
            self.back_send.at[d - 1], self.back_recv.at[d - 1], (self.f, peer, self.t),
        )

    def keep_back(self):
        return pltpu.make_async_copy(
            self.outcome.at[rows_of(self.c)], part(self.mixed, self.c), self.local_sem.at[3]
        )

    def project(self, x, weights, bias):
        for j, column in enumerate((KEY, VALUE, QUERY)):
            product = straight(x, columns_of(weights, column, 512))
            if j == 1:
                product = product + bias[:, 512:1024]
            if j == 2:
                product = product + bias[:, 0:512]
            self.own[j] = product.astype(BF16)
            for d in (4, 1, 7, 5, 3, 2, 6):
                self.push(j, d).start()
            self.keep(j).start()

    def attend(self, length, exact, logs):
        c = self.c
        for j in range(2):
            self.keep(j).wait()
            for d in range(1, 8):
                self.push(j, d).wait_recv()
        mask = key_mask(length, 0, 8 * ROWS)
        keys = self.unit[0]
        values_across = self.unit[1].T
        self.keep(2).wait()

        def step(d, carry):
            block = lax.rem(c + d, 8)

            @pl.when(d > 0)
            def _():
                self.push(2, 8 - d).wait_recv()

            queries = self.unit[2, rows_of(block), :] * jnp.asarray(0.125, BF16)
            scores = across(keys, by_head(queries)) + mask
            top = jnp.max(scores, 0, keepdims=True)
            exponent = jnp.exp(scores - top)
            total = jnp.sum(exponent, 0, keepdims=True)
            outcome = straight(values_across, exponent.astype(BF16)) / total
            both = jnp.concatenate([outcome[:HEAD, :ROWS], outcome[HEAD:, ROWS:]], 0).T
            exact[rows_of(block), :] = both
            self.outcome[rows_of(block), :] = both.astype(BF16)
            logs[pl.ds(block, 1), :] = top + jnp.log(total)

            @pl.when(d > 0)
            def _():
                self.answer(d).start()

            return carry

        lax.fori_loop(0, 8, step, 0)
        self.keep_back().start()

    def collect(self):
        self.keep_back().wait()
        for d in range(1, 8):
            self.answer(d).wait_recv()

    def close(self):
        for d in range(1, 8):
            self.answer(d).wait_send()
            for j in range(3):
                self.push(j, d).wait_send()


class Joins:
    def __init__(self, sent, landed, send_sem, recv_sem):
        t = lax.axis_index("tensor")
        self.partner = (lax.axis_index("fsdp"), lax.axis_index("context"), 1 - t)
        self.sent, self.landed, self.send_sem, self.recv_sem = sent, landed, send_sem, recv_sem

    def copy(self, half):
        return remote(
            self.sent.at[half], self.landed.at[half], self.send_sem.at[half], self.recv_sem.at[half],
            self.partner,
        )

    def offer(self, quarter, term):
        half, side = quarter // 2, quarter % 2
        self.sent[half, :, side * 256 : side * 256 + 256] = term.astype(BF16)
        if side == 1:
            self.copy(half).start()

    def wait(self):
        for half in range(2):
            self.copy(half).wait_recv()

    def total(self, rows):
        return jnp.concatenate(
            [self.sent[half, rows, :].astype(F32) + self.landed[half, rows, :].astype(F32) for half in range(2)],
            1,
        )

    def close(self):
        for half in range(2):
            self.copy(half).wait_send()


def gelu_parts(argument):
    square = argument * argument
    inner = 0.7978845608028654 * argument * (1.0 + 0.044715 * square)
    bend = jnp.tanh(inner)
    half = 0.5 * (1.0 + bend)
    slope = half + 0.5 * argument * (1.0 - bend * bend) * 0.7978845608028654 * (
        1.0 + 3.0 * 0.044715 * square
    )
    return argument * half, slope


def norm_parts(hidden):
    centre = hidden - jnp.mean(hidden, -1, keepdims=True)
    inverse = lax.rsqrt(jnp.mean(centre * centre, -1, keepdims=True) + 1e-05)
    return centre * inverse, inverse


def live_rows(lengths, block, count):
    c = lax.axis_index("context")
    row = block * count + lax.broadcasted_iota(jnp.int32, (count, 1), 0)
    slot = c * ROWS + lax.rem(row, ROWS)
    return jnp.where(slot < jnp.where(row < ROWS, lengths[0], lengths[1]), 1.0, 0.0)


SLAB = 64


def slab_of(block):
    return pl.ds(pl.multiple_of(block * SLAB, SLAB), SLAB)


def pack(weights, own, query, key, value, output, inner, outer, vectors):
    xh, z, xl, y = own
    eye = jnp.where(
        lax.broadcasted_iota(jnp.int32, (16, 16), 0) == lax.broadcasted_iota(jnp.int32, (16, 16), 1), 1.0, 0.0
    ).astype(BF16)

    def put(start, block):
        weights[xh, z, xl, y, :, start : start + block.shape[1]] = block

    put(QUERY, query[...])
    put(KEY, key[...])
    put(VALUE, value[...])
    put(OUT, across(eye, output[...]).astype(BF16))
    put(INNER, inner[...])
    put(OUTER, across(eye, outer[...]).astype(BF16))
    put(EXTRA, across(eye, vectors[...]).astype(BF16))


def forward_kernel(
    x_ref, query, key, value, output, inner, outer, vectors, bias, lengths,
    result_ref, rows_ref, squares_ref, w_out, unit_out, exact_out, logs_out, mixed_out, normed_out, inverse_out,
    middle_out, act_out, slope_out, low_out,
    weights, own, unit, exact, logs, outcome, mixed, normed, inverse, middle, act, slope, low, current,
    sent, landed,
    local_sem, save_sem, gather_send, gather_recv, send_sem, recv_sem, back_send, back_recv, pair_send, pair_recv,
):
    at = place()
    c = lax.axis_index("context")
    t = lax.axis_index("tensor")
    partner = (lax.axis_index("fsdp"), c, 1 - t)
    x = at["x"]
    pack(weights, (x // 2, at["z"], x % 2, at["y"]), query, key, value, output, inner, outer, vectors)
    greet(neighbours(at, (1, -1)) + context_peers() + [partner])
    one, two = (Gather(weights, group, gather_send, gather_recv) for group in range(2))
    one.first(0)
    two.first(0)
    one.onward(0)
    two.onward(0)
    one.settle(0)
    one.first(1)
    two.settle(0)
    two.first(1)
    one.onward(1)
    two.onward(1)
    one.settle(1)
    one.first(2)
    two.settle(1)
    one.onward(2)
    two.first(2)
    current[...] = x_ref[...].astype(F32)
    one.settle(2)
    squares_ref[...] = jnp.zeros_like(squares_ref)
    length = lengths[c // 4]
    saves = []

    def save(source, target):
        copy = pltpu.make_async_copy(source, target, save_sem.at[len(saves)])
        copy.start()
        saves.append(copy)

    closing = [one, two]
    for layer in range(LAYERS):
        first = layer == 0
        heads = Heads(
            own.at[layer], unit.at[layer], outcome.at[layer], mixed.at[layer], local_sem.at[layer],
            send_sem.at[layer], recv_sem.at[layer], back_send.at[layer], back_recv.at[layer],
        )
        joins = [
            Joins(sent.at[layer, stage], landed.at[layer, stage], pair_send.at[layer, stage], pair_recv.at[layer, stage])
            for stage in range(2)
        ]
        heads.project(x_ref[...] if first else low[...], weights, bias)
        heads.attend(length, exact.at[layer], logs.at[layer])
        if first:
            two.onward(2)
        heads.collect()
        if first:
            two.settle(2)
            save(weights, w_out)
            pick = jnp.where(
                lax.broadcasted_iota(jnp.int32, (8, LANES), 0) == lax.broadcasted_iota(jnp.int32, (8, LANES), 1),
                1.0, 0.0,
            ).astype(BF16)
            rows_ref[...] = across(pick, columns_of(weights, EXTRA, LANES))
        for quarter in range(4):
            joins[0].offer(quarter, across(mixed[layer], quarter_of(weights, quarter, OUT, 512)))
        save(unit.at[layer], unit_out.at[layer])
        save(exact.at[layer], exact_out.at[layer])
        save(logs.at[layer], logs_out.at[layer])
        save(mixed.at[layer], mixed_out.at[layer])
        joins[0].wait()

        def after_attention(block, total):
            rows = slab_of(block)
            live = live_rows(lengths, block, SLAB)
            before = current[rows, :]
            branch = joins[0].total(rows) + rows_ref[0:1, :]
            scaled, root = norm_parts(before + branch)
            after = scaled * rows_ref[2:3, :] + rows_ref[3:4, :]
            normed[layer, 0, rows, :] = scaled
            inverse[layer, 0, rows, :] = root
            current[rows, :] = after
            middle[layer, rows, :] = after.astype(BF16)
            return (
                total[0] + jnp.sum(live * before * before, 0, keepdims=True),
                total[1] + jnp.sum(live * branch * branch, 0, keepdims=True),
            )

        zero = jnp.zeros((1, 1024), F32)
        total = lax.fori_loop(0, 256 // SLAB, after_attention, (zero, zero))
        squares_ref[3 * layer : 3 * layer + 1, :] = total[0]
        squares_ref[3 * layer + 1 : 3 * layer + 2, :] = total[1]
        save(middle.at[layer], middle_out.at[layer])

        def hidden(tile, carry):
            start = pl.multiple_of(tile * 512, 512)
            columns = pl.ds(start, 512)
            pre = straight(middle[layer], columns_of(weights, INNER + start, 512)) + bias[:, pl.ds(1024 + start, 512)]
            act_part, slope_part = gelu_parts(pre)
            act[layer, :, columns] = act_part.astype(BF16)
            slope[layer, :, columns] = slope_part.astype(BF16)
            return carry

        lax.fori_loop(0, 4, hidden, 0)
        for quarter in range(4):
            joins[1].offer(quarter, across(act[layer], quarter_of(weights, quarter, OUTER, 2048)))
        save(act.at[layer], act_out.at[layer])
        save(slope.at[layer], slope_out.at[layer])
        joins[1].wait()

        def after_hidden(block, total):
            rows = slab_of(block)
            live = live_rows(lengths, block, SLAB)
            branch = joins[1].total(rows) + rows_ref[1:2, :]
            scaled, root = norm_parts(current[rows, :] + branch)
            after = scaled * rows_ref[4:5, :] + rows_ref[5:6, :]
            normed[layer, 1, rows, :] = scaled
            inverse[layer, 1, rows, :] = root
            current[rows, :] = after
            if first:
                low[rows, :] = after.astype(BF16)
            else:
                result_ref[rows, :] = (after * live).astype(BF16)
            return total + jnp.sum(live * branch * branch, 0, keepdims=True)

        squares_ref[3 * layer + 2 : 3 * layer + 3, :] = lax.fori_loop(0, 256 // SLAB, after_hidden, zero)
        save(normed.at[layer], normed_out.at[layer])
        save(inverse.at[layer], inverse_out.at[layer])
        if first:
            save(low, low_out)
        closing += [heads] + joins
    for item in closing:
        item.close()
    for copy in saves:
        copy.wait()


def run_forward(x, query, key, value, output, inner, outer, vectors, bias, lengths):
    saved = (
        ((*SHARDS, 16, WIDTH), BF16),
        ((2, 3, 1024, LANES), BF16),
        ((2, 1024, LANES), F32),
        ((2, 8, 256), F32),
        ((2, 256, 512), BF16),
        ((2, 2, 256, 1024), F32),
        ((2, 2, 256, 1), F32),
        ((2, 256, 1024), BF16),
        ((2, 256, 2048), BF16),
        ((2, 256, 2048), BF16),
        ((256, 1024), BF16),
    )
    dma = pltpu.SemaphoreType.DMA
    return pl.pallas_call(
        forward_kernel,
        out_shape=(
            jax.ShapeDtypeStruct((256, 1024), BF16),
            jax.ShapeDtypeStruct((8, 1024), F32),
            jax.ShapeDtypeStruct((8, 1024), F32),
            *(jax.ShapeDtypeStruct(shape, kind) for shape, kind in saved),
        ),
        in_specs=[spec(pltpu.VMEM)] * 9 + [spec(pltpu.SMEM)],
        out_specs=(spec(pltpu.VMEM),) * 3 + (spec(pl.ANY),) * len(saved),
        scratch_shapes=[
            pltpu.VMEM((*SHARDS, 16, WIDTH), BF16),
            pltpu.VMEM((2, 3, 256, 512), BF16),
            pltpu.VMEM((2, 3, 1024, LANES), BF16),
            pltpu.VMEM((2, 1024, LANES), F32),
            pltpu.VMEM((2, 8, 256), F32),
            pltpu.VMEM((2, 1024, LANES), BF16),
            pltpu.VMEM((2, 256, 512), BF16),
            pltpu.VMEM((2, 2, 256, 1024), F32),
            pltpu.VMEM((2, 2, 256, 1), F32),
            pltpu.VMEM((2, 256, 1024), BF16),
            pltpu.VMEM((2, 256, 2048), BF16),
            pltpu.VMEM((2, 256, 2048), BF16),
            pltpu.VMEM((256, 1024), BF16),
            pltpu.VMEM((256, 1024), F32),
            pltpu.VMEM((2, 2, 2, 256, 512), BF16),
            pltpu.VMEM((2, 2, 2, 256, 512), BF16),
            dma((2, 4)),
            dma((24,)),
            dma((2, 3, 3, 4)),
            dma((2, 3, 3, 4)),
            dma((2, 3, 7)),
            dma((2, 3, 7)),
            dma((2, 7)),
            dma((2, 7)),
            dma((2, 2, 2)),
            dma((2, 2, 2)),
        ],
        compiler_params=pltpu.CompilerParams(
            collective_id=3, has_side_effects=True, vmem_limit_bytes=LIMIT
        ),
        name="forward_layers",
    )(x, query, key, value, output, inner, outer, vectors, bias, lengths)


def norm_back(grad_out, normed, inverse, gain):
    scaled = grad_out * gain
    return inverse * (
        scaled
        - jnp.mean(scaled, -1, keepdims=True)
        - normed * jnp.mean(scaled * normed, -1, keepdims=True)
    )


def backward_kernel(
    grad_ref, normed2_ref, inverse2_ref, slope_ref, normed1_ref, inverse1_ref, w_ref, vectors_ref,
    outer_grad_ref, inner_grad_ref, first_ref, attn_ref, mixed_grad_ref, sums_ref, bias_ref,
    out_w, inner_w, outer_w, second_buf, sent, landed, w_sem, send_sem, recv_sem,
):
    f = lax.axis_index("fsdp")
    c = lax.axis_index("context")
    t = lax.axis_index("tensor")
    partner = (f, c, 1 - t)
    loads = []
    for j, (column, buffer) in enumerate(((4096, outer_w), (2048, inner_w), (1536, out_w))):
        load = pltpu.make_async_copy(
            w_ref.at[:, pl.ds(column, buffer.shape[1])], buffer, w_sem.at[j]
        )
        load.start()
        loads.append(load)
    greet([partner])

    def join(half):
        return remote(
            sent.at[half], landed.at[half], send_sem.at[half], recv_sem.at[half], partner
        )

    def rows(half):
        return pl.ds(half * ROWS, ROWS)

    sums = [0.0] * 6
    for half in range(2):
        grad = grad_ref[rows(half), :]
        normed = normed2_ref[rows(half), :]
        second = norm_back(grad, normed, inverse2_ref[rows(half), :], vectors_ref[4:5, :])
        low = second.astype(BF16)
        second_buf[rows(half), :] = second
        outer_grad_ref[rows(half), :] = low
        sums[4] += jnp.sum(grad * normed, 0, keepdims=True)
        sums[5] += jnp.sum(grad, 0, keepdims=True)
        sums[1] += jnp.sum(low.astype(F32), 0, keepdims=True)
    loads[0].wait()

    def inner(tile, carry):
        columns = pl.ds(pl.multiple_of(tile * 512, 512), 512)
        act = straight(outer_grad_ref[...], outer_w[:, columns])
        low = (act * slope_ref[:, columns].astype(F32)).astype(BF16)
        inner_grad_ref[:, columns] = low
        bias_ref[:, columns] = jnp.sum(low.astype(F32), 0, keepdims=True)
        return carry

    lax.fori_loop(0, 4, inner, 0)
    loads[1].wait()
    for half in range(2):
        sent[half] = across(inner_grad_ref[rows(half), :], inner_w[...]).astype(BF16)
        join(half).start()
    loads[2].wait()
    for half in range(2):
        join(half).wait_recv()
        middle = second_buf[rows(half), :] + (sent[half].astype(F32) + landed[half].astype(F32))
        normed = normed1_ref[rows(half), :]
        sums[2] += jnp.sum(middle * normed, 0, keepdims=True)
        sums[3] += jnp.sum(middle, 0, keepdims=True)
        first = norm_back(middle, normed, inverse1_ref[rows(half), :], vectors_ref[2:3, :])
        low = first.astype(BF16)
        first_ref[rows(half), :] = first
        attn_ref[rows(half), :] = low
        sums[0] += jnp.sum(low.astype(F32), 0, keepdims=True)
        mixed_grad_ref[rows(half), :] = straight(low, out_w[...]).astype(BF16)
    sums_ref[...] = jnp.zeros_like(sums_ref)
    for j in range(6):
        sums_ref[j : j + 1, :] = sums[j]
    for half in range(2):
        join(half).wait_send()


def backward(grad, saved, gathered, vectors):
    normed1, inverse1, slope, normed2, inverse2 = saved
    return pl.pallas_call(
        backward_kernel,
        out_shape=(
            jax.ShapeDtypeStruct((256, 1024), BF16),
            jax.ShapeDtypeStruct((256, 2048), BF16),
            jax.ShapeDtypeStruct((256, 1024), F32),
            jax.ShapeDtypeStruct((256, 1024), BF16),
            jax.ShapeDtypeStruct((256, 512), BF16),
            jax.ShapeDtypeStruct((8, 1024), F32),
            jax.ShapeDtypeStruct((1, 2048), F32),
        ),
        in_specs=[spec(pltpu.VMEM)] * 6 + [spec(pl.ANY), spec(pltpu.VMEM)],
        out_specs=(spec(pltpu.VMEM),) * 7,
        scratch_shapes=[
            pltpu.VMEM((1024, 512), BF16),
            pltpu.VMEM((1024, 2048), BF16),
            pltpu.VMEM((1024, 2048), BF16),
            pltpu.VMEM((256, 1024), F32),
            pltpu.VMEM((2, ROWS, 1024), BF16),
            pltpu.VMEM((2, ROWS, 1024), BF16),
            pltpu.SemaphoreType.DMA((3,)),
            pltpu.SemaphoreType.DMA((2,)),
            pltpu.SemaphoreType.DMA((2,)),
        ],
        compiler_params=pltpu.CompilerParams(
            collective_id=5, has_side_effects=True, vmem_limit_bytes=LIMIT
        ),
        name="backward",
    )(grad, normed2, inverse2, slope, normed1, inverse1, gathered, vectors)


def attend_back_kernel(
    mixed_grad_ref, unit_ref, outcome_ref, logs_ref, first_ref, w_ref, lengths,
    grads_ref, next_ref, sums_ref,
    w_buf, taken, grad_buf, query_sum, key_value_buf, query_buf, sent, landed,
    w_sem, local_sem, send_sem, recv_sem, back_send, back_recv, pair_send, pair_recv,
):
    f = lax.axis_index("fsdp")
    c = lax.axis_index("context")
    t = lax.axis_index("tensor")
    partner = (f, c, 1 - t)
    loads = []
    for j, column in enumerate((512, 1024, 0)):
        load = pltpu.make_async_copy(w_ref.at[:, pl.ds(column, 512)], w_buf.at[j], w_sem.at[j])
        load.start()
        loads.append(load)
    greet([(f, lax.rem(c + d, 8), t) for d in range(1, 8)] + [partner])

    def push(d):
        peer = lax.rem(c + d, 8)
        return remote(
            part(mixed_grad_ref, peer), taken.at[rows_of(c)],
            send_sem.at[d - 1], recv_sem.at[d - 1], (f, peer, t),
        )

    for d in range(1, 8):
        push(d).start()
    keep = pltpu.make_async_copy(part(mixed_grad_ref, c), taken.at[rows_of(c)], local_sem.at[0])
    keep.start()
    scale = jnp.asarray(0.125, BF16)
    queries = jnp.concatenate(
        [by_head(unit_ref[2, pl.ds(block * ROWS, ROWS), :] * scale) for block in range(8)], 0
    )
    logs = jnp.concatenate([logs_ref[block : block + 1, :] for block in range(8)], 1)
    query_sum[...] = jnp.zeros_like(query_sum)
    keep.wait()
    for d in range(1, 8):
        push(d).wait_recv()
    for block in range(8):
        grad_buf[pl.ds(block * 256, 256), :] = by_head(taken[pl.ds(block * ROWS, ROWS), :])
    head_row = lax.broadcasted_iota(jnp.int32, (8, LANES), 0)
    head_lane = lax.broadcasted_iota(jnp.int32, (8, LANES), 1) // HEAD
    chosen = jnp.where(head_row == head_lane, 1.0, 0.0)
    weighted = lax.dot_general(
        chosen, taken[...].astype(F32) * outcome_ref[...],
        (((1,), (1,)), ((), ())), precision=lax.Precision.HIGHEST, preferred_element_type=F32,
    )
    delta = jnp.concatenate(
        [
            weighted[head : head + 1, block * ROWS : (block + 1) * ROWS]
            for block in range(8)
            for head in range(2)
        ],
        1,
    )
    length = lengths[c // 4]

    def answer(j, d):
        peer = lax.rem(c + d, 8)
        source = query_buf if j == 2 else key_value_buf.at[j]
        return remote(
            source.at[rows_of(peer)], part(grads_ref.at[j], c),
            back_send.at[j, d - 1], back_recv.at[j, d - 1], (f, peer, t),
        )

    def step(turn, carry):
        pair = lax.rem(c // 2 + turn, 4)
        spot = pl.ds(pl.multiple_of(pair * 256, 256), 256)
        keys = unit_ref[0, spot, :]
        values = unit_ref[1, spot, :]
        scores = across(keys, queries) + key_mask(length, pair * 256, 256)
        soft = jnp.exp(scores - logs)
        key_value_buf[1, spot, :] = straight(soft.astype(BF16), grad_buf[...]).astype(BF16)
        soft_grad = across(values, grad_buf[...])
        score_grad = (soft * (soft_grad - delta)).astype(BF16)
        key_value_buf[0, spot, :] = straight(score_grad, queries).astype(BF16)
        query_sum[...] += lax.dot_general(
            score_grad, keys, (((0,), (0,)), ((), ())), preferred_element_type=F32
        )

        for side in range(2):
            block = pair * 2 + side
            d = lax.rem(block - c + 8, 8)

            @pl.when(d > 0)
            def _():
                for j in range(2):
                    answer(j, d).start()

        return carry

    lax.fori_loop(1, 5, step, 0)
    first_lane = lax.broadcasted_iota(jnp.int32, (ROWS, LANES), 1) < HEAD
    for block in range(8):
        start = block * 256
        total = jnp.where(
            first_lane,
            query_sum[pl.ds(start, ROWS), :],
            query_sum[pl.ds(start + ROWS, ROWS), :],
        )
        query_buf[pl.ds(block * ROWS, ROWS), :] = (total * 0.125).astype(BF16)
    for d in range(1, 8):
        answer(2, d).start()
    kept = []
    for j in range(3):
        source = query_buf if j == 2 else key_value_buf.at[j]
        keep = pltpu.make_async_copy(source.at[rows_of(c)], part(grads_ref.at[j], c), local_sem.at[j])
        keep.start()
        kept.append(keep)
    for j in range(3):
        kept[j].wait()
        loads[j].wait()
    for j in range(2):
        for d in range(1, 8):
            answer(j, d).wait_recv()
    sums_ref[...] = jnp.zeros_like(sums_ref)
    sums_ref[1:2, :] = jnp.sum(grads_ref[1].astype(F32), 0, keepdims=True)
    early = across(grads_ref[0], w_buf[0]) + across(grads_ref[1], w_buf[1])
    for d in range(1, 8):
        answer(2, d).wait_recv()
    sums_ref[0:1, :] = jnp.sum(grads_ref[2].astype(F32), 0, keepdims=True)
    sent[...] = (early + across(grads_ref[2], w_buf[2])).astype(BF16)
    swap = remote(sent, landed, pair_send, pair_recv, partner)
    swap.start()
    swap.wait()
    next_ref[...] = first_ref[...] + (sent[...].astype(F32) + landed[...].astype(F32))
    for d in range(1, 8):
        push(d).wait_send()
        for j in range(3):
            answer(j, d).wait_send()


def attend_back(mixed_grad, unit, outcome, logs, first, gathered, lengths):
    return pl.pallas_call(
        attend_back_kernel,
        out_shape=(
            jax.ShapeDtypeStruct((3, 256, 512), BF16),
            jax.ShapeDtypeStruct((256, 1024), F32),
            jax.ShapeDtypeStruct((8, 512), F32),
        ),
        in_specs=[spec(pltpu.VMEM)] * 5 + [spec(pl.ANY), spec(pltpu.SMEM)],
        out_specs=(spec(pltpu.VMEM),) * 3,
        scratch_shapes=[
            pltpu.VMEM((3, 1024, 512), BF16),
            pltpu.VMEM((1024, LANES), BF16),
            pltpu.VMEM((2048, LANES), BF16),
            pltpu.VMEM((2048, LANES), F32),
            pltpu.VMEM((2, 1024, LANES), BF16),
            pltpu.VMEM((1024, LANES), BF16),
            pltpu.VMEM((256, 1024), BF16),
            pltpu.VMEM((256, 1024), BF16),
            pltpu.SemaphoreType.DMA((3,)),
            pltpu.SemaphoreType.DMA((3,)),
            pltpu.SemaphoreType.DMA((7,)),
            pltpu.SemaphoreType.DMA((7,)),
            pltpu.SemaphoreType.DMA((3, 7)),
            pltpu.SemaphoreType.DMA((3, 7)),
            pltpu.SemaphoreType.DMA,
            pltpu.SemaphoreType.DMA,
        ],
        compiler_params=pltpu.CompilerParams(
            collective_id=6, has_side_effects=True, vmem_limit_bytes=LIMIT
        ),
        name="attend_back",
    )(mixed_grad, unit, outcome, logs, first, gathered, lengths)


def body(
    stream,
    lengths,
    query_weight,
    query_bias,
    key_weight,
    value_weight,
    value_bias,
    output_weight,
    output_bias,
    first_gain,
    first_shift,
    inner_weight,
    inner_bias,
    outer_weight,
    outer_bias,
    second_gain,
    second_shift,
    cotangent,
):
    slot_count, seq_count, model_width = stream.shape
    row_count = slot_count * seq_count
    position = lax.axis_index("context") * slot_count + jnp.arange(slot_count, dtype=jnp.int32)
    row_live = (position[None, :] < lengths[:, None]).astype(F32).reshape(row_count, 1)
    vectors = jnp.pad(
        jnp.stack([output_bias, outer_bias, first_gain, first_shift, second_gain, second_shift]),
        ((0, LANES - 6), (0, 0)),
    )
    bias = jnp.concatenate([query_bias, value_bias, inner_bias]).astype(F32)[None]
    low = stream.transpose(1, 0, 2).reshape(row_count, model_width)
    (
        result, vectors, squares, gathered, unit, exact, logs, mixed, normed, inverse, middle, act, slope, low_next,
    ) = run_forward(
        low, query_weight, key_weight, value_weight, output_weight, inner_weight, outer_weight, vectors, bias, lengths
    )
    gathered = gathered.reshape(model_width, WIDTH)
    stored = []
    for repeat in range(LAYERS):
        stored.append(
            (
                low_next if repeat else low, mixed[repeat], unit[repeat], exact[repeat], logs[repeat],
                middle[repeat], act[repeat],
                (normed[repeat, 0], inverse[repeat, 0], slope[repeat], normed[repeat, 1], inverse[repeat, 1]),
            )
        )
    result = result.reshape(seq_count, slot_count, model_width).transpose(1, 0, 2)
    grad = cotangent.transpose(1, 0, 2).reshape(row_count, model_width).astype(F32) * row_live
    taken = []
    for repeat in reversed(range(LAYERS)):
        low, mixed, unit, outcome, logs, middle, act, saved = stored[repeat]
        outer_grad, inner_grad, first, attn, mixed_grad, sums, bias = backward(
            grad, saved, gathered, vectors
        )
        qkv, grad, head_sums = attend_back(mixed_grad, unit, outcome, logs, first, gathered, lengths)
        taken.append((low, qkv, attn, mixed, middle, inner_grad, outer_grad, act, sums, bias, head_sums))

    def twice(left, right):
        return sum(
            lax.dot_general(left(t), right(t), (((0,), (0,)), ((), ())), preferred_element_type=F32)
            for t in taken
        )

    sums = taken[0][8] + taken[1][8]
    bias = taken[0][9] + taken[1][9]
    head_sums = taken[0][10] + taken[1][10]
    grads = jnp.concatenate(
        [
            twice(lambda t: t[0], lambda t: t[1][2]),
            twice(lambda t: t[0], lambda t: t[1][0]),
            twice(lambda t: t[0], lambda t: t[1][1]),
            twice(lambda t: t[2], lambda t: t[3]),
            twice(lambda t: t[4], lambda t: t[5]),
            twice(lambda t: t[6], lambda t: t[7]),
            jnp.pad(sums[:6].T, ((0, 0), (0, LANES - 6))),
        ],
        1,
    ).astype(BF16)
    small = jnp.concatenate(
        [
            head_sums[0],
            head_sums[1],
            bias[0],
            jnp.sum(squares[:6], 1),
            jnp.sum(row_live)[None],
            jnp.zeros((1024 - 7,), F32),
        ]
    ).reshape(32, LANES)
    summed, total = scatter_all(grads.reshape(2, 4, 2, 4, 16, grads.shape[1]), small)
    total = total.reshape(-1)
    square_total, count_total = total[3072:3078].reshape(LAYERS, 3), total[3078]
    root_values = jnp.sqrt(square_total / (count_total * model_width) + 1e-06)
    stream_grad = grad.reshape(seq_count, slot_count, model_width).transpose(1, 0, 2)
    return (
        result,
        stream_grad,
        summed[:, 0:512],
        total[0:512],
        summed[:, 512:1024],
        summed[:, 1024:1536],
        total[512:1024],
        summed[:, 1536:2048].T,
        summed[:, 6144],
        summed[:, 6146],
        summed[:, 6147],
        summed[:, 2048:4096],
        total[1024:3072],
        summed[:, 4096:6144].T,
        summed[:, 6145],
        summed[:, 6148],
        summed[:, 6149],
        root_values,
    )


def solution(mesh):
    in_specs = (
        P("context", "fsdp", None),
        P("fsdp"),
        P(("fsdp", "context"), "tensor"),
        P("tensor"),
        P(("fsdp", "context"), "tensor"),
        P(("fsdp", "context"), "tensor"),
        P("tensor"),
        P("tensor", ("fsdp", "context")),
        P(("fsdp", "context")),
        P(("fsdp", "context")),
        P(("fsdp", "context")),
        P(("fsdp", "context"), "tensor"),
        P("tensor"),
        P("tensor", ("fsdp", "context")),
        P(("fsdp", "context")),
        P(("fsdp", "context")),
        P(("fsdp", "context")),
        P("context", "fsdp", None),
    )
    out_specs = (
        P("context", "fsdp", None),
        P("context", "fsdp", None),
        P(("fsdp", "context"), "tensor"),
        P("tensor"),
        P(("fsdp", "context"), "tensor"),
        P(("fsdp", "context"), "tensor"),
        P("tensor"),
        P("tensor", ("fsdp", "context")),
        P(("fsdp", "context")),
        P(("fsdp", "context")),
        P(("fsdp", "context")),
        P(("fsdp", "context"), "tensor"),
        P("tensor"),
        P("tensor", ("fsdp", "context")),
        P(("fsdp", "context")),
        P(("fsdp", "context")),
        P(("fsdp", "context")),
        P(),
    )
    return jax.shard_map(body, mesh=mesh, in_specs=in_specs, out_specs=out_specs, check_vma=False)
```

profile of v0, /device:TPU:0, one launch (start us, length us, event | category | flops | bytes accessed | tf_op | source)
XLA Modules:
  0.0 327.4 jit_solution(11868828175268627122)
XLA Ops:
  0.7 2.0 copy.56
  2.6 1.8 copy.58.outer
  4.5 1.5 copy.57.output
  5.9 0.8 stack.27
  6.7 0.6 pad.9.vectors
  7.3 0.7 concatenate.40
  8.0 0.7 concatenate.38
  8.7 0.7 concatenate.39
  9.4 0.6 maximum_convert_fusion.bias
  10.0 119.8 %forward_layers.1 = (bf16[256,1024]{1,0:T(8,128)(2,1)}, f32[8,1024]{1,0:T(8,128)}, f32[8,1024]{1,0:T(8,128)}, bf16[2,4,2,4,16,6272]{5,4,3,2,1,0:T(8,128)(2,1)}, ...) custom-call(bf16[256,1024]{1,0:T(8,128)(2,1)} %bitcast.147, ...), custom_call_target="tpu_custom_call" | custom-call | tf_op jit(solution)/shard_map/forward_layers/pallas_call | solution.py:618
  129.8 4.5 %slice_bitcast_fusion = (f32[256,1024]{1,0:T(8,128)}, f32[256,1024]{1,0:T(8,128)}, f32[256,1024]{1,0:T(8,128)}, f32[256,1024]{1,0:T(8,128)}) fusion(f32[2,2,256,1024]{3,2,1,0:T(8,128)} %get-tuple-element.55), kind=kLoop, calls=%fused_computation.17 | loop fusion | bytes 8388608 | tf_op jit(solution)/shard_map/squeeze | solution.py:985
  134.3 0.8 slice_bitcast_fusion.11
  135.1 1.5 slice_bitcast_fusion.1
  137.4 1.1 bitcast_multiply_fusion.grad_ref
  138.5 12.9 %backward.2 = (bf16[256,1024]{1,0:T(8,128)(2,1)}, bf16[256,2048]{1,0:T(8,128)(2,1)}, f32[256,1024]{1,0:T(8,128)}, bf16[256,1024]{1,0:T(8,128)(2,1)}, bf16[256,51...) custom-call(f32[256,1024]{1,0:T(8,128)} %bitcast_multiply_fusion.grad_ref, ...), custom_call_target="tpu_custom_call" | custom-call | tf_op jit(solution)/shard_map/backward/pallas_call | solution.py:746
  151.4 1.3 slice_bitcast_fusion.6
  152.6 1.1 slice_bitcast_fusion.8
  153.7 0.6 slice_bitcast_fusion.17
  154.3 30.1 %attend_back.2 = (bf16[3,256,512]{2,1,0:T(8,128)(2,1)}, f32[256,1024]{1,0:T(8,128)}, f32[8,512]{1,0:T(8,128)}) custom-call(bf16[256,512]{1,0:T(8,128)(2,1)} %get-tuple-element.60.mixed_grad_ref, bf16[3,1024,128]{2,1,0:T(8,128)(2,1)} %get-tuple-element.103.unit_ref, f32[1024,128]{1,0:T(8,128)} %get-tuple-element.105.outcome_ref, ...), custom_call_target="tpu_custom_call" | custom-call | tf_op jit(solution)/shard_map/attend_back/pallas_call | solution.py:909
  184.4 13.2 %backward.3 = (bf16[256,1024]{1,0:T(8,128)(2,1)}, bf16[256,2048]{1,0:T(8,128)(2,1)}, f32[256,1024]{1,0:T(8,128)}, bf16[256,1024]{1,0:T(8,128)(2,1)}, bf16[256,51...) custom-call(f32[256,1024]{1,0:T(8,128)} %get-tuple-element.65.grad_ref, ...), custom_call_target="tpu_custom_call" | custom-call | tf_op jit(solution)/shard_map/backward/pallas_call | solution.py:746
  197.6 28.0 %attend_back.3 = (bf16[3,256,512]{2,1,0:T(8,128)(2,1)}, f32[256,1024]{1,0:T(8,128)}, f32[8,512]{1,0:T(8,128)}) custom-call(bf16[256,512]{1,0:T(8,128)(2,1)} %get-tuple-element.66.mixed_grad_ref, bf16[3,1024,128]{2,1,0:T(8,128)(2,1)} %get-tuple-element.102.unit_ref, f32[1024,128]{1,0:T(8,128)} %get-tuple-element.104.outcome_ref, ...), custom_call_target="tpu_custom_call" | custom-call | tf_op jit(solution)/shard_map/attend_back/pallas_call | solution.py:909
  225.7 0.7 add.54
  226.6 0.7 fusion.35
  227.2 1.3 concatenate.50
  228.6 1.3 fusion.4
  229.9 1.3 add_convert_fusion
  231.4 1.3 fusion.9
  232.8 1.3 add_convert_fusion.1
  234.6 0.5 add_convert_fusion.2
  235.9 0.5 fusion
  236.8 0.5 fusion.1
  237.3 0.5 fusion.23
  237.8 0.5 fusion.2
  238.8 0.5 constant_dynamic-update-slice_fusion.2
  239.4 0.5 constant_dynamic-update-slice_fusion.1
  239.9 4.6 %copy-done = bf16[2,4,2,4,16,6272]{5,4,3,2,1,0:T(8,128)(2,1)} copy-done((bf16[2,4,2,4,16,6272]{5,4,3,2,1,0:T(8,128)(2,1)}, bf16[2,4,2,4,16,6272]{5,4,3,2,1,0:T(8,128)(2,1)S(1)}, u32[]{:S(2)}) %copy-start) | copy-done | bytes 12845080
  244.8 0.7 constant_dynamic-update-slice_fusion.all_ref
  245.5 67.8 %scatter_grads.1 = (f32[16,6272]{1,0:T(8,128)}, f32[32,128]{1,0:T(8,128)}) custom-call(bf16[2,4,2,4,16,6272]{5,4,3,2,1,0:T(8,128)(2,1)} %constant_dynamic-update-slice_fusion.all_ref, f32[32,128]{1,0:T(8,128)} %bitcast.161), custom_call_target="tpu_custom_call" | custom-call | tf_op jit(solution)/shard_map/scatter_grads/pallas_call | solution.py:234
  313.3 1.3 slice.214
  315.3 0.7 fusion.38
  315.9 0.7 sqrt.7
  316.6 1.7 slice_bitcast_fusion.10
  318.3 1.5 slice_bitcast_fusion.15
  319.7 1.3 slice_bitcast_fusion.16
  321.0 1.3 slice_bitcast_fusion.19
  322.4 1.7 slice_reduce_fusion.1
  324.1 1.8 copy.72
  325.9 1.3 copy.73
  (77 shorter events, 3.6 us)
Async XLA Ops:
  129.8 4.5 %copy-start.18 = (f32[2,2,256,1]{3,2,1,0:T(8,128)S(1)}, f32[2,2,256,1]{3,2,1,0:T(8,128)}, u32[]{:S(2)}) copy-start(f32[2,2,256,1]{3,2,1,0:T(8,128)} %get-tuple-element.56) | copy-start | bytes 12292
  129.8 5.3 %copy-start.4 = (bf16[2,256,2048]{2,1,0:T(8,128)(2,1)S(1)}, bf16[2,256,2048]{2,1,0:T(8,128)(2,1)}, u32[]{:S(2)}) copy-start(bf16[2,256,2048]{2,1,0:T(8,128)(2,1)} %get-tuple-element.57) | copy-start | bytes 6291460
  134.3 2.3 copy-start.26
  134.3 2.4 copy-start.15
  138.5 12.9 %copy-start.5 = (bf16[2,3,1024,128]{3,2,1,0:T(8,128)(2,1)S(1)}, bf16[2,3,1024,128]{3,2,1,0:T(8,128)(2,1)}, u32[]{:S(2)}) copy-start(bf16[2,3,1024,128]{3,2,1,0:T(8,128)(2,1)} %get-tuple-element.61) | copy-start | bytes 4718596
  138.5 14.2 %copy-start.10 = (f32[2,1024,128]{2,1,0:T(8,128)S(1)}, f32[2,1024,128]{2,1,0:T(8,128)}, u32[]{:S(2)}) copy-start(f32[2,1024,128]{2,1,0:T(8,128)} %get-tuple-element.62) | copy-start | bytes 3145732
  151.4 2.3 copy-start.25
  197.6 28.1 %copy-start.24 = (f32[8,512]{1,0:T(8,128)S(1)}, f32[8,512]{1,0:T(8,128)}, u32[]{:S(2)}) copy-start(f32[8,512]{1,0:T(8,128)} %get-tuple-element.83) | copy-start | bytes 49156
  197.6 28.8 %copy-start.28 = (f32[1,2048]{1,0:T(1,128)S(1)}, f32[1,2048]{1,0:T(1,128)}, u32[]{:S(2)}) copy-start(f32[1,2048]{1,0:T(1,128)} %get-tuple-element.85) | copy-start | bytes 24580
  197.6 28.8 %copy-start.29 = (f32[1,2048]{1,0:T(1,128)S(1)}, f32[1,2048]{1,0:T(1,128)}, u32[]{:S(2)}) copy-start(f32[1,2048]{1,0:T(1,128)} %get-tuple-element.86) | copy-start | bytes 24580
  197.6 28.8 %copy-start.22 = (f32[8,1024]{1,0:T(8,128)S(1)}, f32[8,1024]{1,0:T(8,128)}, u32[]{:S(2)}) copy-start(f32[8,1024]{1,0:T(8,128)} %get-tuple-element.87) | copy-start | bytes 98308
  197.6 28.9 %copy-start.27 = (s32[2]{0:T(128)S(1)}, s32[2]{0:T(128)}, u32[]{:S(2)}) copy-start(s32[2]{0:T(128)} %lengths.5) | copy-start | bytes 28
  197.6 30.9 %copy-start.3 = (bf16[2,256,2048]{2,1,0:T(8,128)(2,1)S(1)}, bf16[2,256,2048]{2,1,0:T(8,128)(2,1)}, u32[]{:S(2)}) copy-start(bf16[2,256,2048]{2,1,0:T(8,128)(2,1)} %get-tuple-element.79) | copy-start | bytes 6291460
  197.6 30.9 %copy-start.11 = (bf16[256,1024]{1,0:T(8,128)(2,1)S(1)}, bf16[256,1024]{1,0:T(8,128)(2,1)}, u32[]{:S(2)}) copy-start(bf16[256,1024]{1,0:T(8,128)(2,1)} %get-tuple-element.78) | copy-start | bytes 1572868
  228.6 1.3 copy-start.14
  229.9 1.4 copy-start.6
  229.9 1.5 copy-start.7
  231.4 1.3 copy-start.8
  232.7 1.4 copy-start.19
  232.7 1.4 copy-start.20
  232.7 1.9 copy-start.16
  234.1 1.0 copy-start.2
  234.1 1.3 copy-start.12
  234.1 1.7 copy-start.1
  234.1 1.7 copy-start.13
  239.3 5.2 %copy-start.21 = (f32[8,1024]{1,0:T(8,128)S(1)}, f32[8,1024]{1,0:T(8,128)}, u32[]{:S(2)}) copy-start(f32[8,1024]{1,0:T(8,128)} %get-tuple-element.81) | copy-start | bytes 98308
  239.4 5.1 %copy-start.23 = (f32[8,1024]{1,0:T(8,128)S(1)}, f32[8,1024]{1,0:T(8,128)}, u32[]{:S(2)}) copy-start(f32[8,1024]{1,0:T(8,128)} %get-tuple-element.82) | copy-start | bytes 98308
  239.9 4.6 %copy-start = (bf16[2,4,2,4,16,6272]{5,4,3,2,1,0:T(8,128)(2,1)}, bf16[2,4,2,4,16,6272]{5,4,3,2,1,0:T(8,128)(2,1)S(1)}, u32[]{:S(2)}) copy-start(bf16[2,4,2,4,16,6272]{5,4,3,2,1,0:T(8,128)(2,1)S(1)} %constant_dynamic-update-slice_fusion.1) | copy-start | bytes 38535172
  245.5 78.5 %copy-start.9 = (f32[256,1024]{1,0:T(8,128)S(1)}, f32[256,1024]{1,0:T(8,128)}, u32[]{:S(2)}) copy-start(f32[256,1024]{1,0:T(8,128)} %get-tuple-element.68) | copy-start | bytes 3145732
  245.5 80.3 %copy-start.17 = (bf16[256,1024]{1,0:T(8,128)(2,1)S(1)}, bf16[256,1024]{1,0:T(8,128)(2,1)}, u32[]{:S(2)}) copy-start(bf16[256,1024]{1,0:T(8,128)(2,1)} %get-tuple-element.54) | copy-start | bytes 1572868
where the time goes:
time: 331 us; the launch traced here: 327 us
  Pallas kernels  272 us (82%)
  local copies, waits for them, and re-layouts  40.3 us (12%)
  matrix products  9.03 us (3%)
  other arithmetic  4.38 us (1%)
    pallas_call x1, Pallas kernels, run_forward(): pl.pallas_call(forward_kernel, out_shape=(jax.ShapeDtypeStruct((256, 1024...  120 us
    pallas_call x1, Pallas kernels, scatter_all(): pl.pallas_call(scatter_kernel, out_shape=(jax.ShapeDtypeStruct((rows, wid...  67.8 us
    pallas_call x2, Pallas kernels, attend_back(): pl.pallas_call(attend_back_kernel, out_shape=(jax.ShapeDtypeStruct((3, 25...  58.1 us
    pallas_call x2, Pallas kernels, backward(): pl.pallas_call(backward_kernel, out_shape=(jax.ShapeDtypeStruct((256, 102...  26.1 us
    unnamed x69, local copies, waits for them, and re-layouts  10.2 us
    dot_general x12, matrix products, twice(): lax.dot_general(left(t), right(t), (((0,), (0,)), ((), ())), preferred_el...  9.03 us

commit v1 on v0

--- a/solution.py
+++ b/solution.py
@@ -125,118 +125,6 @@
 
 def part(ref, peer):
     return ref.at[rows_of(peer // 4), rows_of(peer % 4)]
-
-
-def parts_of(width):
-    tiles = width//LANES
-    cuts = [tiles*i//6*LANES for i in range(7)]
-    return [((cuts[2*i], cuts[2*i+1]-cuts[2*i]), (cuts[2*i+1], cuts[2*i+2]-cuts[2*i+1])) for i in range(3)]
-
-def scatter_kernel(all_ref, small_ref, own_ref, total_ref, work, small_land, load_sem, send_sem, recv_sem, small_send, small_recv, *landings):
-    at = place()
-    parts = parts_of(all_ref.shape[-1])
-    loads=[]
-    for part in range(3):
-        lo,hi=parts[part]; both=pl.ds(lo[0],lo[1]+hi[1])
-        cp=pltpu.make_async_copy(all_ref.at[:,:,:,:,:,both], work.at[:,:,:,:,:,both], load_sem.at[part]); cp.start(); loads.append(cp)
-    greet(neighbours(at, (1, 2, 3)))
-    for cp in loads: cp.wait()
-
-    def push(part,phase,kind,origin,whole,cols,axis,step):
-        land=landings[phase*3+part]
-        src=shards(work,origin,whole,cols)
-        return pltpu.make_async_remote_copy(src_ref=src,dst_ref=land.at[kind] if cols[1]==land.shape[-1] else land.at[kind,...,pl.ds(0,cols[1])],send_sem=send_sem.at[part,phase,kind],recv_sem=recv_sem.at[part,phase,kind],device_id=device(shifted(at,axis,step)),device_id_type=MESH)
-
-    def add(origin,whole,cols,land_list):
-        x=origin["x"]
-        xs=[(a,b) for a in range(2) for b in range(2)] if "x" in whole else [(x//2,x%2)]
-        zs=list(range(4)) if "z" in whole else [origin["z"]]
-        ys=list(range(4)) if "y" in whole else [origin["y"]]
-        sx="x" in whole; sz="z" in whole; sy="y" in whole
-        def one(ix,iz,iy):
-            xh,xl=(ix//2,ix%2) if sx else (x//2,x%2)
-            z=iz if sz else origin["z"]; y=iy if sy else origin["y"]
-            index=(xh,z,xl,y,slice(None),pl.ds(cols[0],cols[1]))
-            total=work[index].astype(jnp.float32)
-            for land,kind in land_list:
-                li=(kind,)
-                if sx: li+=(xh,)
-                if sz: li+=(z,)
-                if sx: li+=(xl,)
-                if sy: li+=(y,)
-                li+=(slice(None),pl.ds(0,cols[1]))
-                total=total+land[li].astype(jnp.float32)
-            work[index]=total.astype(work.dtype)
-        nx=4 if sx else 1; nz=4 if sz else 1; ny=4 if sy else 1
-        n=nx*nz*ny
-        def body(i,_):
-            one(i//(nz*ny), (i//ny)%nz, i%ny); return 0
-        if n==1: one(0,0,0)
-        else: lax.fori_loop(0,n,body,0)
-
-    total_ref[...]=small_ref[...]
-    for phase in range(3):
-        early=[]
-        small=[]
-        for step in (1,2,3):
-            cp=pltpu.make_async_remote_copy(src_ref=total_ref,dst_ref=small_land.at[phase,step-1],send_sem=small_send.at[phase,step-1],recv_sem=small_recv.at[phase,step-1],device_id=device(shifted(at,"xyz"[phase],step)),device_id_type=MESH)
-            cp.start(); small.append(cp)
-        for part in range(3):
-            order=ORDERS[part][::-1]; axis=order[phase]; whole=order[phase+1:]
-            lo,hi=parts[part]
-            far=shifted(at,axis,2); up=shifted(at,axis,1); down=shifted(at,axis,-1)
-            a=push(part,phase,0,far,whole,lo,axis,1); a.start()
-            b=push(part,phase,1,far,whole,hi,axis,-1); b.start()
-            c=push(part,phase,2,up,whole,hi,axis,1); c.start()
-            d=push(part,phase,3,down,whole,lo,axis,-1); d.start()
-            early.append((a,b,c,d))
-        late=[]
-        for part in range(3):
-            order=ORDERS[part][::-1]; axis=order[phase]; whole=order[phase+1:]
-            lo,hi=parts[part]; land=landings[phase*3+part]
-            up=shifted(at,axis,1); down=shifted(at,axis,-1)
-            a,b,c,d=early[part]
-            a.wait_recv(); add(up,whole,lo,[(land,0)])
-            e=push(part,phase,4,up,whole,lo,axis,1); e.start()
-            b.wait_recv(); add(down,whole,hi,[(land,1)])
-            f=push(part,phase,5,down,whole,hi,axis,-1); f.start()
-            late.append((e,f))
-        for part in range(3):
-            order=ORDERS[part][::-1]; axis=order[phase]; whole=order[phase+1:]
-            lo,hi=parts[part]; land=landings[phase*3+part]
-            a,b,c,d=early[part]; e,f=late[part]
-            c.wait_recv(); f.wait_recv()
-            add(at,whole,hi,[(land,2),(land,5)])
-            d.wait_recv(); e.wait_recv()
-            add(at,whole,lo,[(land,3),(land,4)])
-        for part in range(3):
-            for cp in early[part]+late[part]: cp.wait_send()
-        for cp in small: cp.wait_recv()
-        for cp in small: cp.wait_send()
-        total_ref[...]=total_ref[...]+small_land[phase,0]+small_land[phase,1]+small_land[phase,2]
-    x=at["x"]
-    own_ref[...]=work[x//2,at["z"],x%2,at["y"]].astype(jnp.float32)
-
-def scatter_all(whole, small):
-    rows,width=whole.shape[-2:]
-    parts=parts_of(width)
-    landings=[]
-    for phase in range(3):
-        for part in range(3):
-            order=ORDERS[part][::-1]; w=order[phase+1:]
-            shape=[6]
-            if "x" in w: shape.append(2)
-            if "z" in w: shape.append(4)
-            if "x" in w: shape.append(2)
-            if "y" in w: shape.append(4)
-            shape+= [rows, max(parts[part][0][1],parts[part][1][1])]
-            landings.append(pltpu.VMEM(tuple(shape), whole.dtype))
-    return pl.pallas_call(scatter_kernel,
-        out_shape=(jax.ShapeDtypeStruct((rows,width), jnp.float32),jax.ShapeDtypeStruct(small.shape, jnp.float32)),
-        in_specs=[pl.BlockSpec(memory_space=pl.ANY),pl.BlockSpec(memory_space=pltpu.VMEM)], out_specs=(pl.BlockSpec(memory_space=pltpu.VMEM),pl.BlockSpec(memory_space=pltpu.VMEM)),
-        scratch_shapes=[pltpu.VMEM(whole.shape, whole.dtype), pltpu.VMEM((3,3)+small.shape,jnp.float32), pltpu.SemaphoreType.DMA((3,)), pltpu.SemaphoreType.DMA((3,3,6)), pltpu.SemaphoreType.DMA((3,3,6)), pltpu.SemaphoreType.DMA((3,3)), pltpu.SemaphoreType.DMA((3,3))]+landings,
-        compiler_params=pltpu.CompilerParams(collective_id=2, has_side_effects=True, vmem_limit_bytes=60*2**20),
-        name="scatter_grads")(whole, small)
 
 
 class Gather:
@@ -669,275 +557,574 @@
     )
 
 
+class Scatter:
+    def __init__(self, work, group, landings, send_sem, recv_sem):
+        self.at = place()
+        self.work, self.group, self.landings = work, group, landings
+        self.send_sem, self.recv_sem = send_sem, recv_sem
+        self.parts = thirds(group)
+        self.sent = {}
+
+    def ring(self, third, phase):
+        order = ORDERS[third][::-1]
+        return order[phase], order[phase + 1 :]
+
+    def send(self, third, phase, kind, away, cols, step):
+        axis, whole = self.ring(third, phase)
+        land = self.landings[third][phase].at[kind]
+        if cols[1] != land.shape[-1]:
+            land = land.at[..., pl.ds(0, cols[1])]
+        index = (self.group, third, phase, kind)
+        copy = remote(
+            shards(self.work, shifted(self.at, axis, away), whole, cols), land,
+            self.send_sem.at[index], self.recv_sem.at[index], device(shifted(self.at, axis, step)),
+        )
+        copy.start()
+        self.sent[third, phase, kind] = copy
+
+    def add(self, third, phase, away, cols, kinds):
+        axis, whole = self.ring(third, phase)
+        origin = shifted(self.at, axis, away)
+        land = self.landings[third][phase]
+        x = origin["x"]
+        wide = {name: name in whole for name in "xyz"}
+        columns = pl.ds(cols[0], cols[1])
+
+        def one(ix, iz):
+            xh, xl = (ix // 2, ix % 2) if wide["x"] else (x // 2, x % 2)
+            z = iz if wide["z"] else origin["z"]
+            y = slice(None) if wide["y"] else origin["y"]
+            index = (xh, z, xl, y, slice(None), columns)
+            total = self.work[index].astype(F32)
+            for kind in kinds:
+                at = (kind,)
+                at += (xh,) if wide["x"] else ()
+                at += (z,) if wide["z"] else ()
+                at += (xl,) if wide["x"] else ()
+                at += (slice(None),) if wide["y"] else ()
+                total = total + land[at + (slice(None), pl.ds(0, cols[1]))].astype(F32)
+            self.work[index] = total.astype(BF16)
+
+        count_x = 4 if wide["x"] else 1
+        count_z = 4 if wide["z"] else 1
+        if count_x * count_z == 1:
+            one(0, 0)
+        else:
+            def turn(i, carry):
+                one(i // count_z, i % count_z)
+                return carry
+
+            lax.fori_loop(0, count_x * count_z, turn, 0)
+
+    def first(self, phase, third):
+        low, high = self.parts[third]
+        self.send(third, phase, 0, 2, low, 1)
+        self.send(third, phase, 1, 2, high, -1)
+        self.send(third, phase, 2, 1, high, 1)
+        self.send(third, phase, 3, -1, low, -1)
+
+    def onward(self, phase, third):
+        low, high = self.parts[third]
+        self.sent[third, phase, 0].wait_recv()
+        self.add(third, phase, 1, low, (0,))
+        self.send(third, phase, 4, 1, low, 1)
+        self.sent[third, phase, 1].wait_recv()
+        self.add(third, phase, -1, high, (1,))
+        self.send(third, phase, 5, -1, high, -1)
+
+    def settle(self, phase, third):
+        low, high = self.parts[third]
+        self.sent[third, phase, 2].wait_recv()
+        self.sent[third, phase, 5].wait_recv()
+        self.add(third, phase, 0, high, (2, 5))
+        self.sent[third, phase, 3].wait_recv()
+        self.sent[third, phase, 4].wait_recv()
+        self.add(third, phase, 0, low, (3, 4))
+
+    def close(self):
+        for copy in self.sent.values():
+            copy.wait_send()
+
+
+def landing_shapes(group):
+    shapes = []
+    for third in range(3):
+        order = ORDERS[third][::-1]
+        low, high = thirds(group)[third]
+        for phase in range(3):
+            whole = order[phase + 1 :]
+            shape = [6]
+            shape += [2] if "x" in whole else []
+            shape += [4] if "z" in whole else []
+            shape += [2] if "x" in whole else []
+            shape += [4] if "y" in whole else []
+            shapes.append(pltpu.VMEM((*shape, 16, max(low[1], high[1])), BF16))
+    return shapes
+
+
+class Totals:
+    def __init__(self, total, landed, send_sem, recv_sem):
+        self.at = place()
+        self.total, self.landed, self.send_sem, self.recv_sem = total, landed, send_sem, recv_sem
+
+    def copy(self, phase, step):
+        return remote(
+            self.total, self.landed.at[phase, step - 1], self.send_sem.at[phase, step - 1],
+            self.recv_sem.at[phase, step - 1], device(shifted(self.at, "xyz"[phase], step)),
+        )
+
+    def first(self, phase):
+        for step in (1, 2, 3):
+            self.copy(phase, step).start()
+
+    def settle(self, phase):
+        for step in (1, 2, 3):
+            self.copy(phase, step).wait()
+        self.total[...] += self.landed[phase, 0] + self.landed[phase, 1] + self.landed[phase, 2]
+
+
+class HeadsBack:
+    def __init__(self, mixed_grad, taken, key_value, query, grads, local_sem, send_sem, recv_sem, back_send, back_recv):
+        self.f = lax.axis_index("fsdp")
+        self.c = lax.axis_index("context")
+        self.t = lax.axis_index("tensor")
+        self.mixed_grad, self.taken, self.grads = mixed_grad, taken, grads
+        self.sources = (key_value.at[0], key_value.at[1], query)
+        self.key_value, self.query = key_value, query
+        self.local_sem, self.send_sem, self.recv_sem = local_sem, send_sem, recv_sem
+        self.back_send, self.back_recv = back_send, back_recv
+
+    def push(self, d):
+        peer = lax.rem(self.c + d, 8)
+        return remote(
+            part(self.mixed_grad, peer), self.taken.at[rows_of(self.c)],
+            self.send_sem.at[d - 1], self.recv_sem.at[d - 1], (self.f, peer, self.t),
+        )
+
+    def keep(self):
+        return pltpu.make_async_copy(
+            part(self.mixed_grad, self.c), self.taken.at[rows_of(self.c)], self.local_sem.at[3]
+        )
+
+    def answer(self, j, d):
+        peer = lax.rem(self.c + d, 8)
+        return remote(
+            self.sources[j].at[rows_of(peer)], part(self.grads.at[j], self.c),
+            self.back_send.at[j, d - 1], self.back_recv.at[j, d - 1], (self.f, peer, self.t),
+        )
+
+    def keep_back(self, j):
+        return pltpu.make_async_copy(
+            self.sources[j].at[rows_of(self.c)], part(self.grads.at[j], self.c), self.local_sem.at[j]
+        )
+
+    def start(self):
+        for d in (4, 1, 7, 5, 3, 2, 6):
+            self.push(d).start()
+        self.keep().start()
+
+    def attend(self, length, unit, exact, logs_ref, grad_buf, query_sum):
+        c = self.c
+        scale = jnp.asarray(0.125, BF16)
+        queries = jnp.concatenate(
+            [by_head(unit[2, pl.ds(block * ROWS, ROWS), :] * scale) for block in range(8)], 0
+        )
+        logs = jnp.concatenate([logs_ref[block : block + 1, :] for block in range(8)], 1)
+        query_sum[...] = jnp.zeros_like(query_sum)
+        self.keep().wait()
+        for d in range(1, 8):
+            self.push(d).wait_recv()
+        for block in range(8):
+            grad_buf[pl.ds(block * 256, 256), :] = by_head(self.taken[pl.ds(block * ROWS, ROWS), :])
+        head_row = lax.broadcasted_iota(jnp.int32, (8, LANES), 0)
+        head_lane = lax.broadcasted_iota(jnp.int32, (8, LANES), 1) // HEAD
+        chosen = jnp.where(head_row == head_lane, 1.0, 0.0)
+        weighted = lax.dot_general(
+            chosen, self.taken[...].astype(F32) * exact[...],
+            (((1,), (1,)), ((), ())), precision=lax.Precision.HIGHEST, preferred_element_type=F32,
+        )
+        delta = jnp.concatenate(
+            [
+                weighted[head : head + 1, block * ROWS : (block + 1) * ROWS]
+                for block in range(8)
+                for head in range(2)
+            ],
+            1,
+        )
+
+        def step(turn, carry):
+            pair = lax.rem(c // 2 + turn, 4)
+            spot = pl.ds(pl.multiple_of(pair * 256, 256), 256)
+            keys = unit[0, spot, :]
+            values = unit[1, spot, :]
+            scores = across(keys, queries) + key_mask(length, pair * 256, 256)
+            soft = jnp.exp(scores - logs)
+            self.key_value[1, spot, :] = straight(soft.astype(BF16), grad_buf[...]).astype(BF16)
+            soft_grad = across(values, grad_buf[...])
+            score_grad = (soft * (soft_grad - delta)).astype(BF16)
+            self.key_value[0, spot, :] = straight(score_grad, queries).astype(BF16)
+            query_sum[...] += lax.dot_general(
+                score_grad, keys, (((0,), (0,)), ((), ())), preferred_element_type=F32
+            )
+
+            for side in range(2):
+                d = lax.rem(pair * 2 + side - c + 8, 8)
+
+                @pl.when(d > 0)
+                def _():
+                    for j in range(2):
+                        self.answer(j, d).start()
+
+            return carry
+
+        lax.fori_loop(1, 5, step, 0)
+        first_lane = lax.broadcasted_iota(jnp.int32, (ROWS, LANES), 1) < HEAD
+        for block in range(8):
+            start = block * 256
+            total = jnp.where(
+                first_lane, query_sum[pl.ds(start, ROWS), :], query_sum[pl.ds(start + ROWS, ROWS), :]
+            )
+            self.query[pl.ds(block * ROWS, ROWS), :] = (total * 0.125).astype(BF16)
+        for d in (4, 1, 7, 5, 3, 2, 6):
+            self.answer(2, d).start()
+        for j in range(3):
+            self.keep_back(j).start()
+
+    def collect(self, j):
+        self.keep_back(j).wait()
+        for d in range(1, 8):
+            self.answer(j, d).wait_recv()
+
+    def close(self):
+        for d in range(1, 8):
+            self.push(d).wait_send()
+            for j in range(3):
+                self.answer(j, d).wait_send()
+
+
+def put_quarter(work, quarter, start, value):
+    z = 2 * (quarter % 2)
+    work[quarter // 2, z : z + 2, :, :, :, pl.ds(start, value.shape[1])] = value.astype(BF16).reshape(
+        2, 2, 4, 16, value.shape[1]
+    )
+
+
+def weight_grad(work, start, left, right, width):
+    turned = left.T
+    tile = 512
+
+    def turn(i, carry):
+        offset = pl.multiple_of(i * tile, tile)
+        term = right[:, :, pl.ds(offset, tile)].reshape(512, tile)
+        for quarter in range(4):
+            put_quarter(work, quarter, start + offset, straight(turned[quarter * 256 : quarter * 256 + 256], term))
+        return carry
+
+    lax.fori_loop(0, width // tile, turn, 0)
+
+
 def backward_kernel(
-    grad_ref, normed2_ref, inverse2_ref, slope_ref, normed1_ref, inverse1_ref, w_ref, vectors_ref,
-    outer_grad_ref, inner_grad_ref, first_ref, attn_ref, mixed_grad_ref, sums_ref, bias_ref,
-    out_w, inner_w, outer_w, second_buf, sent, landed, w_sem, send_sem, recv_sem,
+    cotangent, low0, rows_ref, squares, lengths,
+    w_in, unit_in, exact_in, logs_in, mixed_in, normed_in, inverse_in, middle_in, act_in, slope_in, low1_in,
+    stream_grad, query_out, key_out, value_out, output_out, inner_out, outer_out, vector_out, total_ref, root_ref,
+    weights, unit, exact, logs, mixed, normed, inverse, middle, act, slope, low,
+    attn_grad, inner_grad, outer_grad, grads, mixed_grad, trunk,
+    taken, grad_buf, query_sum, key_value, query_buf, sent, landed, total_land,
+    load_sem, local_sem, send_sem, recv_sem, back_send, back_recv, pair_send, pair_recv,
+    total_send, total_recv, scatter_send, scatter_recv, *landings,
 ):
-    f = lax.axis_index("fsdp")
+    at = place()
     c = lax.axis_index("context")
     t = lax.axis_index("tensor")
-    partner = (f, c, 1 - t)
-    loads = []
-    for j, (column, buffer) in enumerate(((4096, outer_w), (2048, inner_w), (1536, out_w))):
-        load = pltpu.make_async_copy(
-            w_ref.at[:, pl.ds(column, buffer.shape[1])], buffer, w_sem.at[j]
-        )
-        load.start()
-        loads.append(load)
-    greet([partner])
-
-    def join(half):
-        return remote(
-            sent.at[half], landed.at[half], send_sem.at[half], recv_sem.at[half], partner
-        )
-
-    def rows(half):
-        return pl.ds(half * ROWS, ROWS)
-
-    sums = [0.0] * 6
-    for half in range(2):
-        grad = grad_ref[rows(half), :]
-        normed = normed2_ref[rows(half), :]
-        second = norm_back(grad, normed, inverse2_ref[rows(half), :], vectors_ref[4:5, :])
-        low = second.astype(BF16)
-        second_buf[rows(half), :] = second
-        outer_grad_ref[rows(half), :] = low
-        sums[4] += jnp.sum(grad * normed, 0, keepdims=True)
-        sums[5] += jnp.sum(grad, 0, keepdims=True)
-        sums[1] += jnp.sum(low.astype(F32), 0, keepdims=True)
-    loads[0].wait()
-
-    def inner(tile, carry):
-        columns = pl.ds(pl.multiple_of(tile * 512, 512), 512)
-        act = straight(outer_grad_ref[...], outer_w[:, columns])
-        low = (act * slope_ref[:, columns].astype(F32)).astype(BF16)
-        inner_grad_ref[:, columns] = low
-        bias_ref[:, columns] = jnp.sum(low.astype(F32), 0, keepdims=True)
-        return carry
-
-    lax.fori_loop(0, 4, inner, 0)
-    loads[1].wait()
-    for half in range(2):
-        sent[half] = across(inner_grad_ref[rows(half), :], inner_w[...]).astype(BF16)
-        join(half).start()
-    loads[2].wait()
-    for half in range(2):
-        join(half).wait_recv()
-        middle = second_buf[rows(half), :] + (sent[half].astype(F32) + landed[half].astype(F32))
-        normed = normed1_ref[rows(half), :]
-        sums[2] += jnp.sum(middle * normed, 0, keepdims=True)
-        sums[3] += jnp.sum(middle, 0, keepdims=True)
-        first = norm_back(middle, normed, inverse1_ref[rows(half), :], vectors_ref[2:3, :])
-        low = first.astype(BF16)
-        first_ref[rows(half), :] = first
-        attn_ref[rows(half), :] = low
-        sums[0] += jnp.sum(low.astype(F32), 0, keepdims=True)
-        mixed_grad_ref[rows(half), :] = straight(low, out_w[...]).astype(BF16)
-    sums_ref[...] = jnp.zeros_like(sums_ref)
-    for j in range(6):
-        sums_ref[j : j + 1, :] = sums[j]
-    for half in range(2):
-        join(half).wait_send()
-
-
-def backward(grad, saved, gathered, vectors):
-    normed1, inverse1, slope, normed2, inverse2 = saved
+    partner = (lax.axis_index("fsdp"), c, 1 - t)
+    loads, started = {}, []
+
+    def load(name, source, target):
+        copy = pltpu.make_async_copy(source, target, load_sem.at[len(started)])
+        copy.start()
+        started.append(copy)
+        loads[name] = copy
+
+    def load_weights(name, start, width):
+        columns = (slice(None),) * 5 + (pl.ds(start, width),)
+        load(name, w_in.at[columns], weights.at[columns])
+
+    load("normed", normed_in.at[1], normed)
+    load("inverse", inverse_in.at[1], inverse)
+    load_weights("outer", OUTER, 2048)
+    load("slope", slope_in.at[1], slope)
+    load_weights("inner", INNER, 2048)
+    load_weights("out", OUT, 512)
+    load("unit", unit_in.at[1], unit)
+    load("exact", exact_in.at[1], exact)
+    load("logs", logs_in.at[1], logs)
+    load_weights("qkv", QUERY, 1536)
+    load("act", act_in, act)
+    load("mixed", mixed_in, mixed)
+    load("middle", middle_in, middle)
+    load("low1", low1_in, low.at[1])
+    low[0] = low0[...]
+    greet(neighbours(at, (1, 2, 3)) + context_peers() + [partner])
+
+    three = [landings[9 * group : 9 * group + 9] for group in range(2)]
+    one, two = (
+        Scatter(weights, group, [three[group][3 * i : 3 * i + 3] for i in range(3)], scatter_send, scatter_recv)
+        for group in range(2)
+    )
+    zero = jnp.zeros((1, 1024), F32)
+    sums = [zero] * 6
+    bias_sum = jnp.zeros((1, 2048), F32)
+    head_sum = [jnp.zeros((1, 512), F32)] * 2
+    length = lengths[c // 4]
+    closing = [one, two]
+    total_ref[...] = jnp.zeros_like(total_ref)
+
+    for layer in (1, 0):
+        last = layer == 0
+        joins = [
+            Joins(sent.at[layer, stage], landed.at[layer, stage], pair_send.at[layer, stage], pair_recv.at[layer, stage])
+            for stage in range(2)
+        ]
+        heads = HeadsBack(
+            mixed_grad.at[layer], taken.at[layer], key_value.at[layer], query_buf.at[layer], grads.at[layer],
+            local_sem.at[layer], send_sem.at[layer], recv_sem.at[layer], back_send.at[layer], back_recv.at[layer],
+        )
+        for name in ("normed", "inverse"):
+            loads[name].wait()
+
+        def from_output(block, total):
+            rows = slab_of(block)
+            if last:
+                grad = trunk[rows, :]
+            else:
+                grad = cotangent[rows, :].astype(F32) * live_rows(lengths, block, SLAB)
+            scaled = normed[1, rows, :]
+            second = norm_back(grad, scaled, inverse[1, rows, :], rows_ref[4:5, :])
+            small = second.astype(BF16)
+            trunk[rows, :] = second
+            outer_grad[layer, rows, :] = small
+            return (
+                total[0] + jnp.sum(small.astype(F32), 0, keepdims=True),
+                total[1] + jnp.sum(grad * scaled, 0, keepdims=True),
+                total[2] + jnp.sum(grad, 0, keepdims=True),
+            )
+
+        sums[1], sums[4], sums[5] = lax.fori_loop(0, 256 // SLAB, from_output, (sums[1], sums[4], sums[5]))
+        loads["slope"].wait()
+        if not last:
+            loads["outer"].wait()
+
+        def hidden(tile, carry):
+            start = pl.multiple_of(tile * 512, 512)
+            columns = pl.ds(start, 512)
+            grad = straight(outer_grad[layer], columns_of(weights, OUTER + start, 512))
+            small = (grad * slope[:, columns].astype(F32)).astype(BF16)
+            inner_grad[layer, :, columns] = small
+            total_ref[0:1, columns] += jnp.sum(small.astype(F32), 0, keepdims=True)
+            return carry
+
+        lax.fori_loop(0, 4, hidden, 0)
+        if not last:
+            loads["inner"].wait()
+        for quarter in range(4):
+            joins[0].offer(quarter, across(inner_grad[layer], quarter_of(weights, quarter, INNER, 2048)))
+        joins[0].wait()
+
+        def from_middle(block, total):
+            rows = slab_of(block)
+            grad = trunk[rows, :] + joins[0].total(rows)
+            scaled = normed[0, rows, :]
+            first = norm_back(grad, scaled, inverse[0, rows, :], rows_ref[2:3, :])
+            small = first.astype(BF16)
+            trunk[rows, :] = first
+            attn_grad[layer, rows, :] = small
+            return (
+                total[0] + jnp.sum(small.astype(F32), 0, keepdims=True),
+                total[1] + jnp.sum(grad * scaled, 0, keepdims=True),
+                total[2] + jnp.sum(grad, 0, keepdims=True),
+            )
+
+        sums[0], sums[2], sums[3] = lax.fori_loop(0, 256 // SLAB, from_middle, (sums[0], sums[2], sums[3]))
+        if not last:
+            loads["out"].wait()
+        mixed_grad[layer] = straight(attn_grad[layer], columns_of(weights, OUT, 512)).astype(BF16)
+        heads.start()
+        if last:
+            weight_grad(weights, OUT, attn_grad[...].reshape(512, 1024), mixed, 512)
+            weight_grad(weights, INNER, middle[...].reshape(512, 1024), inner_grad, 2048)
+            two.first(0, 0)
+            weight_grad(weights, OUTER, outer_grad[...].reshape(512, 1024), act, 2048)
+            two.first(0, 1)
+            columns = jnp.concatenate(sums + [jnp.zeros((LANES - 6, 1024), F32)], 0).T
+            weights[:, :, :, :, :, EXTRA:WIDTH] = columns.astype(BF16).reshape(*SHARDS, 16, LANES)
+            two.first(0, 2)
+        else:
+            load("normed", normed_in.at[0], normed)
+            load("inverse", inverse_in.at[0], inverse)
+            load("slope", slope_in.at[0], slope)
+        for name in ("unit", "exact", "logs"):
+            loads[name].wait()
+        heads.attend(length, unit, exact, logs, grad_buf, query_sum)
+        if last:
+            for third in range(3):
+                two.onward(0, third)
+        else:
+            load("unit", unit_in.at[0], unit)
+            load("exact", exact_in.at[0], exact)
+            load("logs", logs_in.at[0], logs)
+            loads["qkv"].wait()
+        heads.collect(0)
+        heads.collect(1)
+        head_sum[1] = head_sum[1] + jnp.sum(grads[layer, 1].astype(F32), 0, keepdims=True)
+        early = [
+            across(grads[layer, 0], quarter_of(weights, quarter, KEY, 512))
+            + across(grads[layer, 1], quarter_of(weights, quarter, VALUE, 512))
+            for quarter in range(4)
+        ]
+        heads.collect(2)
+        head_sum[0] = head_sum[0] + jnp.sum(grads[layer, 2].astype(F32), 0, keepdims=True)
+        for quarter in range(4):
+            joins[1].offer(
+                quarter, early[quarter] + across(grads[layer, 2], quarter_of(weights, quarter, QUERY, 512))
+            )
+        if last:
+            left = low[...].reshape(512, 1024)
+            for start, j in ((KEY, 0), (VALUE, 1), (QUERY, 2)):
+                weight_grad(weights, start, left, grads.at[:, j], 512)
+            for third in range(3):
+                one.first(0, third)
+            total_ref[1:2, 0:512] = head_sum[0]
+            total_ref[1:2, 512:1024] = head_sum[1]
+            total_ref[2:8, 0:1024] = squares[0:6, :]
+            count = sum(jnp.clip(lengths[s] - c * ROWS, 0, ROWS) for s in range(2)).astype(F32)
+            total_ref[1:2, 1024:1152] = jnp.full((1, LANES), count, F32)
+        else:
+            for name in ("act", "mixed", "middle", "low1"):
+                loads[name].wait()
+        joins[1].wait()
+
+        def to_input(block, carry):
+            rows = slab_of(block)
+            grad = trunk[rows, :] + joins[1].total(rows)
+            if last:
+                stream_grad[rows, :] = grad
+            else:
+                trunk[rows, :] = grad
+            return carry
+
+        lax.fori_loop(0, 256 // SLAB, to_input, 0)
+        closing += [heads] + joins
+
+    totals = Totals(total_ref, total_land, total_send, total_recv)
+    thirds_all = range(3)
+    totals.first(0)
+    for third in thirds_all:
+        two.settle(0, third)
+        two.first(1, third)
+    for third in thirds_all:
+        one.onward(0, third)
+    totals.settle(0)
+    totals.first(1)
+    for third in thirds_all:
+        two.onward(1, third)
+    for third in thirds_all:
+        one.settle(0, third)
+        one.first(1, third)
+    for third in thirds_all:
+        two.settle(1, third)
+        two.first(2, third)
+    totals.settle(1)
+    totals.first(2)
+    for third in thirds_all:
+        one.onward(1, third)
+    for third in thirds_all:
+        two.onward(2, third)
+    for third in thirds_all:
+        one.settle(1, third)
+        one.first(2, third)
+    for third in thirds_all:
+        two.settle(2, third)
+    totals.settle(2)
+    for third in thirds_all:
+        one.onward(2, third)
+    for third in thirds_all:
+        one.settle(2, third)
+    x = at["x"]
+
+    def own(start, width):
+        return weights[x // 2, at["z"], x % 2, at["y"], :, start : start + width].astype(F32)
+
+    query_out[...] = own(QUERY, 512)
+    key_out[...] = own(KEY, 512)
+    value_out[...] = own(VALUE, 512)
+    output_out[...] = own(OUT, 512).T
+    inner_out[...] = own(INNER, 2048)
+    outer_out[...] = own(OUTER, 2048).T
+    vector_out[...] = own(EXTRA, LANES).T[0:8, :]
+    for item in closing:
+        item.close()
+    scale = 1.0 / (total_ref[1:2, 1024:1025] * 1024.0)
+    square = jnp.sum(total_ref[:, 0:1024], 1, keepdims=True)
+    root_ref[...] = jnp.broadcast_to(jnp.sqrt(square * scale + 1e-06), root_ref.shape)
+
+
+def run_backward(cotangent, low, rows, squares, lengths, saved):
+    dma = pltpu.SemaphoreType.DMA
+    out = lambda *shape: jax.ShapeDtypeStruct(shape, F32)
     return pl.pallas_call(
         backward_kernel,
         out_shape=(
-            jax.ShapeDtypeStruct((256, 1024), BF16),
-            jax.ShapeDtypeStruct((256, 2048), BF16),
-            jax.ShapeDtypeStruct((256, 1024), F32),
-            jax.ShapeDtypeStruct((256, 1024), BF16),
-            jax.ShapeDtypeStruct((256, 512), BF16),
-            jax.ShapeDtypeStruct((8, 1024), F32),
-            jax.ShapeDtypeStruct((1, 2048), F32),
+            out(256, 1024), out(16, 512), out(16, 512), out(16, 512), out(512, 16), out(16, 2048), out(2048, 16),
+            out(8, 16), out(8, 2048), out(8, LANES),
         ),
-        in_specs=[spec(pltpu.VMEM)] * 6 + [spec(pl.ANY), spec(pltpu.VMEM)],
-        out_specs=(spec(pltpu.VMEM),) * 7,
+        in_specs=[spec(pltpu.VMEM)] * 4 + [spec(pltpu.SMEM)] + [spec(pl.ANY)] * len(saved),
+        out_specs=(spec(pltpu.VMEM),) * 10,
         scratch_shapes=[
-            pltpu.VMEM((1024, 512), BF16),
-            pltpu.VMEM((1024, 2048), BF16),
-            pltpu.VMEM((1024, 2048), BF16),
+            pltpu.VMEM((*SHARDS, 16, WIDTH), BF16),
+            pltpu.VMEM((3, 1024, LANES), BF16),
+            pltpu.VMEM((1024, LANES), F32),
+            pltpu.VMEM((8, 256), F32),
+            pltpu.VMEM((2, 256, 512), BF16),
+            pltpu.VMEM((2, 256, 1024), F32),
+            pltpu.VMEM((2, 256, 1), F32),
+            pltpu.VMEM((2, 256, 1024), BF16),
+            pltpu.VMEM((2, 256, 2048), BF16),
+            pltpu.VMEM((256, 2048), BF16),
+            pltpu.VMEM((2, 256, 1024), BF16),
+            pltpu.VMEM((2, 256, 1024), BF16),
+            pltpu.VMEM((2, 256, 2048), BF16),
+            pltpu.VMEM((2, 256, 1024), BF16),
+            pltpu.VMEM((2, 3, 256, 512), BF16),
+            pltpu.VMEM((2, 256, 512), BF16),
             pltpu.VMEM((256, 1024), F32),
-            pltpu.VMEM((2, ROWS, 1024), BF16),
-            pltpu.VMEM((2, ROWS, 1024), BF16),
-            pltpu.SemaphoreType.DMA((3,)),
-            pltpu.SemaphoreType.DMA((2,)),
-            pltpu.SemaphoreType.DMA((2,)),
+            pltpu.VMEM((2, 1024, LANES), BF16),
+            pltpu.VMEM((2048, LANES), BF16),
+            pltpu.VMEM((2048, LANES), F32),
+            pltpu.VMEM((2, 2, 1024, LANES), BF16),
+            pltpu.VMEM((2, 1024, LANES), BF16),
+            pltpu.VMEM((2, 2, 2, 256, 512), BF16),
+            pltpu.VMEM((2, 2, 2, 256, 512), BF16),
+            pltpu.VMEM((3, 3, 8, 2048), F32),
+            dma((32,)),
+            dma((2, 4)),
+            dma((2, 7)),
+            dma((2, 7)),
+            dma((2, 3, 7)),
+            dma((2, 3, 7)),
+            dma((2, 2, 2)),
+            dma((2, 2, 2)),
+            dma((3, 3)),
+            dma((3, 3)),
+            dma((2, 3, 3, 6)),
+            dma((2, 3, 3, 6)),
+            *landing_shapes(0),
+            *landing_shapes(1),
         ],
         compiler_params=pltpu.CompilerParams(
-            collective_id=5, has_side_effects=True, vmem_limit_bytes=LIMIT
+            collective_id=4, has_side_effects=True, vmem_limit_bytes=LIMIT
         ),
-        name="backward",
-    )(grad, normed2, inverse2, slope, normed1, inverse1, gathered, vectors)
-
-
-def attend_back_kernel(
-    mixed_grad_ref, unit_ref, outcome_ref, logs_ref, first_ref, w_ref, lengths,
-    grads_ref, next_ref, sums_ref,
-    w_buf, taken, grad_buf, query_sum, key_value_buf, query_buf, sent, landed,
-    w_sem, local_sem, send_sem, recv_sem, back_send, back_recv, pair_send, pair_recv,
-):
-    f = lax.axis_index("fsdp")
-    c = lax.axis_index("context")
-    t = lax.axis_index("tensor")
-    partner = (f, c, 1 - t)
-    loads = []
-    for j, column in enumerate((512, 1024, 0)):
-        load = pltpu.make_async_copy(w_ref.at[:, pl.ds(column, 512)], w_buf.at[j], w_sem.at[j])
-        load.start()
-        loads.append(load)
-    greet([(f, lax.rem(c + d, 8), t) for d in range(1, 8)] + [partner])
-
-    def push(d):
-        peer = lax.rem(c + d, 8)
-        return remote(
-            part(mixed_grad_ref, peer), taken.at[rows_of(c)],
-            send_sem.at[d - 1], recv_sem.at[d - 1], (f, peer, t),
-        )
-
-    for d in range(1, 8):
-        push(d).start()
-    keep = pltpu.make_async_copy(part(mixed_grad_ref, c), taken.at[rows_of(c)], local_sem.at[0])
-    keep.start()
-    scale = jnp.asarray(0.125, BF16)
-    queries = jnp.concatenate(
-        [by_head(unit_ref[2, pl.ds(block * ROWS, ROWS), :] * scale) for block in range(8)], 0
-    )
-    logs = jnp.concatenate([logs_ref[block : block + 1, :] for block in range(8)], 1)
-    query_sum[...] = jnp.zeros_like(query_sum)
-    keep.wait()
-    for d in range(1, 8):
-        push(d).wait_recv()
-    for block in range(8):
-        grad_buf[pl.ds(block * 256, 256), :] = by_head(taken[pl.ds(block * ROWS, ROWS), :])
-    head_row = lax.broadcasted_iota(jnp.int32, (8, LANES), 0)
-    head_lane = lax.broadcasted_iota(jnp.int32, (8, LANES), 1) // HEAD
-    chosen = jnp.where(head_row == head_lane, 1.0, 0.0)
-    weighted = lax.dot_general(
-        chosen, taken[...].astype(F32) * outcome_ref[...],
-        (((1,), (1,)), ((), ())), precision=lax.Precision.HIGHEST, preferred_element_type=F32,
-    )
-    delta = jnp.concatenate(
-        [
-            weighted[head : head + 1, block * ROWS : (block + 1) * ROWS]
-            for block in range(8)
-            for head in range(2)
-        ],
-        1,
-    )
-    length = lengths[c // 4]
-
-    def answer(j, d):
-        peer = lax.rem(c + d, 8)
-        source = query_buf if j == 2 else key_value_buf.at[j]
-        return remote(
-            source.at[rows_of(peer)], part(grads_ref.at[j], c),
-            back_send.at[j, d - 1], back_recv.at[j, d - 1], (f, peer, t),
-        )
-
-    def step(turn, carry):
-        pair = lax.rem(c // 2 + turn, 4)
-        spot = pl.ds(pl.multiple_of(pair * 256, 256), 256)
-        keys = unit_ref[0, spot, :]
-        values = unit_ref[1, spot, :]
-        scores = across(keys, queries) + key_mask(length, pair * 256, 256)
-        soft = jnp.exp(scores - logs)
-        key_value_buf[1, spot, :] = straight(soft.astype(BF16), grad_buf[...]).astype(BF16)
-        soft_grad = across(values, grad_buf[...])
-        score_grad = (soft * (soft_grad - delta)).astype(BF16)
-        key_value_buf[0, spot, :] = straight(score_grad, queries).astype(BF16)
-        query_sum[...] += lax.dot_general(
-            score_grad, keys, (((0,), (0,)), ((), ())), preferred_element_type=F32
-        )
-
-        for side in range(2):
-            block = pair * 2 + side
-            d = lax.rem(block - c + 8, 8)
-
-            @pl.when(d > 0)
-            def _():
-                for j in range(2):
-                    answer(j, d).start()
-
-        return carry
-
-    lax.fori_loop(1, 5, step, 0)
-    first_lane = lax.broadcasted_iota(jnp.int32, (ROWS, LANES), 1) < HEAD
-    for block in range(8):
-        start = block * 256
-        total = jnp.where(
-            first_lane,
-            query_sum[pl.ds(start, ROWS), :],
-            query_sum[pl.ds(start + ROWS, ROWS), :],
-        )
-        query_buf[pl.ds(block * ROWS, ROWS), :] = (total * 0.125).astype(BF16)
-    for d in range(1, 8):
-        answer(2, d).start()
-    kept = []
-    for j in range(3):
-        source = query_buf if j == 2 else key_value_buf.at[j]
-        keep = pltpu.make_async_copy(source.at[rows_of(c)], part(grads_ref.at[j], c), local_sem.at[j])
-        keep.start()
-        kept.append(keep)
-    for j in range(3):
-        kept[j].wait()
-        loads[j].wait()
-    for j in range(2):
-        for d in range(1, 8):
-            answer(j, d).wait_recv()
-    sums_ref[...] = jnp.zeros_like(sums_ref)
-    sums_ref[1:2, :] = jnp.sum(grads_ref[1].astype(F32), 0, keepdims=True)
-    early = across(grads_ref[0], w_buf[0]) + across(grads_ref[1], w_buf[1])
-    for d in range(1, 8):
-        answer(2, d).wait_recv()
-    sums_ref[0:1, :] = jnp.sum(grads_ref[2].astype(F32), 0, keepdims=True)
-    sent[...] = (early + across(grads_ref[2], w_buf[2])).astype(BF16)
-    swap = remote(sent, landed, pair_send, pair_recv, partner)
-    swap.start()
-    swap.wait()
-    next_ref[...] = first_ref[...] + (sent[...].astype(F32) + landed[...].astype(F32))
-    for d in range(1, 8):
-        push(d).wait_send()
-        for j in range(3):
-            answer(j, d).wait_send()
-
-
-def attend_back(mixed_grad, unit, outcome, logs, first, gathered, lengths):
-    return pl.pallas_call(
-        attend_back_kernel,
-        out_shape=(
-            jax.ShapeDtypeStruct((3, 256, 512), BF16),
-            jax.ShapeDtypeStruct((256, 1024), F32),
-            jax.ShapeDtypeStruct((8, 512), F32),
-        ),
-        in_specs=[spec(pltpu.VMEM)] * 5 + [spec(pl.ANY), spec(pltpu.SMEM)],
-        out_specs=(spec(pltpu.VMEM),) * 3,
-        scratch_shapes=[
-            pltpu.VMEM((3, 1024, 512), BF16),
-            pltpu.VMEM((1024, LANES), BF16),
-            pltpu.VMEM((2048, LANES), BF16),
-            pltpu.VMEM((2048, LANES), F32),
-            pltpu.VMEM((2, 1024, LANES), BF16),
-            pltpu.VMEM((1024, LANES), BF16),
-            pltpu.VMEM((256, 1024), BF16),
-            pltpu.VMEM((256, 1024), BF16),
-            pltpu.SemaphoreType.DMA((3,)),
-            pltpu.SemaphoreType.DMA((3,)),
-            pltpu.SemaphoreType.DMA((7,)),
-            pltpu.SemaphoreType.DMA((7,)),
-            pltpu.SemaphoreType.DMA((3, 7)),
-            pltpu.SemaphoreType.DMA((3, 7)),
-            pltpu.SemaphoreType.DMA,
-            pltpu.SemaphoreType.DMA,
-        ],
-        compiler_params=pltpu.CompilerParams(
-            collective_id=6, has_side_effects=True, vmem_limit_bytes=LIMIT
-        ),
-        name="attend_back",
-    )(mixed_grad, unit, outcome, logs, first, gathered, lengths)
+        name="backward_layers",
+    )(cotangent, low, rows, squares, lengths, *saved)
 
 
 def body(
@@ -962,95 +1149,42 @@
 ):
     slot_count, seq_count, model_width = stream.shape
     row_count = slot_count * seq_count
-    position = lax.axis_index("context") * slot_count + jnp.arange(slot_count, dtype=jnp.int32)
-    row_live = (position[None, :] < lengths[:, None]).astype(F32).reshape(row_count, 1)
     vectors = jnp.pad(
         jnp.stack([output_bias, outer_bias, first_gain, first_shift, second_gain, second_shift]),
         ((0, LANES - 6), (0, 0)),
     )
     bias = jnp.concatenate([query_bias, value_bias, inner_bias]).astype(F32)[None]
     low = stream.transpose(1, 0, 2).reshape(row_count, model_width)
-    (
-        result, vectors, squares, gathered, unit, exact, logs, mixed, normed, inverse, middle, act, slope, low_next,
-    ) = run_forward(
+    result, rows, squares, *saved = run_forward(
         low, query_weight, key_weight, value_weight, output_weight, inner_weight, outer_weight, vectors, bias, lengths
     )
-    gathered = gathered.reshape(model_width, WIDTH)
-    stored = []
-    for repeat in range(LAYERS):
-        stored.append(
-            (
-                low_next if repeat else low, mixed[repeat], unit[repeat], exact[repeat], logs[repeat],
-                middle[repeat], act[repeat],
-                (normed[repeat, 0], inverse[repeat, 0], slope[repeat], normed[repeat, 1], inverse[repeat, 1]),
-            )
-        )
-    result = result.reshape(seq_count, slot_count, model_width).transpose(1, 0, 2)
-    grad = cotangent.transpose(1, 0, 2).reshape(row_count, model_width).astype(F32) * row_live
-    taken = []
-    for repeat in reversed(range(LAYERS)):
-        low, mixed, unit, outcome, logs, middle, act, saved = stored[repeat]
-        outer_grad, inner_grad, first, attn, mixed_grad, sums, bias = backward(
-            grad, saved, gathered, vectors
-        )
-        qkv, grad, head_sums = attend_back(mixed_grad, unit, outcome, logs, first, gathered, lengths)
-        taken.append((low, qkv, attn, mixed, middle, inner_grad, outer_grad, act, sums, bias, head_sums))
-
-    def twice(left, right):
-        return sum(
-            lax.dot_general(left(t), right(t), (((0,), (0,)), ((), ())), preferred_element_type=F32)
-            for t in taken
-        )
-
-    sums = taken[0][8] + taken[1][8]
-    bias = taken[0][9] + taken[1][9]
-    head_sums = taken[0][10] + taken[1][10]
-    grads = jnp.concatenate(
-        [
-            twice(lambda t: t[0], lambda t: t[1][2]),
-            twice(lambda t: t[0], lambda t: t[1][0]),
-            twice(lambda t: t[0], lambda t: t[1][1]),
-            twice(lambda t: t[2], lambda t: t[3]),
-            twice(lambda t: t[4], lambda t: t[5]),
-            twice(lambda t: t[6], lambda t: t[7]),
-            jnp.pad(sums[:6].T, ((0, 0), (0, LANES - 6))),
-        ],
-        1,
-    ).astype(BF16)
-    small = jnp.concatenate(
-        [
-            head_sums[0],
-            head_sums[1],
-            bias[0],
-            jnp.sum(squares[:6], 1),
-            jnp.sum(row_live)[None],
-            jnp.zeros((1024 - 7,), F32),
-        ]
-    ).reshape(32, LANES)
-    summed, total = scatter_all(grads.reshape(2, 4, 2, 4, 16, grads.shape[1]), small)
-    total = total.reshape(-1)
-    square_total, count_total = total[3072:3078].reshape(LAYERS, 3), total[3078]
-    root_values = jnp.sqrt(square_total / (count_total * model_width) + 1e-06)
-    stream_grad = grad.reshape(seq_count, slot_count, model_width).transpose(1, 0, 2)
+    grad = cotangent.transpose(1, 0, 2).reshape(row_count, model_width)
+    (
+        stream_grad, grad_query, grad_key, grad_value, grad_output, grad_inner, grad_outer, grad_vectors, totals, roots,
+    ) = run_backward(grad, low, rows, squares, lengths, saved)
+
+    def slots_first(matrix):
+        return matrix.reshape(seq_count, slot_count, model_width).transpose(1, 0, 2)
+
     return (
-        result,
-        stream_grad,
-        summed[:, 0:512],
-        total[0:512],
-        summed[:, 512:1024],
-        summed[:, 1024:1536],
-        total[512:1024],
-        summed[:, 1536:2048].T,
-        summed[:, 6144],
-        summed[:, 6146],
-        summed[:, 6147],
-        summed[:, 2048:4096],
-        total[1024:3072],
-        summed[:, 4096:6144].T,
-        summed[:, 6145],
-        summed[:, 6148],
-        summed[:, 6149],
-        root_values,
+        slots_first(result),
+        slots_first(stream_grad),
+        grad_query,
+        totals[1, 0:512],
+        grad_key,
+        grad_value,
+        totals[1, 512:1024],
+        grad_output,
+        grad_vectors[0],
+        grad_vectors[2],
+        grad_vectors[3],
+        grad_inner,
+        totals[0],
+        grad_outer,
+        grad_vectors[1],
+        grad_vectors[4],
+        grad_vectors[5],
+        roots[2:8, 0].reshape(LAYERS, 3),
     )
 
 

time: 331 us -> 268 us (0.81); the launches traced: 327 us -> 268 us
  Pallas kernels: 272 us -> 243 us
  local copies, waits for them, and re-layouts: 40.3 us -> 23.5 us
  matrix products: 9.03 us -> 0 us
  other arithmetic: 4.38 us -> 0.61 us
    pallas_call x5 -> x1, Pallas kernels: 152 us -> 123 us  [run_backward(): pl.pallas_call(backward_kernel, out_shape=(out(256, 1024), out(16, 512),...]
    squeeze x6 -> x1, local copies, waits for them, and re-layouts: 9.67 us -> 0.53 us  [body(): grad_vectors[5]]
    dot_general x12 -> x0, matrix products: 9.03 us -> none  [twice(): lax.dot_general(left(t), right(t), (((0,), (0,)), ((), ())), preferred_el...]
    unnamed x69 -> x26, local copies, waits for them, and re-layouts: 10.2 us -> 7.54 us
where the time goes in v1:
time: 268 us
  Pallas kernels  243 us (91%)
  local copies, waits for them, and re-layouts  23.5 us (9%)
    pallas_call x1, Pallas kernels, run_backward(): pl.pallas_call(backward_kernel, out_shape=(out(256, 1024), out(16, 512),...  123 us
    pallas_call x1, Pallas kernels, run_forward(): pl.pallas_call(forward_kernel, out_shape=(jax.ShapeDtypeStruct((256, 1024...  120 us
    unnamed x26, local copies, waits for them, and re-layouts  7.54 us
    reshape x2, local copies, waits for them, and re-layouts, slots_first(): return matrix.reshape(seq_count, slot_count, model_width).transpose(1, 0, 2)  5.48 us

profile of v1, /device:TPU:0, one launch (start us, length us, event | category | flops | bytes accessed | tf_op | source)
XLA Modules:
  0.0 267.8 jit_solution(7307402870958082151)
XLA Ops:
  0.7 0.0 copy-start.1
  0.7 0.7 concatenate.16
  1.4 0.7 concatenate.17
  2.1 0.8 stack.27
  2.8 0.7 concatenate.18
  3.5 0.6 maximum_convert_fusion.bias
  4.2 0.6 pad.4.vectors
  4.8 1.5 copy.45.output
  6.3 2.0 copy.44
  8.2 1.8 copy.46.outer
  10.0 0.0 copy-done.1
  10.1 1.0 copy.48
  11.0 119.8 %forward_layers.1 = (bf16[256,1024]{1,0:T(8,128)(2,1)}, f32[8,1024]{1,0:T(8,128)}, f32[8,1024]{1,0:T(8,128)}, bf16[2,4,2,4,16,6272]{5,4,3,2,1,0:T(8,128)(2,1)}, ...) custom-call(bf16[256,1024]{1,0:T(8,128)(2,1)} %bitcast.33, ...), custom_call_target="tpu_custom_call" | custom-call | tf_op jit(solution)/shard_map/forward_layers/pallas_call | solution.py:506
  130.8 2.4 copy.55
  133.2 123.1 %backward_layers.1 = (f32[256,1024]{1,0:T(8,128)}, f32[16,512]{1,0:T(8,128)}, f32[16,512]{1,0:T(8,128)}, f32[16,512]{1,0:T(8,128)}, f32[512,16]{1,0:T(8,128)}, /...) custom-call(bf16[256,1024]{1,0:T(8,128)(2,1)} %bitcast.35, ...), custom_call_target="tpu_custom_call" | custom-call | tf_op jit(solution)/shard_map/backward_layers/pallas_call | solution.py:1074
  256.3 0.0 copy-start.7
  256.3 0.0 copy-start.8
  256.3 0.0 copy-start.2
  256.4 0.0 copy-start
  256.4 0.0 copy-start.6
  256.4 0.0 copy-start.5
  256.4 0.0 copy-start.4
  256.4 0.0 copy-start.3
  256.4 3.1 %copy.54 = f32[2,128,1024]{2,0,1:T(2,128)} copy(f32[2,128,1024]{2,1,0:T(8,128)} %bitcast.37) | data formatting | bytes 2097152 | tf_op jit(solution)/shard_map/reshape | solution.py:1167
  259.5 0.0 copy-done.7
  259.5 0.1 slice_reduce_fusion
  259.6 0.6 reshape_squeeze.3
  260.3 0.0 copy-done.8
  260.3 0.5 slice_bitcast_fusion
  260.8 1.3 fusion
  262.1 1.4 slice.35
  263.6 0.0 copy-done.2
  263.6 0.7 copy.50
  264.3 0.0 copy-done
  264.3 1.0 copy.51
  265.3 0.0 copy-done.6
  265.3 0.6 copy.60
  265.9 0.0 copy-done.5
  265.9 0.6 copy.61
  266.5 0.0 copy-done.4
  266.5 0.6 copy.62
  267.1 0.0 copy-done.3
  267.1 0.7 copy.63
Async XLA Ops:
  0.7 9.4 %copy-start.1 = (bf16[128,2,1024]{2,1,0:T(2,128)(2,1)S(1)}, bf16[128,2,1024]{2,1,0:T(2,128)(2,1)}, u32[]{:S(2)}) copy-start(bf16[128,2,1024]{2,1,0:T(2,128)(2,1)} %param.35) | copy-start | bytes 1572868
  256.3 3.2 %copy-start.7 = (f32[8,128]{1,0:T(8,128)S(1)}, f32[8,128]{1,0:T(8,128)}, u32[]{:S(2)}) copy-start(f32[8,128]{1,0:T(8,128)} %get-tuple-element.65) | copy-start | bytes 12292
  256.3 3.9 %copy-start.8 = (f32[8,16]{1,0:T(8,128)S(1)}, f32[8,16]{1,0:T(8,128)}, u32[]{:S(2)}) copy-start(f32[8,16]{1,0:T(8,128)} %get-tuple-element.62) | copy-start | bytes 1540
  256.3 7.2 %copy-start.2 = (f32[512,16]{1,0:T(8,128)S(1)}, f32[512,16]{1,0:T(8,128)}, u32[]{:S(2)}) copy-start(f32[512,16]{1,0:T(8,128)} %get-tuple-element.91) | copy-start | bytes 98308
  256.4 7.9 %copy-start = (f32[2048,16]{1,0:T(8,128)S(1)}, f32[2048,16]{1,0:T(8,128)}, u32[]{:S(2)}) copy-start(f32[2048,16]{1,0:T(8,128)} %get-tuple-element.97) | copy-start | bytes 393220
  256.4 8.9 %copy-start.6 = (f32[16,512]{1,0:T(8,128)S(1)}, f32[16,512]{1,0:T(8,128)}, u32[]{:S(2)}) copy-start(f32[16,512]{1,0:T(8,128)} %get-tuple-element.130) | copy-start | bytes 98308
  256.4 9.5 %copy-start.5 = (f32[16,512]{1,0:T(8,128)S(1)}, f32[16,512]{1,0:T(8,128)}, u32[]{:S(2)}) copy-start(f32[16,512]{1,0:T(8,128)} %get-tuple-element.132) | copy-start | bytes 98308
  256.4 10.1 %copy-start.4 = (f32[16,512]{1,0:T(8,128)S(1)}, f32[16,512]{1,0:T(8,128)}, u32[]{:S(2)}) copy-start(f32[16,512]{1,0:T(8,128)} %get-tuple-element.133) | copy-start | bytes 98308
  256.4 10.7 %copy-start.3 = (f32[16,2048]{1,0:T(8,128)S(1)}, f32[16,2048]{1,0:T(8,128)}, u32[]{:S(2)}) copy-start(f32[16,2048]{1,0:T(8,128)} %get-tuple-element.139) | copy-start | bytes 393220

commit v2 on v1

--- a/solution.py
+++ b/solution.py
@@ -15,7 +15,7 @@
 ROWS = 128
 LIMIT = 60 * 2**20
 WIDTH = 6272
-QUERY, KEY, VALUE, OUT, INNER, OUTER, EXTRA = 0, 512, 1024, 1536, 2048, 4096, 6144
+QUERY, KEY, VALUE, OUT, EXTRA, INNER, OUTER = 0, 512, 1024, 1536, 2048, 2176, 4224
 GROUPS = ((QUERY, OUT), (OUT, WIDTH))
 ORDERS = ("zyx", "yxz", "xzy")
 SHARDS = (2, 4, 2, 4)
@@ -152,6 +152,17 @@
             both = (low[0], low[1] + high[1])
             self.send(third, phase, 0, self.at, both, 1)
             self.send(third, phase, 1, self.at, both, -1)
+
+    def direct(self, phase):
+        for third in range(3):
+            low, high = self.parts[third]
+            for step in (1, 2, 3):
+                self.send(third, phase, step - 1, self.at, (low[0], low[1] + high[1]), step)
+
+    def arrive(self, phase):
+        for third in range(3):
+            for kind in range(3):
+                self.sent[third, phase, kind].wait_recv()
 
     def onward(self, phase):
         for third in range(3):
@@ -217,7 +228,7 @@
                 self.push(j, d).start()
             self.keep(j).start()
 
-    def attend(self, length, exact, logs):
+    def attend(self, length, exact, logs, midway):
         c = self.c
         for j in range(2):
             self.keep(j).wait()
@@ -252,7 +263,9 @@
 
             return carry
 
-        lax.fori_loop(0, 8, step, 0)
+        lax.fori_loop(0, 4, step, 0)
+        midway()
+        lax.fori_loop(4, 8, step, 0)
         self.keep_back().start()
 
     def collect(self):
@@ -333,27 +346,36 @@
 
 def pack(weights, own, query, key, value, output, inner, outer, vectors):
     xh, z, xl, y = own
+
+    def put(start, block):
+        weights[xh, z, xl, y, :, start : start + block.shape[1]] = block
+
+    put(QUERY, query[...])
+    put(KEY, key[...])
+    put(VALUE, value[...])
+    put(OUT, output[...])
+    put(INNER, inner[...])
+    put(OUTER, outer[...])
     eye = jnp.where(
         lax.broadcasted_iota(jnp.int32, (16, 16), 0) == lax.broadcasted_iota(jnp.int32, (16, 16), 1), 1.0, 0.0
     ).astype(BF16)
-
-    def put(start, block):
-        weights[xh, z, xl, y, :, start : start + block.shape[1]] = block
-
-    put(QUERY, query[...])
-    put(KEY, key[...])
-    put(VALUE, value[...])
-    put(OUT, across(eye, output[...]).astype(BF16))
-    put(INNER, inner[...])
-    put(OUTER, across(eye, outer[...]).astype(BF16))
-    put(EXTRA, across(eye, vectors[...]).astype(BF16))
+    rows = [vector[...].astype(F32).reshape(1, 16) for vector in vectors]
+    table = jnp.concatenate(rows + [jnp.zeros((LANES - 6, 16), F32)], 0).astype(BF16)
+    put(EXTRA, across(eye, table).astype(BF16))
+
+
+def rows_by_sequence(source, target, keep):
+    whole = source[...].astype(F32)
+    for s in range(2):
+        target[s * ROWS : s * ROWS + ROWS, :] = (whole[:, s, :] * keep(s)).astype(target.dtype)
 
 
 def forward_kernel(
-    x_ref, query, key, value, output, inner, outer, vectors, bias, lengths,
-    result_ref, rows_ref, squares_ref, w_out, unit_out, exact_out, logs_out, mixed_out, normed_out, inverse_out,
+    stream, cotangent, query, key, value, output, inner, outer, bias0, bias1, gain1, shift1, gain2, shift2,
+    query_bias, value_bias, inner_bias, lengths,
+    x_ref, grad_ref, result_ref, rows_ref, squares_ref, w_out, unit_out, exact_out, logs_out, mixed_out, normed_out, inverse_out,
     middle_out, act_out, slope_out, low_out,
-    weights, own, unit, exact, logs, outcome, mixed, normed, inverse, middle, act, slope, low, current,
+    weights, bias, own, unit, exact, logs, outcome, mixed, normed, inverse, middle, act, slope, low, current,
     sent, landed,
     local_sem, save_sem, gather_send, gather_recv, send_sem, recv_sem, back_send, back_recv, pair_send, pair_recv,
 ):
@@ -362,25 +384,31 @@
     t = lax.axis_index("tensor")
     partner = (lax.axis_index("fsdp"), c, 1 - t)
     x = at["x"]
-    pack(weights, (x // 2, at["z"], x % 2, at["y"]), query, key, value, output, inner, outer, vectors)
-    greet(neighbours(at, (1, -1)) + context_peers() + [partner])
+    pack(
+        weights, (x // 2, at["z"], x % 2, at["y"]), query, key, value, output, inner, outer,
+        (bias0, bias1, gain1, shift1, gain2, shift2),
+    )
+    greet(neighbours(at, (1, 2, 3)) + context_peers() + [partner])
     one, two = (Gather(weights, group, gather_send, gather_recv) for group in range(2))
-    one.first(0)
-    two.first(0)
-    one.onward(0)
-    two.onward(0)
-    one.settle(0)
-    one.first(1)
-    two.settle(0)
+    one.direct(0)
+    two.direct(0)
+    rows_by_sequence(stream, x_ref, lambda s: 1.0)
+    one.arrive(0)
+    one.direct(1)
+    two.arrive(0)
     two.first(1)
-    one.onward(1)
+    bias[:, 0:512] = query_bias[...].astype(F32).reshape(1, 512)
+    bias[:, 512:1024] = value_bias[...].astype(F32).reshape(1, 512)
+    bias[:, 1024:3072] = inner_bias[...].astype(F32).reshape(1, 2048)
+    one.arrive(1)
+    one.first(2)
     two.onward(1)
-    one.settle(1)
-    one.first(2)
+    position = c * ROWS + lax.broadcasted_iota(jnp.int32, (ROWS, 1), 0)
+    rows_by_sequence(cotangent, grad_ref, lambda s: jnp.where(position < lengths[s], 1.0, 0.0))
+    current[...] = x_ref[...].astype(F32)
+    one.onward(2)
     two.settle(1)
-    one.onward(2)
     two.first(2)
-    current[...] = x_ref[...].astype(F32)
     one.settle(2)
     squares_ref[...] = jnp.zeros_like(squares_ref)
     length = lengths[c // 4]
@@ -403,9 +431,7 @@
             for stage in range(2)
         ]
         heads.project(x_ref[...] if first else low[...], weights, bias)
-        heads.attend(length, exact.at[layer], logs.at[layer])
-        if first:
-            two.onward(2)
+        heads.attend(length, exact.at[layer], logs.at[layer], (lambda: two.onward(2)) if first else (lambda: None))
         heads.collect()
         if first:
             two.settle(2)
@@ -488,7 +514,7 @@
         copy.wait()
 
 
-def run_forward(x, query, key, value, output, inner, outer, vectors, bias, lengths):
+def run_forward(*arguments):
     saved = (
         ((*SHARDS, 16, WIDTH), BF16),
         ((2, 3, 1024, LANES), BF16),
@@ -507,14 +533,17 @@
         forward_kernel,
         out_shape=(
             jax.ShapeDtypeStruct((256, 1024), BF16),
+            jax.ShapeDtypeStruct((256, 1024), BF16),
+            jax.ShapeDtypeStruct((256, 1024), BF16),
             jax.ShapeDtypeStruct((8, 1024), F32),
             jax.ShapeDtypeStruct((8, 1024), F32),
             *(jax.ShapeDtypeStruct(shape, kind) for shape, kind in saved),
         ),
-        in_specs=[spec(pltpu.VMEM)] * 9 + [spec(pltpu.SMEM)],
-        out_specs=(spec(pltpu.VMEM),) * 3 + (spec(pl.ANY),) * len(saved),
+        in_specs=[spec(pltpu.VMEM)] * 17 + [spec(pltpu.SMEM)],
+        out_specs=(spec(pltpu.VMEM),) * 5 + (spec(pl.ANY),) * len(saved),
         scratch_shapes=[
             pltpu.VMEM((*SHARDS, 16, WIDTH), BF16),
+            pltpu.VMEM((1, 3072), F32),
             pltpu.VMEM((2, 3, 256, 512), BF16),
             pltpu.VMEM((2, 3, 1024, LANES), BF16),
             pltpu.VMEM((2, 1024, LANES), F32),
@@ -545,7 +574,7 @@
             collective_id=3, has_side_effects=True, vmem_limit_bytes=LIMIT
         ),
         name="forward_layers",
-    )(x, query, key, value, output, inner, outer, vectors, bias, lengths)
+    )(*arguments)
 
 
 def norm_back(grad_out, normed, inverse, gain):
@@ -623,6 +652,17 @@
         self.send(third, phase, 2, 1, high, 1)
         self.send(third, phase, 3, -1, low, -1)
 
+    def direct(self, phase, third):
+        low, high = self.parts[third]
+        for step in (1, 2, 3):
+            self.send(third, phase, step - 1, step, (low[0], low[1] + high[1]), step)
+
+    def arrive(self, phase, third):
+        low, high = self.parts[third]
+        for kind in range(3):
+            self.sent[third, phase, kind].wait_recv()
+        self.add(third, phase, 0, (low[0], low[1] + high[1]), (0, 1, 2))
+
     def onward(self, phase, third):
         low, high = self.parts[third]
         self.sent[third, phase, 0].wait_recv()
@@ -646,6 +686,9 @@
             copy.wait_send()
 
 
+DIRECT = ((1, 2), (2,))
+
+
 def landing_shapes(group):
     shapes = []
     for third in range(3):
@@ -653,12 +696,14 @@
         low, high = thirds(group)[third]
         for phase in range(3):
             whole = order[phase + 1 :]
-            shape = [6]
+            direct = phase in DIRECT[group]
+            shape = [3 if direct else 6]
             shape += [2] if "x" in whole else []
             shape += [4] if "z" in whole else []
             shape += [2] if "x" in whole else []
             shape += [4] if "y" in whole else []
-            shapes.append(pltpu.VMEM((*shape, 16, max(low[1], high[1])), BF16))
+            width = low[1] + high[1] if direct else max(low[1], high[1])
+            shapes.append(pltpu.VMEM((*shape, 16, width), BF16))
     return shapes
 
 
@@ -824,11 +869,11 @@
 
 
 def backward_kernel(
-    cotangent, low0, rows_ref, squares, lengths,
-    w_in, unit_in, exact_in, logs_in, mixed_in, normed_in, inverse_in, middle_in, act_in, slope_in, low1_in,
-    stream_grad, query_out, key_out, value_out, output_out, inner_out, outer_out, vector_out, total_ref, root_ref,
+    cotangent, rows_ref, squares, lengths,
+    low0, result_in, w_in, unit_in, exact_in, logs_in, mixed_in, normed_in, inverse_in, middle_in, act_in, slope_in, low1_in,
+    stream_grad, result_ref, query_out, key_out, value_out, output_out, inner_out, outer_out, vector_out, total_ref, root_ref,
     weights, unit, exact, logs, mixed, normed, inverse, middle, act, slope, low,
-    attn_grad, inner_grad, outer_grad, grads, mixed_grad, trunk,
+    attn_grad, inner_grad, outer_grad, grads, mixed_grad, trunk, result,
     taken, grad_buf, query_sum, key_value, query_buf, sent, landed, total_land,
     load_sem, local_sem, send_sem, recv_sem, back_send, back_recv, pair_send, pair_recv,
     total_send, total_recv, scatter_send, scatter_recv, *landings,
@@ -863,7 +908,8 @@
     load("mixed", mixed_in, mixed)
     load("middle", middle_in, middle)
     load("low1", low1_in, low.at[1])
-    low[0] = low0[...]
+    load("result", result_in, result)
+    load("low0", low0, low.at[0])
     greet(neighbours(at, (1, 2, 3)) + context_peers() + [partner])
 
     three = [landings[9 * group : 9 * group + 9] for group in range(2)]
@@ -897,7 +943,7 @@
             if last:
                 grad = trunk[rows, :]
             else:
-                grad = cotangent[rows, :].astype(F32) * live_rows(lengths, block, SLAB)
+                grad = cotangent[rows, :].astype(F32)
             scaled = normed[1, rows, :]
             second = norm_back(grad, scaled, inverse[1, rows, :], rows_ref[4:5, :])
             small = second.astype(BF16)
@@ -928,6 +974,11 @@
             loads["inner"].wait()
         for quarter in range(4):
             joins[0].offer(quarter, across(inner_grad[layer], quarter_of(weights, quarter, INNER, 2048)))
+        if last:
+            weight_grad(weights, OUTER, outer_grad[...].reshape(512, 1024), act, 2048)
+            two.first(0, 2)
+            weight_grad(weights, INNER, middle[...].reshape(512, 1024), inner_grad, 2048)
+            two.first(0, 1)
         joins[0].wait()
 
         def from_middle(block, total):
@@ -951,13 +1002,9 @@
         heads.start()
         if last:
             weight_grad(weights, OUT, attn_grad[...].reshape(512, 1024), mixed, 512)
-            weight_grad(weights, INNER, middle[...].reshape(512, 1024), inner_grad, 2048)
+            columns = jnp.concatenate(sums + [jnp.zeros((LANES - 6, 1024), F32)], 0).T
+            weights[:, :, :, :, :, EXTRA : EXTRA + LANES] = columns.astype(BF16).reshape(*SHARDS, 16, LANES)
             two.first(0, 0)
-            weight_grad(weights, OUTER, outer_grad[...].reshape(512, 1024), act, 2048)
-            two.first(0, 1)
-            columns = jnp.concatenate(sums + [jnp.zeros((LANES - 6, 1024), F32)], 0).T
-            weights[:, :, :, :, :, EXTRA:WIDTH] = columns.astype(BF16).reshape(*SHARDS, 16, LANES)
-            two.first(0, 2)
         else:
             load("normed", normed_in.at[0], normed)
             load("inverse", inverse_in.at[0], inverse)
@@ -966,7 +1013,7 @@
             loads[name].wait()
         heads.attend(length, unit, exact, logs, grad_buf, query_sum)
         if last:
-            for third in range(3):
+            for third in (2, 1, 0):
                 two.onward(0, third)
         else:
             load("unit", unit_in.at[0], unit)
@@ -999,56 +1046,49 @@
             count = sum(jnp.clip(lengths[s] - c * ROWS, 0, ROWS) for s in range(2)).astype(F32)
             total_ref[1:2, 1024:1152] = jnp.full((1, LANES), count, F32)
         else:
-            for name in ("act", "mixed", "middle", "low1"):
+            for name in ("act", "mixed", "middle", "low0", "low1", "result"):
                 loads[name].wait()
         joins[1].wait()
 
         def to_input(block, carry):
             rows = slab_of(block)
-            grad = trunk[rows, :] + joins[1].total(rows)
-            if last:
-                stream_grad[rows, :] = grad
-            else:
-                trunk[rows, :] = grad
+            trunk[rows, :] += joins[1].total(rows)
             return carry
 
         lax.fori_loop(0, 256 // SLAB, to_input, 0)
         closing += [heads] + joins
 
     totals = Totals(total_ref, total_land, total_send, total_recv)
-    thirds_all = range(3)
     totals.first(0)
-    for third in thirds_all:
+    for third in (2, 1, 0):
         two.settle(0, third)
         two.first(1, third)
-    for third in thirds_all:
+    for s in range(2):
+        stream_grad[:, s, :] = trunk[s * ROWS : s * ROWS + ROWS, :]
+    for third in range(3):
         one.onward(0, third)
     totals.settle(0)
     totals.first(1)
-    for third in thirds_all:
+    for third in (2, 1, 0):
         two.onward(1, third)
-    for third in thirds_all:
+    pairs = [result[s * ROWS : s * ROWS + ROWS, :].astype(F32) for s in range(2)]
+    result_ref[...] = jnp.stack(pairs, 1).astype(BF16)
+    for third in range(3):
         one.settle(0, third)
-        one.first(1, third)
-    for third in thirds_all:
+        one.direct(1, third)
+    for third in (2, 1, 0):
         two.settle(1, third)
-        two.first(2, third)
+        two.direct(2, third)
     totals.settle(1)
     totals.first(2)
-    for third in thirds_all:
-        one.onward(1, third)
-    for third in thirds_all:
-        two.onward(2, third)
-    for third in thirds_all:
-        one.settle(1, third)
-        one.first(2, third)
-    for third in thirds_all:
-        two.settle(2, third)
+    for third in range(3):
+        one.arrive(1, third)
+        one.direct(2, third)
+    for third in (2, 1, 0):
+        two.arrive(2, third)
     totals.settle(2)
-    for third in thirds_all:
-        one.onward(2, third)
-    for third in thirds_all:
-        one.settle(2, third)
+    for third in range(3):
+        one.arrive(2, third)
     x = at["x"]
 
     def own(start, width):
@@ -1057,9 +1097,9 @@
     query_out[...] = own(QUERY, 512)
     key_out[...] = own(KEY, 512)
     value_out[...] = own(VALUE, 512)
-    output_out[...] = own(OUT, 512).T
+    output_out[...] = own(OUT, 512)
     inner_out[...] = own(INNER, 2048)
-    outer_out[...] = own(OUTER, 2048).T
+    outer_out[...] = own(OUTER, 2048)
     vector_out[...] = own(EXTRA, LANES).T[0:8, :]
     for item in closing:
         item.close()
@@ -1068,17 +1108,18 @@
     root_ref[...] = jnp.broadcast_to(jnp.sqrt(square * scale + 1e-06), root_ref.shape)
 
 
-def run_backward(cotangent, low, rows, squares, lengths, saved):
+def run_backward(grad, rows, squares, lengths, saved):
     dma = pltpu.SemaphoreType.DMA
     out = lambda *shape: jax.ShapeDtypeStruct(shape, F32)
     return pl.pallas_call(
         backward_kernel,
         out_shape=(
-            out(256, 1024), out(16, 512), out(16, 512), out(16, 512), out(512, 16), out(16, 2048), out(2048, 16),
+            out(ROWS, 2, 1024), jax.ShapeDtypeStruct((ROWS, 2, 1024), BF16),
+            out(16, 512), out(16, 512), out(16, 512), out(16, 512), out(16, 2048), out(16, 2048),
             out(8, 16), out(8, 2048), out(8, LANES),
         ),
-        in_specs=[spec(pltpu.VMEM)] * 4 + [spec(pltpu.SMEM)] + [spec(pl.ANY)] * len(saved),
-        out_specs=(spec(pltpu.VMEM),) * 10,
+        in_specs=[spec(pltpu.VMEM)] * 3 + [spec(pltpu.SMEM)] + [spec(pl.ANY)] * len(saved),
+        out_specs=(spec(pltpu.VMEM),) * 11,
         scratch_shapes=[
             pltpu.VMEM((*SHARDS, 16, WIDTH), BF16),
             pltpu.VMEM((3, 1024, LANES), BF16),
@@ -1097,6 +1138,7 @@
             pltpu.VMEM((2, 3, 256, 512), BF16),
             pltpu.VMEM((2, 256, 512), BF16),
             pltpu.VMEM((256, 1024), F32),
+            pltpu.VMEM((256, 1024), BF16),
             pltpu.VMEM((2, 1024, LANES), BF16),
             pltpu.VMEM((2048, LANES), BF16),
             pltpu.VMEM((2048, LANES), F32),
@@ -1124,7 +1166,45 @@
             collective_id=4, has_side_effects=True, vmem_limit_bytes=LIMIT
         ),
         name="backward_layers",
-    )(cotangent, low, rows, squares, lengths, *saved)
+    )(grad, rows, squares, lengths, *saved)
+
+
+def finish_kernel(
+    stream_in, result_in, query_in, key_in, value_in, output_in, inner_in, outer_in, vectors, totals, roots,
+    result, stream_grad, query, key, value, output, inner, outer, query_sum, value_sum, inner_sum, *rest,
+):
+    for source, target in (
+        (result_in, result), (stream_in, stream_grad), (query_in, query), (key_in, key), (value_in, value),
+        (output_in, output), (inner_in, inner), (outer_in, outer),
+    ):
+        target[...] = source[...]
+    query_sum[...] = totals[1:2, 0:512].reshape(512)
+    value_sum[...] = totals[1:2, 512:1024].reshape(512)
+    inner_sum[...] = totals[0:1, :].reshape(2048)
+    for j in range(6):
+        rest[j][...] = vectors[j : j + 1, :].reshape(16)
+    rest[6][...] = jnp.concatenate(
+        [
+            jnp.concatenate([roots[2 + 3 * layer + j : 3 + 3 * layer + j, 0:1] for j in range(3)], 1)
+            for layer in range(LAYERS)
+        ],
+        0,
+    )
+
+
+def finish(partial):
+    out = lambda *shape: jax.ShapeDtypeStruct(shape, F32)
+    return pl.pallas_call(
+        finish_kernel,
+        out_shape=(
+            jax.ShapeDtypeStruct((ROWS, 2, 1024), BF16), out(ROWS, 2, 1024),
+            out(16, 512), out(16, 512), out(16, 512), out(16, 512), out(16, 2048), out(16, 2048),
+            out(512), out(512), out(2048), *(out(16) for _ in range(6)), out(LAYERS, 3),
+        ),
+        in_specs=[spec(pltpu.VMEM)] * 11,
+        out_specs=(spec(pltpu.VMEM),) * 18,
+        name="finish",
+    )(*partial)
 
 
 def body(
@@ -1147,44 +1227,36 @@
     second_shift,
     cotangent,
 ):
-    slot_count, seq_count, model_width = stream.shape
-    row_count = slot_count * seq_count
-    vectors = jnp.pad(
-        jnp.stack([output_bias, outer_bias, first_gain, first_shift, second_gain, second_shift]),
-        ((0, LANES - 6), (0, 0)),
+    grad_in = cotangent
+    low, grad, result, rows, squares, *saved = run_forward(
+        stream, grad_in, query_weight, key_weight, value_weight, output_weight.T, inner_weight, outer_weight.T,
+        output_bias, outer_bias, first_gain, first_shift, second_gain, second_shift,
+        query_bias, value_bias, inner_bias, lengths,
     )
-    bias = jnp.concatenate([query_bias, value_bias, inner_bias]).astype(F32)[None]
-    low = stream.transpose(1, 0, 2).reshape(row_count, model_width)
-    result, rows, squares, *saved = run_forward(
-        low, query_weight, key_weight, value_weight, output_weight, inner_weight, outer_weight, vectors, bias, lengths
-    )
-    grad = cotangent.transpose(1, 0, 2).reshape(row_count, model_width)
+    partial = run_backward(grad, rows, squares, lengths, [low, result, *saved])
     (
-        stream_grad, grad_query, grad_key, grad_value, grad_output, grad_inner, grad_outer, grad_vectors, totals, roots,
-    ) = run_backward(grad, low, rows, squares, lengths, saved)
-
-    def slots_first(matrix):
-        return matrix.reshape(seq_count, slot_count, model_width).transpose(1, 0, 2)
-
+        result, stream_grad, grad_query, grad_key, grad_value, grad_output, grad_inner, grad_outer,
+        query_sum, value_sum, inner_sum, *vectors, roots,
+    ) = finish(partial)
     return (
-        slots_first(result),
-        slots_first(stream_grad),
+        result,
+        stream_grad,
         grad_query,
-        totals[1, 0:512],
+        query_sum,
         grad_key,
         grad_value,
-        totals[1, 512:1024],
-        grad_output,
-        grad_vectors[0],
-        grad_vectors[2],
-        grad_vectors[3],
+        value_sum,
+        grad_output.T,
+        vectors[0],
+        vectors[2],
+        vectors[3],
         grad_inner,
-        totals[0],
-        grad_outer,
-        grad_vectors[1],
-        grad_vectors[4],
-        grad_vectors[5],
-        roots[2:8, 0].reshape(LAYERS, 3),
+        inner_sum,
+        grad_outer.T,
+        vectors[1],
+        vectors[4],
+        vectors[5],
+        roots,
     )
 
 

time: 268 us -> 243 us (0.907)
  local copies, waits for them, and re-layouts: 23.5 us -> 0 us
    unnamed x26 -> x0, local copies, waits for them, and re-layouts: 7.54 us -> none
    reshape x2 -> x0, local copies, waits for them, and re-layouts: 5.48 us -> none  [slots_first(): return matrix.reshape(seq_count, slot_count, model_width).transpose(1, 0, 2)]
    pallas_call x1, Pallas kernels: 120 us -> 117 us  [run_forward(): pl.pallas_call(forward_kernel, out_shape=(jax.ShapeDtypeStruct((256, 1024...]
    transpose x2 -> x0, local copies, waits for them, and re-layouts: 2.91 us -> none  [the longest x1 1.95 us: body(): low = stream.transpose(1, 0, 2).reshape(row_count, model_width)]
    slice x3 -> x0, local copies, waits for them, and re-layouts: 2.88 us -> none  [the longest x1 1.44 us: body(): totals[0]]
    pallas_call x1 -> x2, Pallas kernels: 123 us -> 126 us  [the longest x1 123 us: run_backward(): pl.pallas_call(backward_kernel, out_shape=(out(ROWS, 2, 1024), jax.ShapeD...]
where the time goes in v2:
time: 243 us
  Pallas kernels  242 us (100%)
    pallas_call x1, Pallas kernels, run_backward(): pl.pallas_call(backward_kernel, out_shape=(out(ROWS, 2, 1024), jax.ShapeD...  123 us
    pallas_call x1, Pallas kernels, run_forward(): pl.pallas_call(forward_kernel, out_shape=(jax.ShapeDtypeStruct((256, 1024...  117 us

profile of v2, /device:TPU:0, one launch (start us, length us, event | category | flops | bytes accessed | tf_op | source)
XLA Modules:
  0.0 243.3 jit_solution(8483202988389257536)
XLA Ops:
  0.7 116.8 %forward_layers.1 = (bf16[256,1024]{1,0:T(8,128)(2,1)}, bf16[256,1024]{1,0:T(8,128)(2,1)}, bf16[256,1024]{1,0:T(8,128)(2,1)}, f32[8,1024]{1,0:T(8,128)}, f32[8,1...) custom-call(bf16[128,2,1024]{2,1,0:T(2,128)(2,1)} %stream.1, ...), custom_call_target="tpu_custom_call" | custom-call | tf_op jit(solution)/shard_map/forward_layers/pallas_call | solution.py:532
  117.5 122.7 %backward_layers.1 = (f32[128,2,1024]{2,1,0:T(2,128)}, bf16[128,2,1024]{2,1,0:T(2,128)(2,1)}, f32[16,512]{1,0:T(8,128)}, f32[16,512]{1,0:T(8,128)}, f32[16,512]{...) custom-call(bf16[256,1024]{1,0:T(8,128)(2,1)} %get-tuple-element.63., ...), custom_call_target="tpu_custom_call" | custom-call | tf_op jit(solution)/shard_map/backward_layers/pallas_call | solution.py:1114
  240.2 2.9 %finish.1 = (bf16[128,2,1024]{2,1,0:T(2,128)(2,1)}, f32[128,2,1024]{2,1,0:T(2,128)}, f32[16,512]{1,0:T(8,128)}, f32[16,512]{1,0:T(8,128)}, f32[16,512]{1,0:T(8,1...) custom-call(f32[128,2,1024]{2,1,0:T(2,128)} %get-tuple-element.79.st, ...), custom_call_target="tpu_custom_call" | custom-call | tf_op jit(solution)/shard_map/finish/pallas_call | solution.py:1197

commit v3 on v2

--- a/solution.py
+++ b/solution.py
@@ -16,7 +16,8 @@
 LIMIT = 60 * 2**20
 WIDTH = 6272
 QUERY, KEY, VALUE, OUT, EXTRA, INNER, OUTER = 0, 512, 1024, 1536, 2048, 2176, 4224
-GROUPS = ((QUERY, OUT), (OUT, WIDTH))
+GROUPS = ((QUERY, OUT), (OUT, OUTER), (OUTER, WIDTH))
+TILES = (((2, 2), (2, 2), (2, 2)), ((3, 3), (4, 5), (3, 3)), ((2, 3), (3, 3), (2, 3)))
 ORDERS = ("zyx", "yxz", "xzy")
 SHARDS = (2, 4, 2, 4)
 
@@ -82,13 +83,15 @@
 
 
 def thirds(group):
-    start, end = GROUPS[group]
-    tiles = (end - start) // LANES
-    cuts = [start + tiles * i // 6 * LANES for i in range(7)]
-    return [
-        ((cuts[2 * i], cuts[2 * i + 1] - cuts[2 * i]), (cuts[2 * i + 1], cuts[2 * i + 2] - cuts[2 * i + 1]))
-        for i in range(3)
-    ]
+    start = GROUPS[group][0]
+    parts = []
+    for pair in TILES[group]:
+        halves = []
+        for tiles in pair:
+            halves.append((start, tiles * LANES))
+            start += tiles * LANES
+        parts.append(tuple(halves))
+    return parts
 
 
 def across(left, right):
@@ -280,11 +283,13 @@
                 self.push(j, d).wait_send()
 
 
-class Joins:
-    def __init__(self, sent, landed, send_sem, recv_sem):
+class Join:
+    def __init__(self, number, before, sent, landed, send_sem, recv_sem):
         t = lax.axis_index("tensor")
         self.partner = (lax.axis_index("fsdp"), lax.axis_index("context"), 1 - t)
-        self.sent, self.landed, self.send_sem, self.recv_sem = sent, landed, send_sem, recv_sem
+        self.sent, self.landed = sent.at[number % 2], landed.at[number % 2]
+        self.send_sem, self.recv_sem = send_sem.at[number], recv_sem.at[number]
+        self.before = before
 
     def copy(self, half):
         return remote(
@@ -294,6 +299,8 @@
 
     def offer(self, quarter, term):
         half, side = quarter // 2, quarter % 2
+        if side == 0 and self.before is not None:
+            self.before.copy(half).wait_send()
         self.sent[half, :, side * 256 : side * 256 + 256] = term.astype(BF16)
         if side == 1:
             self.copy(half).start()
@@ -368,213 +375,6 @@
     whole = source[...].astype(F32)
     for s in range(2):
         target[s * ROWS : s * ROWS + ROWS, :] = (whole[:, s, :] * keep(s)).astype(target.dtype)
-
-
-def forward_kernel(
-    stream, cotangent, query, key, value, output, inner, outer, bias0, bias1, gain1, shift1, gain2, shift2,
-    query_bias, value_bias, inner_bias, lengths,
-    x_ref, grad_ref, result_ref, rows_ref, squares_ref, w_out, unit_out, exact_out, logs_out, mixed_out, normed_out, inverse_out,
-    middle_out, act_out, slope_out, low_out,
-    weights, bias, own, unit, exact, logs, outcome, mixed, normed, inverse, middle, act, slope, low, current,
-    sent, landed,
-    local_sem, save_sem, gather_send, gather_recv, send_sem, recv_sem, back_send, back_recv, pair_send, pair_recv,
-):
-    at = place()
-    c = lax.axis_index("context")
-    t = lax.axis_index("tensor")
-    partner = (lax.axis_index("fsdp"), c, 1 - t)
-    x = at["x"]
-    pack(
-        weights, (x // 2, at["z"], x % 2, at["y"]), query, key, value, output, inner, outer,
-        (bias0, bias1, gain1, shift1, gain2, shift2),
-    )
-    greet(neighbours(at, (1, 2, 3)) + context_peers() + [partner])
-    one, two = (Gather(weights, group, gather_send, gather_recv) for group in range(2))
-    one.direct(0)
-    two.direct(0)
-    rows_by_sequence(stream, x_ref, lambda s: 1.0)
-    one.arrive(0)
-    one.direct(1)
-    two.arrive(0)
-    two.first(1)
-    bias[:, 0:512] = query_bias[...].astype(F32).reshape(1, 512)
-    bias[:, 512:1024] = value_bias[...].astype(F32).reshape(1, 512)
-    bias[:, 1024:3072] = inner_bias[...].astype(F32).reshape(1, 2048)
-    one.arrive(1)
-    one.first(2)
-    two.onward(1)
-    position = c * ROWS + lax.broadcasted_iota(jnp.int32, (ROWS, 1), 0)
-    rows_by_sequence(cotangent, grad_ref, lambda s: jnp.where(position < lengths[s], 1.0, 0.0))
-    current[...] = x_ref[...].astype(F32)
-    one.onward(2)
-    two.settle(1)
-    two.first(2)
-    one.settle(2)
-    squares_ref[...] = jnp.zeros_like(squares_ref)
-    length = lengths[c // 4]
-    saves = []
-
-    def save(source, target):
-        copy = pltpu.make_async_copy(source, target, save_sem.at[len(saves)])
-        copy.start()
-        saves.append(copy)
-
-    closing = [one, two]
-    for layer in range(LAYERS):
-        first = layer == 0
-        heads = Heads(
-            own.at[layer], unit.at[layer], outcome.at[layer], mixed.at[layer], local_sem.at[layer],
-            send_sem.at[layer], recv_sem.at[layer], back_send.at[layer], back_recv.at[layer],
-        )
-        joins = [
-            Joins(sent.at[layer, stage], landed.at[layer, stage], pair_send.at[layer, stage], pair_recv.at[layer, stage])
-            for stage in range(2)
-        ]
-        heads.project(x_ref[...] if first else low[...], weights, bias)
-        heads.attend(length, exact.at[layer], logs.at[layer], (lambda: two.onward(2)) if first else (lambda: None))
-        heads.collect()
-        if first:
-            two.settle(2)
-            save(weights, w_out)
-            pick = jnp.where(
-                lax.broadcasted_iota(jnp.int32, (8, LANES), 0) == lax.broadcasted_iota(jnp.int32, (8, LANES), 1),
-                1.0, 0.0,
-            ).astype(BF16)
-            rows_ref[...] = across(pick, columns_of(weights, EXTRA, LANES))
-        for quarter in range(4):
-            joins[0].offer(quarter, across(mixed[layer], quarter_of(weights, quarter, OUT, 512)))
-        save(unit.at[layer], unit_out.at[layer])
-        save(exact.at[layer], exact_out.at[layer])
-        save(logs.at[layer], logs_out.at[layer])
-        save(mixed.at[layer], mixed_out.at[layer])
-        joins[0].wait()
-
-        def after_attention(block, total):
-            rows = slab_of(block)
-            live = live_rows(lengths, block, SLAB)
-            before = current[rows, :]
-            branch = joins[0].total(rows) + rows_ref[0:1, :]
-            scaled, root = norm_parts(before + branch)
-            after = scaled * rows_ref[2:3, :] + rows_ref[3:4, :]
-            normed[layer, 0, rows, :] = scaled
-            inverse[layer, 0, rows, :] = root
-            current[rows, :] = after
-            middle[layer, rows, :] = after.astype(BF16)
-            return (
-                total[0] + jnp.sum(live * before * before, 0, keepdims=True),
-                total[1] + jnp.sum(live * branch * branch, 0, keepdims=True),
-            )
-
-        zero = jnp.zeros((1, 1024), F32)
-        total = lax.fori_loop(0, 256 // SLAB, after_attention, (zero, zero))
-        squares_ref[3 * layer : 3 * layer + 1, :] = total[0]
-        squares_ref[3 * layer + 1 : 3 * layer + 2, :] = total[1]
-        save(middle.at[layer], middle_out.at[layer])
-
-        def hidden(tile, carry):
-            start = pl.multiple_of(tile * 512, 512)
-            columns = pl.ds(start, 512)
-            pre = straight(middle[layer], columns_of(weights, INNER + start, 512)) + bias[:, pl.ds(1024 + start, 512)]
-            act_part, slope_part = gelu_parts(pre)
-            act[layer, :, columns] = act_part.astype(BF16)
-            slope[layer, :, columns] = slope_part.astype(BF16)
-            return carry
-
-        lax.fori_loop(0, 4, hidden, 0)
-        for quarter in range(4):
-            joins[1].offer(quarter, across(act[layer], quarter_of(weights, quarter, OUTER, 2048)))
-        save(act.at[layer], act_out.at[layer])
-        save(slope.at[layer], slope_out.at[layer])
-        joins[1].wait()
-
-        def after_hidden(block, total):
-            rows = slab_of(block)
-            live = live_rows(lengths, block, SLAB)
-            branch = joins[1].total(rows) + rows_ref[1:2, :]
-            scaled, root = norm_parts(current[rows, :] + branch)
-            after = scaled * rows_ref[4:5, :] + rows_ref[5:6, :]
-            normed[layer, 1, rows, :] = scaled
-            inverse[layer, 1, rows, :] = root
-            current[rows, :] = after
-            if first:
-                low[rows, :] = after.astype(BF16)
-            else:
-                result_ref[rows, :] = (after * live).astype(BF16)
-            return total + jnp.sum(live * branch * branch, 0, keepdims=True)
-
-        squares_ref[3 * layer + 2 : 3 * layer + 3, :] = lax.fori_loop(0, 256 // SLAB, after_hidden, zero)
-        save(normed.at[layer], normed_out.at[layer])
-        save(inverse.at[layer], inverse_out.at[layer])
-        if first:
-            save(low, low_out)
-        closing += [heads] + joins
-    for item in closing:
-        item.close()
-    for copy in saves:
-        copy.wait()
-
-
-def run_forward(*arguments):
-    saved = (
-        ((*SHARDS, 16, WIDTH), BF16),
-        ((2, 3, 1024, LANES), BF16),
-        ((2, 1024, LANES), F32),
-        ((2, 8, 256), F32),
-        ((2, 256, 512), BF16),
-        ((2, 2, 256, 1024), F32),
-        ((2, 2, 256, 1), F32),
-        ((2, 256, 1024), BF16),
-        ((2, 256, 2048), BF16),
-        ((2, 256, 2048), BF16),
-        ((256, 1024), BF16),
-    )
-    dma = pltpu.SemaphoreType.DMA
-    return pl.pallas_call(
-        forward_kernel,
-        out_shape=(
-            jax.ShapeDtypeStruct((256, 1024), BF16),
-            jax.ShapeDtypeStruct((256, 1024), BF16),
-            jax.ShapeDtypeStruct((256, 1024), BF16),
-            jax.ShapeDtypeStruct((8, 1024), F32),
-            jax.ShapeDtypeStruct((8, 1024), F32),
-            *(jax.ShapeDtypeStruct(shape, kind) for shape, kind in saved),
-        ),
-        in_specs=[spec(pltpu.VMEM)] * 17 + [spec(pltpu.SMEM)],
-        out_specs=(spec(pltpu.VMEM),) * 5 + (spec(pl.ANY),) * len(saved),
-        scratch_shapes=[
-            pltpu.VMEM((*SHARDS, 16, WIDTH), BF16),
-            pltpu.VMEM((1, 3072), F32),
-            pltpu.VMEM((2, 3, 256, 512), BF16),
-            pltpu.VMEM((2, 3, 1024, LANES), BF16),
-            pltpu.VMEM((2, 1024, LANES), F32),
-            pltpu.VMEM((2, 8, 256), F32),
-            pltpu.VMEM((2, 1024, LANES), BF16),
-            pltpu.VMEM((2, 256, 512), BF16),
-            pltpu.VMEM((2, 2, 256, 1024), F32),
-            pltpu.VMEM((2, 2, 256, 1), F32),
-            pltpu.VMEM((2, 256, 1024), BF16),
-            pltpu.VMEM((2, 256, 2048), BF16),
-            pltpu.VMEM((2, 256, 2048), BF16),
-            pltpu.VMEM((256, 1024), BF16),
-            pltpu.VMEM((256, 1024), F32),
-            pltpu.VMEM((2, 2, 2, 256, 512), BF16),
-            pltpu.VMEM((2, 2, 2, 256, 512), BF16),
-            dma((2, 4)),
-            dma((24,)),
-            dma((2, 3, 3, 4)),
-            dma((2, 3, 3, 4)),
-            dma((2, 3, 7)),
-            dma((2, 3, 7)),
-            dma((2, 7)),
-            dma((2, 7)),
-            dma((2, 2, 2)),
-            dma((2, 2, 2)),
-        ],
-        compiler_params=pltpu.CompilerParams(
-            collective_id=3, has_side_effects=True, vmem_limit_bytes=LIMIT
-        ),
-        name="forward_layers",
-    )(*arguments)
 
 
 def norm_back(grad_out, normed, inverse, gain):
@@ -686,7 +486,7 @@
             copy.wait_send()
 
 
-DIRECT = ((1, 2), (2,))
+DIRECT = ((1, 2), (2,), (2,))
 
 
 def landing_shapes(group):
@@ -768,7 +568,7 @@
             self.push(d).start()
         self.keep().start()
 
-    def attend(self, length, unit, exact, logs_ref, grad_buf, query_sum):
+    def attend(self, length, unit, exact, logs_ref, grad_buf, query_sum, ahead, midway):
         c = self.c
         scale = jnp.asarray(0.125, BF16)
         queries = jnp.concatenate(
@@ -776,6 +576,7 @@
         )
         logs = jnp.concatenate([logs_ref[block : block + 1, :] for block in range(8)], 1)
         query_sum[...] = jnp.zeros_like(query_sum)
+        ahead()
         self.keep().wait()
         for d in range(1, 8):
             self.push(d).wait_recv()
@@ -822,7 +623,9 @@
 
             return carry
 
-        lax.fori_loop(1, 5, step, 0)
+        lax.fori_loop(1, 3, step, 0)
+        midway()
+        lax.fori_loop(3, 5, step, 0)
         first_lane = lax.broadcasted_iota(jnp.int32, (ROWS, LANES), 1) < HEAD
         for block in range(8):
             start = block * 256
@@ -868,84 +671,151 @@
     lax.fori_loop(0, width // tile, turn, 0)
 
 
-def backward_kernel(
-    cotangent, rows_ref, squares, lengths,
-    low0, result_in, w_in, unit_in, exact_in, logs_in, mixed_in, normed_in, inverse_in, middle_in, act_in, slope_in, low1_in,
-    stream_grad, result_ref, query_out, key_out, value_out, output_out, inner_out, outer_out, vector_out, total_ref, root_ref,
-    weights, unit, exact, logs, mixed, normed, inverse, middle, act, slope, low,
-    attn_grad, inner_grad, outer_grad, grads, mixed_grad, trunk, result,
-    taken, grad_buf, query_sum, key_value, query_buf, sent, landed, total_land,
-    load_sem, local_sem, send_sem, recv_sem, back_send, back_recv, pair_send, pair_recv,
-    total_send, total_recv, scatter_send, scatter_recv, *landings,
+def layers_kernel(
+    stream, cotangent, query, key, value, output, inner, outer, bias0, bias1, gain1, shift1, gain2, shift2,
+    query_bias, value_bias, inner_bias, lengths,
+    stream_grad, result_ref, query_out, key_out, value_out, output_out, inner_out, outer_out, vector_out, total_ref,
+    root_ref,
+    weights, bias, rows_ref, low, grad_in, result, trunk,
+    own, unit, exact, logs, outcome, mixed, normed, inverse, middle, act, slope,
+    attn_grad, inner_grad, outer_grad, grads, mixed_grad, taken, grad_buf, query_sum, key_value, query_buf,
+    sent, landed, total_land,
+    local_sem, gather_send, gather_recv, send_sem, recv_sem, back_send, back_recv, pair_send, pair_recv,
+    turn_local, turn_send, turn_recv, turn_back_send, turn_back_recv, total_send, total_recv,
+    scatter_send, scatter_recv, *landings,
 ):
     at = place()
     c = lax.axis_index("context")
     t = lax.axis_index("tensor")
     partner = (lax.axis_index("fsdp"), c, 1 - t)
-    loads, started = {}, []
-
-    def load(name, source, target):
-        copy = pltpu.make_async_copy(source, target, load_sem.at[len(started)])
-        copy.start()
-        started.append(copy)
-        loads[name] = copy
-
-    def load_weights(name, start, width):
-        columns = (slice(None),) * 5 + (pl.ds(start, width),)
-        load(name, w_in.at[columns], weights.at[columns])
-
-    load("normed", normed_in.at[1], normed)
-    load("inverse", inverse_in.at[1], inverse)
-    load_weights("outer", OUTER, 2048)
-    load("slope", slope_in.at[1], slope)
-    load_weights("inner", INNER, 2048)
-    load_weights("out", OUT, 512)
-    load("unit", unit_in.at[1], unit)
-    load("exact", exact_in.at[1], exact)
-    load("logs", logs_in.at[1], logs)
-    load_weights("qkv", QUERY, 1536)
-    load("act", act_in, act)
-    load("mixed", mixed_in, mixed)
-    load("middle", middle_in, middle)
-    load("low1", low1_in, low.at[1])
-    load("result", result_in, result)
-    load("low0", low0, low.at[0])
+    x = at["x"]
+    closing = []
+    joined = []
+
+    def new_join():
+        before = joined[-2] if len(joined) > 1 else None
+        joined.append(Join(len(joined), before, sent, landed, pair_send, pair_recv))
+        return joined[-1]
+
+    pack(
+        weights, (x // 2, at["z"], x % 2, at["y"]), query, key, value, output, inner, outer,
+        (bias0, bias1, gain1, shift1, gain2, shift2),
+    )
     greet(neighbours(at, (1, 2, 3)) + context_peers() + [partner])
-
-    three = [landings[9 * group : 9 * group + 9] for group in range(2)]
-    one, two = (
-        Scatter(weights, group, [three[group][3 * i : 3 * i + 3] for i in range(3)], scatter_send, scatter_recv)
-        for group in range(2)
-    )
+    one, two, three = (Gather(weights, group, gather_send, gather_recv) for group in range(3))
+    gathers = (one, two, three)
+    for group in gathers:
+        group.direct(0)
+    rows_by_sequence(stream, low.at[0], lambda s: 1.0)
+    one.arrive(0)
+    one.direct(1)
+    two.arrive(0)
+    two.first(1)
+    three.arrive(0)
+    three.first(1)
+    bias[:, 0:512] = query_bias[...].astype(F32).reshape(1, 512)
+    bias[:, 512:1024] = value_bias[...].astype(F32).reshape(1, 512)
+    bias[:, 1024:3072] = inner_bias[...].astype(F32).reshape(1, 2048)
+    one.arrive(1)
+    one.first(2)
+    two.onward(1)
+    three.onward(1)
+    position = c * ROWS + lax.broadcasted_iota(jnp.int32, (ROWS, 1), 0)
+    rows_by_sequence(cotangent, grad_in, lambda s: jnp.where(position < lengths[s], 1.0, 0.0))
+    trunk[...] = low[0].astype(F32)
+    total_ref[...] = jnp.zeros_like(total_ref)
+    one.onward(2)
+    two.settle(1)
+    two.first(2)
+    one.settle(2)
+    length = lengths[c // 4]
     zero = jnp.zeros((1, 1024), F32)
     sums = [zero] * 6
-    bias_sum = jnp.zeros((1, 2048), F32)
-    head_sum = [jnp.zeros((1, 512), F32)] * 2
-    length = lengths[c // 4]
-    closing = [one, two]
-    total_ref[...] = jnp.zeros_like(total_ref)
-
-    for layer in (1, 0):
-        last = layer == 0
-        joins = [
-            Joins(sent.at[layer, stage], landed.at[layer, stage], pair_send.at[layer, stage], pair_recv.at[layer, stage])
-            for stage in range(2)
-        ]
-        heads = HeadsBack(
-            mixed_grad.at[layer], taken.at[layer], key_value.at[layer], query_buf.at[layer], grads.at[layer],
-            local_sem.at[layer], send_sem.at[layer], recv_sem.at[layer], back_send.at[layer], back_recv.at[layer],
-        )
-        for name in ("normed", "inverse"):
-            loads[name].wait()
-
-        def from_output(block, total):
+
+    for layer in range(LAYERS):
+        first = layer == 0
+        heads = Heads(
+            own, unit.at[layer], outcome.at[layer], mixed.at[layer], local_sem.at[layer],
+            send_sem.at[layer], recv_sem.at[layer], back_send.at[layer], back_recv.at[layer],
+        )
+        if not first:
+            closing.pop().close()
+        closing.append(heads)
+        heads.project(low[layer], weights, bias)
+        if first:
+            three.settle(1)
+            three.first(2)
+            two.onward(2)
+        heads.attend(length, exact.at[layer], logs.at[layer], (lambda: three.onward(2)) if first else (lambda: None))
+        heads.collect()
+        if first:
+            two.settle(2)
+            pick = jnp.where(
+                lax.broadcasted_iota(jnp.int32, (8, LANES), 0) == lax.broadcasted_iota(jnp.int32, (8, LANES), 1),
+                1.0, 0.0,
+            ).astype(BF16)
+            rows_ref[...] = across(pick, columns_of(weights, EXTRA, LANES))
+        join = new_join()
+        for quarter in range(4):
+            join.offer(quarter, across(mixed[layer], quarter_of(weights, quarter, OUT, 512)))
+        join.wait()
+
+        def after_attention(block, total):
             rows = slab_of(block)
-            if last:
-                grad = trunk[rows, :]
-            else:
-                grad = cotangent[rows, :].astype(F32)
-            scaled = normed[1, rows, :]
-            second = norm_back(grad, scaled, inverse[1, rows, :], rows_ref[4:5, :])
+            live = live_rows(lengths, block, SLAB)
+            before = trunk[rows, :]
+            branch = join.total(rows) + rows_ref[0:1, :]
+            scaled, root = norm_parts(before + branch)
+            after = scaled * rows_ref[2:3, :] + rows_ref[3:4, :]
+            normed[2 * layer, rows, :] = scaled
+            inverse[2 * layer, rows, :] = root
+            trunk[rows, :] = after
+            middle[layer, rows, :] = after.astype(BF16)
+            return (
+                total[0] + jnp.sum(live * before * before, 0, keepdims=True),
+                total[1] + jnp.sum(live * branch * branch, 0, keepdims=True),
+            )
+
+        squares = lax.fori_loop(0, 256 // SLAB, after_attention, (zero, zero))
+        total_ref[2 + 3 * layer : 3 + 3 * layer, 0:1024] = squares[0]
+        total_ref[3 + 3 * layer : 4 + 3 * layer, 0:1024] = squares[1]
+
+        def hidden(tile, carry):
+            start = pl.multiple_of(tile * 512, 512)
+            columns = pl.ds(start, 512)
+            pre = straight(middle[layer], columns_of(weights, INNER + start, 512)) + bias[:, pl.ds(1024 + start, 512)]
+            act_part, slope_part = gelu_parts(pre)
+            act[layer, :, columns] = act_part.astype(BF16)
+            slope[layer, :, columns] = slope_part.astype(BF16)
+            return carry
+
+        lax.fori_loop(0, 4, hidden, 0)
+        if first:
+            three.settle(2)
+        join = new_join()
+        for quarter in range(4):
+            join.offer(quarter, across(act[layer], quarter_of(weights, quarter, OUTER, 2048)))
+        join.wait()
+
+        def after_hidden(block, total):
+            rows = slab_of(block)
+            live = live_rows(lengths, block, SLAB)
+            branch = join.total(rows) + rows_ref[1:2, :]
+            scaled, root = norm_parts(trunk[rows, :] + branch)
+            after = scaled * rows_ref[4:5, :] + rows_ref[5:6, :]
+            square = total[0] + jnp.sum(live * branch * branch, 0, keepdims=True)
+            if first:
+                normed[1, rows, :] = scaled
+                inverse[1, rows, :] = root
+                trunk[rows, :] = after
+                low[1, rows, :] = after.astype(BF16)
+                return (square,)
+            result[rows, :] = (after * live).astype(BF16)
+            grad = grad_in[rows, :].astype(F32)
+            return (square, *from_output(rows, grad, scaled, root, total[1:]))
+
+        def from_output(rows, grad, scaled, root, total, layer=layer):
+            second = norm_back(grad, scaled, root, rows_ref[4:5, :])
             small = second.astype(BF16)
             trunk[rows, :] = second
             outer_grad[layer, rows, :] = small
@@ -955,39 +825,72 @@
                 total[2] + jnp.sum(grad, 0, keepdims=True),
             )
 
-        sums[1], sums[4], sums[5] = lax.fori_loop(0, 256 // SLAB, from_output, (sums[1], sums[4], sums[5]))
-        loads["slope"].wait()
-        if not last:
-            loads["outer"].wait()
-
-        def hidden(tile, carry):
+        initial = (zero,) if first else (zero,) * 4
+        square, *back = lax.fori_loop(0, 256 // SLAB, after_hidden, initial)
+        total_ref[4 + 3 * layer : 5 + 3 * layer, 0:1024] = square
+        if not first:
+            sums[1], sums[4], sums[5] = back
+
+    for item in gathers:
+        item.close()
+    grouped = [landings[9 * group : 9 * group + 9] for group in range(3)]
+    one, two, three = (
+        Scatter(weights, group, [grouped[group][3 * i : 3 * i + 3] for i in range(3)], scatter_send, scatter_recv)
+        for group in range(3)
+    )
+    closing += [one, two, three]
+    head_sum = [jnp.zeros((1, 512), F32)] * 2
+    each = range(3)
+    idle = lambda: None
+
+    def onward(group, phase):
+        for third in each:
+            group.onward(phase, third)
+
+    for layer in (1, 0):
+        last = layer == 0
+        heads = HeadsBack(
+            mixed_grad.at[layer], taken.at[layer], key_value.at[layer], query_buf.at[layer], grads.at[layer],
+            turn_local.at[layer], turn_send.at[layer], turn_recv.at[layer], turn_back_send.at[layer],
+            turn_back_recv.at[layer],
+        )
+        closing.append(heads)
+        if last:
+
+            def from_above(block, total):
+                rows = slab_of(block)
+                grad = trunk[rows, :] + join.total(rows)
+                return from_output(rows, grad, normed[1, rows, :], inverse[1, rows, :], total, 0)
+
+            sums[1], sums[4], sums[5] = lax.fori_loop(0, 256 // SLAB, from_above, (sums[1], sums[4], sums[5]))
+
+        def hidden_back(tile, carry):
             start = pl.multiple_of(tile * 512, 512)
             columns = pl.ds(start, 512)
             grad = straight(outer_grad[layer], columns_of(weights, OUTER + start, 512))
-            small = (grad * slope[:, columns].astype(F32)).astype(BF16)
+            small = (grad * slope[layer, :, columns].astype(F32)).astype(BF16)
             inner_grad[layer, :, columns] = small
             total_ref[0:1, columns] += jnp.sum(small.astype(F32), 0, keepdims=True)
             return carry
 
-        lax.fori_loop(0, 4, hidden, 0)
-        if not last:
-            loads["inner"].wait()
+        lax.fori_loop(0, 4, hidden_back, 0)
+        join = new_join()
         for quarter in range(4):
-            joins[0].offer(quarter, across(inner_grad[layer], quarter_of(weights, quarter, INNER, 2048)))
+            join.offer(quarter, across(inner_grad[layer], quarter_of(weights, quarter, INNER, 2048)))
         if last:
             weight_grad(weights, OUTER, outer_grad[...].reshape(512, 1024), act, 2048)
-            two.first(0, 2)
+            for third in each:
+                three.first(0, third)
             weight_grad(weights, INNER, middle[...].reshape(512, 1024), inner_grad, 2048)
-            two.first(0, 1)
-        joins[0].wait()
+        join.wait()
 
         def from_middle(block, total):
             rows = slab_of(block)
-            grad = trunk[rows, :] + joins[0].total(rows)
-            scaled = normed[0, rows, :]
-            first = norm_back(grad, scaled, inverse[0, rows, :], rows_ref[2:3, :])
-            small = first.astype(BF16)
-            trunk[rows, :] = first
+            grad = trunk[rows, :] + join.total(rows)
+            scaled = normed[2 * layer, rows, :]
+            before = norm_back(grad, scaled, inverse[2 * layer, rows, :], rows_ref[2:3, :])
+            small = before.astype(BF16)
+            trunk[rows, :] = before
             attn_grad[layer, rows, :] = small
             return (
                 total[0] + jnp.sum(small.astype(F32), 0, keepdims=True),
@@ -996,30 +899,22 @@
             )
 
         sums[0], sums[2], sums[3] = lax.fori_loop(0, 256 // SLAB, from_middle, (sums[0], sums[2], sums[3]))
-        if not last:
-            loads["out"].wait()
         mixed_grad[layer] = straight(attn_grad[layer], columns_of(weights, OUT, 512)).astype(BF16)
         heads.start()
         if last:
             weight_grad(weights, OUT, attn_grad[...].reshape(512, 1024), mixed, 512)
             columns = jnp.concatenate(sums + [jnp.zeros((LANES - 6, 1024), F32)], 0).T
             weights[:, :, :, :, :, EXTRA : EXTRA + LANES] = columns.astype(BF16).reshape(*SHARDS, 16, LANES)
-            two.first(0, 0)
-        else:
-            load("normed", normed_in.at[0], normed)
-            load("inverse", inverse_in.at[0], inverse)
-            load("slope", slope_in.at[0], slope)
-        for name in ("unit", "exact", "logs"):
-            loads[name].wait()
-        heads.attend(length, unit, exact, logs, grad_buf, query_sum)
+            for third in each:
+                two.first(0, third)
+        heads.attend(
+            length, unit.at[layer], exact.at[layer], logs.at[layer], grad_buf, query_sum,
+            (lambda: onward(three, 0)) if last else idle, (lambda: onward(two, 0)) if last else idle,
+        )
         if last:
-            for third in (2, 1, 0):
-                two.onward(0, third)
-        else:
-            load("unit", unit_in.at[0], unit)
-            load("exact", exact_in.at[0], exact)
-            load("logs", logs_in.at[0], logs)
-            loads["qkv"].wait()
+            for third in each:
+                three.settle(0, third)
+                three.first(1, third)
         heads.collect(0)
         heads.collect(1)
         head_sum[1] = head_sum[1] + jnp.sum(grads[layer, 1].astype(F32), 0, keepdims=True)
@@ -1028,145 +923,153 @@
             + across(grads[layer, 1], quarter_of(weights, quarter, VALUE, 512))
             for quarter in range(4)
         ]
+        left = low[...].reshape(512, 1024)
+        if last:
+            weight_grad(weights, KEY, left, grads.at[:, 0], 512)
+            one.first(0, 1)
+            weight_grad(weights, VALUE, left, grads.at[:, 1], 512)
+            one.first(0, 2)
         heads.collect(2)
         head_sum[0] = head_sum[0] + jnp.sum(grads[layer, 2].astype(F32), 0, keepdims=True)
+        join = new_join()
         for quarter in range(4):
-            joins[1].offer(
+            join.offer(
                 quarter, early[quarter] + across(grads[layer, 2], quarter_of(weights, quarter, QUERY, 512))
             )
         if last:
-            left = low[...].reshape(512, 1024)
-            for start, j in ((KEY, 0), (VALUE, 1), (QUERY, 2)):
-                weight_grad(weights, start, left, grads.at[:, j], 512)
-            for third in range(3):
-                one.first(0, third)
+            weight_grad(weights, QUERY, left, grads.at[:, 2], 512)
+            one.first(0, 0)
             total_ref[1:2, 0:512] = head_sum[0]
             total_ref[1:2, 512:1024] = head_sum[1]
-            total_ref[2:8, 0:1024] = squares[0:6, :]
             count = sum(jnp.clip(lengths[s] - c * ROWS, 0, ROWS) for s in range(2)).astype(F32)
             total_ref[1:2, 1024:1152] = jnp.full((1, LANES), count, F32)
         else:
-            for name in ("act", "mixed", "middle", "low0", "low1", "result"):
-                loads[name].wait()
-        joins[1].wait()
-
-        def to_input(block, carry):
-            rows = slab_of(block)
-            trunk[rows, :] += joins[1].total(rows)
-            return carry
-
-        lax.fori_loop(0, 256 // SLAB, to_input, 0)
-        closing += [heads] + joins
+            join.wait()
 
     totals = Totals(total_ref, total_land, total_send, total_recv)
     totals.first(0)
-    for third in (2, 1, 0):
+    for third in each:
         two.settle(0, third)
         two.first(1, third)
+    onward(three, 1)
+    join.wait()
     for s in range(2):
-        stream_grad[:, s, :] = trunk[s * ROWS : s * ROWS + ROWS, :]
-    for third in range(3):
-        one.onward(0, third)
+        rows = pl.ds(s * ROWS, ROWS)
+        stream_grad[:, s, :] = trunk[rows, :] + join.total(rows)
+    onward(one, 0)
     totals.settle(0)
     totals.first(1)
-    for third in (2, 1, 0):
-        two.onward(1, third)
-    pairs = [result[s * ROWS : s * ROWS + ROWS, :].astype(F32) for s in range(2)]
-    result_ref[...] = jnp.stack(pairs, 1).astype(BF16)
-    for third in range(3):
+    for third in each:
+        three.settle(1, third)
+        three.direct(2, third)
+    onward(two, 1)
+    result_ref[...] = jnp.stack([result[s * ROWS : s * ROWS + ROWS, :].astype(F32) for s in range(2)], 1).astype(BF16)
+    for third in (1, 2, 0):
         one.settle(0, third)
         one.direct(1, third)
-    for third in (2, 1, 0):
+    totals.settle(1)
+    totals.first(2)
+    for third in each:
         two.settle(1, third)
         two.direct(2, third)
-    totals.settle(1)
-    totals.first(2)
-    for third in range(3):
+    for third in each:
+        three.arrive(2, third)
+    for third in (1, 2, 0):
         one.arrive(1, third)
         one.direct(2, third)
-    for third in (2, 1, 0):
+
+    def mine(start, width):
+        return weights[x // 2, at["z"], x % 2, at["y"], :, start : start + width].astype(F32)
+
+    outer_out[...] = mine(OUTER, 2048)
+    for third in each:
         two.arrive(2, third)
+    output_out[...] = mine(OUT, 512)
+    inner_out[...] = mine(INNER, 2048)
+    vector_out[...] = mine(EXTRA, LANES).T[0:8, :]
     totals.settle(2)
-    for third in range(3):
-        one.arrive(2, third)
-    x = at["x"]
-
-    def own(start, width):
-        return weights[x // 2, at["z"], x % 2, at["y"], :, start : start + width].astype(F32)
-
-    query_out[...] = own(QUERY, 512)
-    key_out[...] = own(KEY, 512)
-    value_out[...] = own(VALUE, 512)
-    output_out[...] = own(OUT, 512)
-    inner_out[...] = own(INNER, 2048)
-    outer_out[...] = own(OUTER, 2048)
-    vector_out[...] = own(EXTRA, LANES).T[0:8, :]
-    for item in closing:
-        item.close()
     scale = 1.0 / (total_ref[1:2, 1024:1025] * 1024.0)
     square = jnp.sum(total_ref[:, 0:1024], 1, keepdims=True)
     root_ref[...] = jnp.broadcast_to(jnp.sqrt(square * scale + 1e-06), root_ref.shape)
-
-
-def run_backward(grad, rows, squares, lengths, saved):
+    for third in (1, 2, 0):
+        one.arrive(2, third)
+    query_out[...] = mine(QUERY, 512)
+    key_out[...] = mine(KEY, 512)
+    value_out[...] = mine(VALUE, 512)
+    for item in closing + joined[-2:]:
+        item.close()
+
+
+def run_layers(*arguments):
     dma = pltpu.SemaphoreType.DMA
     out = lambda *shape: jax.ShapeDtypeStruct(shape, F32)
+    vmem = lambda kind, *shape: pltpu.VMEM(shape, kind)
     return pl.pallas_call(
-        backward_kernel,
+        layers_kernel,
         out_shape=(
             out(ROWS, 2, 1024), jax.ShapeDtypeStruct((ROWS, 2, 1024), BF16),
             out(16, 512), out(16, 512), out(16, 512), out(16, 512), out(16, 2048), out(16, 2048),
             out(8, 16), out(8, 2048), out(8, LANES),
         ),
-        in_specs=[spec(pltpu.VMEM)] * 3 + [spec(pltpu.SMEM)] + [spec(pl.ANY)] * len(saved),
+        in_specs=[spec(pltpu.VMEM)] * 17 + [spec(pltpu.SMEM)],
         out_specs=(spec(pltpu.VMEM),) * 11,
         scratch_shapes=[
-            pltpu.VMEM((*SHARDS, 16, WIDTH), BF16),
-            pltpu.VMEM((3, 1024, LANES), BF16),
-            pltpu.VMEM((1024, LANES), F32),
-            pltpu.VMEM((8, 256), F32),
-            pltpu.VMEM((2, 256, 512), BF16),
-            pltpu.VMEM((2, 256, 1024), F32),
-            pltpu.VMEM((2, 256, 1), F32),
-            pltpu.VMEM((2, 256, 1024), BF16),
-            pltpu.VMEM((2, 256, 2048), BF16),
-            pltpu.VMEM((256, 2048), BF16),
-            pltpu.VMEM((2, 256, 1024), BF16),
-            pltpu.VMEM((2, 256, 1024), BF16),
-            pltpu.VMEM((2, 256, 2048), BF16),
-            pltpu.VMEM((2, 256, 1024), BF16),
-            pltpu.VMEM((2, 3, 256, 512), BF16),
-            pltpu.VMEM((2, 256, 512), BF16),
-            pltpu.VMEM((256, 1024), F32),
-            pltpu.VMEM((256, 1024), BF16),
-            pltpu.VMEM((2, 1024, LANES), BF16),
-            pltpu.VMEM((2048, LANES), BF16),
-            pltpu.VMEM((2048, LANES), F32),
-            pltpu.VMEM((2, 2, 1024, LANES), BF16),
-            pltpu.VMEM((2, 1024, LANES), BF16),
-            pltpu.VMEM((2, 2, 2, 256, 512), BF16),
-            pltpu.VMEM((2, 2, 2, 256, 512), BF16),
-            pltpu.VMEM((3, 3, 8, 2048), F32),
-            dma((32,)),
+            vmem(BF16, *SHARDS, 16, WIDTH),
+            vmem(F32, 1, 3072),
+            vmem(F32, 8, 1024),
+            vmem(BF16, 2, 256, 1024),
+            vmem(BF16, 256, 1024),
+            vmem(BF16, 256, 1024),
+            vmem(F32, 256, 1024),
+            vmem(BF16, 3, 256, 512),
+            vmem(BF16, 2, 3, 1024, LANES),
+            vmem(F32, 2, 1024, LANES),
+            vmem(F32, 2, 8, 256),
+            vmem(BF16, 2, 1024, LANES),
+            vmem(BF16, 2, 256, 512),
+            vmem(F32, 3, 256, 1024),
+            vmem(F32, 3, 256, 1),
+            vmem(BF16, 2, 256, 1024),
+            vmem(BF16, 2, 256, 2048),
+            vmem(BF16, 2, 256, 2048),
+            vmem(BF16, 2, 256, 1024),
+            vmem(BF16, 2, 256, 2048),
+            vmem(BF16, 2, 256, 1024),
+            vmem(BF16, 2, 3, 256, 512),
+            vmem(BF16, 2, 256, 512),
+            vmem(BF16, 2, 1024, LANES),
+            vmem(BF16, 2048, LANES),
+            vmem(F32, 2048, LANES),
+            vmem(BF16, 2, 2, 1024, LANES),
+            vmem(BF16, 2, 1024, LANES),
+            vmem(BF16, 2, 2, 256, 512),
+            vmem(BF16, 2, 2, 256, 512),
+            vmem(F32, 3, 3, 8, 2048),
+            dma((2, 4)),
+            dma((3, 3, 3, 4)),
+            dma((3, 3, 3, 4)),
+            dma((2, 3, 7)),
+            dma((2, 3, 7)),
+            dma((2, 7)),
+            dma((2, 7)),
+            dma((8, 2)),
+            dma((8, 2)),
             dma((2, 4)),
             dma((2, 7)),
             dma((2, 7)),
             dma((2, 3, 7)),
             dma((2, 3, 7)),
-            dma((2, 2, 2)),
-            dma((2, 2, 2)),
             dma((3, 3)),
             dma((3, 3)),
-            dma((2, 3, 3, 6)),
-            dma((2, 3, 3, 6)),
-            *landing_shapes(0),
-            *landing_shapes(1),
+            dma((3, 3, 3, 6)),
+            dma((3, 3, 3, 6)),
+            *(shape for group in range(3) for shape in landing_shapes(group)),
         ],
         compiler_params=pltpu.CompilerParams(
-            collective_id=4, has_side_effects=True, vmem_limit_bytes=LIMIT
+            collective_id=3, has_side_effects=True, vmem_limit_bytes=LIMIT
         ),
-        name="backward_layers",
-    )(grad, rows, squares, lengths, *saved)
+        name="layers",
+    )(*arguments)
 
 
 def finish_kernel(
@@ -1227,13 +1130,11 @@
     second_shift,
     cotangent,
 ):
-    grad_in = cotangent
-    low, grad, result, rows, squares, *saved = run_forward(
-        stream, grad_in, query_weight, key_weight, value_weight, output_weight.T, inner_weight, outer_weight.T,
+    partial = run_layers(
+        stream, cotangent, query_weight, key_weight, value_weight, output_weight.T, inner_weight, outer_weight.T,
         output_bias, outer_bias, first_gain, first_shift, second_gain, second_shift,
         query_bias, value_bias, inner_bias, lengths,
     )
-    partial = run_backward(grad, rows, squares, lengths, [low, result, *saved])
     (
         result, stream_grad, grad_query, grad_key, grad_value, grad_output, grad_inner, grad_outer,
         query_sum, value_sum, inner_sum, *vectors, roots,

time: 243 us -> 235 us (0.967); the launches traced: 243 us -> 232 us
  Pallas kernels: 242 us -> 231 us
    pallas_call x2 -> x1, Pallas kernels: 240 us -> 228 us  [run_layers(): pl.pallas_call(layers_kernel, out_shape=(out(ROWS, 2, 1024), jax.ShapeDty...]
where the time goes in v3:
time: 235 us; the launch traced here: 232 us
  Pallas kernels  231 us (98%)
    pallas_call x1, Pallas kernels, run_layers(): pl.pallas_call(layers_kernel, out_shape=(out(ROWS, 2, 1024), jax.ShapeDty...  228 us

profile of v3, /device:TPU:0, one launch (start us, length us, event | category | flops | bytes accessed | tf_op | source)
XLA Modules:
  0.0 231.9 jit_solution(1692989500819042451)
XLA Ops:
  0.7 227.9 %layers.1 = (f32[128,2,1024]{2,1,0:T(2,128)}, bf16[128,2,1024]{2,1,0:T(2,128)(2,1)}, f32[16,512]{1,0:T(8,128)}, f32[16,512]{1,0:T(8,128)}, f32[16,512]{1,0:T(8,1...) custom-call(bf16[128,2,1024]{2,1,0:T(2,128)(2,1)} %stream.1, ...), custom_call_target="tpu_custom_call" | custom-call | tf_op jit(solution)/shard_map/layers/pallas_call | solution.py:1007
  228.6 2.9 %finish.1 = (bf16[128,2,1024]{2,1,0:T(2,128)(2,1)}, f32[128,2,1024]{2,1,0:T(2,128)}, f32[16,512]{1,0:T(8,128)}, f32[16,512]{1,0:T(8,128)}, f32[16,512]{1,0:T(8,1...) custom-call(f32[128,2,1024]{2,1,0:T(2,128)} %get-tuple-element.47.st, ...), custom_call_target="tpu_custom_call" | custom-call | tf_op jit(solution)/shard_map/finish/pallas_call | solution.py:1100

commit v4 on v3

--- a/solution.py
+++ b/solution.py
@@ -73,6 +73,23 @@
     )
 
 
+def drain(ref, sem):
+    pltpu.make_async_copy(ref, ref, sem).wait()
+
+
+def bulk(ref, count, group):
+    start, end = GROUPS[group]
+    picks = {
+        3: (0, 0, 0, slice(0, 3)),
+        8: (0, slice(0, 2), 0),
+        12: (0, slice(0, 3), 0),
+        32: (0,),
+        48: (slice(None), slice(0, 3)),
+    }[count]
+    picks = picks + (slice(None),) * (5 - len(picks))
+    return ref.at[picks + (pl.ds(start, end - start),)]
+
+
 def shards(ref, at, whole, cols):
     x = at["x"]
     xh = slice(None) if "x" in whole else x // 2
@@ -141,49 +158,52 @@
     def send(self, third, phase, kind, origin, cols, step):
         order = ORDERS[third]
         block = shards(self.weights, origin, order[:phase], cols)
-        index = (self.group, third, phase, kind)
+        if kind is None or kind > 1:
+            slot = 6
+        else:
+            slot = 2 * third + kind
         copy = remote(
-            block, block, self.send_sem.at[index], self.recv_sem.at[index],
+            block, block, self.send_sem.at[self.group, phase], self.recv_sem.at[self.group, phase, slot],
             device(shifted(self.at, order[phase], step)),
         )
         copy.start()
         self.sent[third, phase, kind] = copy
 
-    def first(self, phase):
-        for third in range(3):
-            low, high = self.parts[third]
-            both = (low[0], low[1] + high[1])
-            self.send(third, phase, 0, self.at, both, 1)
-            self.send(third, phase, 1, self.at, both, -1)
+    def first(self, phase, thirds_now=range(3), pieces=(0, 1)):
+        for piece in pieces:
+            for third in thirds_now:
+                low, high = self.parts[third]
+                self.send(third, phase, 2 * piece, self.at, (low, high)[piece], 1)
+                self.send(third, phase, 2 * piece + 1, self.at, (high, low)[piece], -1)
 
     def direct(self, phase):
         for third in range(3):
             low, high = self.parts[third]
             for step in (1, 2, 3):
-                self.send(third, phase, step - 1, self.at, (low[0], low[1] + high[1]), step)
+                self.send(third, phase, None, self.at, (low[0], low[1] + high[1]), step)
 
     def arrive(self, phase):
-        for third in range(3):
-            for kind in range(3):
-                self.sent[third, phase, kind].wait_recv()
-
-    def onward(self, phase):
-        for third in range(3):
+        drain(bulk(self.weights, (3, 12)[phase], self.group), self.recv_sem.at[self.group, phase, 6])
+
+    def onward(self, phase, thirds_now=range(3)):
+        for third in thirds_now:
             axis = ORDERS[third][phase]
             low, high = self.parts[third]
             self.sent[third, phase, 0].wait_recv()
-            self.send(third, phase, 2, shifted(self.at, axis, -1), low, 1)
+            self.send(third, phase, 4, shifted(self.at, axis, -1), low, 1)
             self.sent[third, phase, 1].wait_recv()
-            self.send(third, phase, 3, shifted(self.at, axis, 1), high, -1)
+            self.send(third, phase, 5, shifted(self.at, axis, 1), high, -1)
 
     def settle(self, phase):
-        for third in range(3):
-            self.sent[third, phase, 2].wait_recv()
-            self.sent[third, phase, 3].wait_recv()
+        drain(bulk(self.weights, (2, 8, 32)[phase], self.group), self.recv_sem.at[self.group, phase, 6])
 
     def close(self):
-        for copy in self.sent.values():
-            copy.wait_send()
+        for phase in range(3):
+            drain(bulk(self.weights, (3, 12, 48)[phase], self.group), self.send_sem.at[self.group, phase])
+
+
+def seven(ref):
+    return ref.at[pl.ds(0, 7 * ROWS)]
 
 
 class Heads:
@@ -199,7 +219,7 @@
         peer = lax.rem(self.c + d, 8)
         return remote(
             part(self.own.at[j], peer), self.unit.at[j, rows_of(self.c)],
-            self.send_sem.at[j, d - 1], self.recv_sem.at[j, d - 1], (self.f, peer, self.t),
+            self.send_sem.at[j], self.recv_sem.at[j, d - 1 if j == 2 else 0], (self.f, peer, self.t),
         )
 
     def keep(self, j):
@@ -211,7 +231,7 @@
         peer = lax.rem(self.c + d, 8)
         return remote(
             self.outcome.at[rows_of(peer)], part(self.mixed, self.c),
-            self.back_send.at[d - 1], self.back_recv.at[d - 1], (self.f, peer, self.t),
+            self.back_send.at[0], self.back_recv.at[0], (self.f, peer, self.t),
         )
 
     def keep_back(self):
@@ -231,12 +251,11 @@
                 self.push(j, d).start()
             self.keep(j).start()
 
-    def attend(self, length, exact, logs, midway):
+    def attend(self, length, exact, logs):
         c = self.c
         for j in range(2):
             self.keep(j).wait()
-            for d in range(1, 8):
-                self.push(j, d).wait_recv()
+            drain(seven(self.outcome), self.recv_sem.at[j, 0])
         mask = key_mask(length, 0, 8 * ROWS)
         keys = self.unit[0]
         values_across = self.unit[1].T
@@ -266,21 +285,17 @@
 
             return carry
 
-        lax.fori_loop(0, 4, step, 0)
-        midway()
-        lax.fori_loop(4, 8, step, 0)
+        lax.fori_loop(0, 8, step, 0)
         self.keep_back().start()
 
     def collect(self):
         self.keep_back().wait()
-        for d in range(1, 8):
-            self.answer(d).wait_recv()
+        drain(seven(self.outcome), self.back_recv.at[0])
 
     def close(self):
-        for d in range(1, 8):
-            self.answer(d).wait_send()
-            for j in range(3):
-                self.push(j, d).wait_send()
+        drain(seven(self.outcome), self.back_send.at[0])
+        for j in range(3):
+            drain(seven(self.outcome), self.send_sem.at[j])
 
 
 class Join:
@@ -288,26 +303,24 @@
         t = lax.axis_index("tensor")
         self.partner = (lax.axis_index("fsdp"), lax.axis_index("context"), 1 - t)
         self.sent, self.landed = sent.at[number % 2], landed.at[number % 2]
-        self.send_sem, self.recv_sem = send_sem.at[number], recv_sem.at[number]
+        self.send_sem, self.recv_sem = send_sem.at[number % 2], recv_sem.at[number % 2]
         self.before = before
 
     def copy(self, half):
         return remote(
-            self.sent.at[half], self.landed.at[half], self.send_sem.at[half], self.recv_sem.at[half],
-            self.partner,
+            self.sent.at[half], self.landed.at[half], self.send_sem, self.recv_sem, self.partner,
         )
 
     def offer(self, quarter, term):
         half, side = quarter // 2, quarter % 2
-        if side == 0 and self.before is not None:
-            self.before.copy(half).wait_send()
+        if quarter == 0 and self.before is not None:
+            self.before.close()
         self.sent[half, :, side * 256 : side * 256 + 256] = term.astype(BF16)
         if side == 1:
             self.copy(half).start()
 
     def wait(self):
-        for half in range(2):
-            self.copy(half).wait_recv()
+        drain(self.landed, self.recv_sem)
 
     def total(self, rows):
         return jnp.concatenate(
@@ -316,8 +329,7 @@
         )
 
     def close(self):
-        for half in range(2):
-            self.copy(half).wait_send()
+        drain(self.sent, self.send_sem)
 
 
 def gelu_parts(argument):
@@ -403,10 +415,13 @@
         land = self.landings[third][phase].at[kind]
         if cols[1] != land.shape[-1]:
             land = land.at[..., pl.ds(0, cols[1])]
-        index = (self.group, third, phase, kind)
+        slot = kind // 2 + 1 if kind > 1 else kind
+        if phase in DIRECT[self.group]:
+            slot = 0
         copy = remote(
             shards(self.work, shifted(self.at, axis, away), whole, cols), land,
-            self.send_sem.at[index], self.recv_sem.at[index], device(shifted(self.at, axis, step)),
+            self.send_sem.at[self.group, phase], self.recv_sem.at[self.group, phase, third, slot],
+            device(shifted(self.at, axis, step)),
         )
         copy.start()
         self.sent[third, phase, kind] = copy
@@ -434,23 +449,26 @@
                 total = total + land[at + (slice(None), pl.ds(0, cols[1]))].astype(F32)
             self.work[index] = total.astype(BF16)
 
-        count_x = 4 if wide["x"] else 1
         count_z = 4 if wide["z"] else 1
-        if count_x * count_z == 1:
-            one(0, 0)
+        if not wide["x"]:
+            for iz in range(count_z):
+                one(0, iz)
         else:
-            def turn(i, carry):
-                one(i // count_z, i % count_z)
+            def turn(ix, carry):
+                for iz in range(count_z):
+                    one(ix, iz)
                 return carry
 
-            lax.fori_loop(0, count_x * count_z, turn, 0)
-
-    def first(self, phase, third):
+            lax.fori_loop(0, 4, turn, 0)
+
+    def first(self, phase, third, pieces=(0, 1)):
         low, high = self.parts[third]
-        self.send(third, phase, 0, 2, low, 1)
-        self.send(third, phase, 1, 2, high, -1)
-        self.send(third, phase, 2, 1, high, 1)
-        self.send(third, phase, 3, -1, low, -1)
+        if 0 in pieces:
+            self.send(third, phase, 0, 2, low, 1)
+            self.send(third, phase, 1, 2, high, -1)
+        if 1 in pieces:
+            self.send(third, phase, 2, 1, high, 1)
+            self.send(third, phase, 3, -1, low, -1)
 
     def direct(self, phase, third):
         low, high = self.parts[third]
@@ -459,8 +477,7 @@
 
     def arrive(self, phase, third):
         low, high = self.parts[third]
-        for kind in range(3):
-            self.sent[third, phase, kind].wait_recv()
+        drain(self.landings[third][phase], self.recv_sem.at[self.group, phase, third, 0])
         self.add(third, phase, 0, (low[0], low[1] + high[1]), (0, 1, 2))
 
     def onward(self, phase, third):
@@ -474,16 +491,16 @@
 
     def settle(self, phase, third):
         low, high = self.parts[third]
-        self.sent[third, phase, 2].wait_recv()
-        self.sent[third, phase, 5].wait_recv()
+        axis, whole = self.ring(third, phase)
+        block = shards(self.work, self.at, whole, (low[0], low[1] + high[1]))
+        for slot in (2, 3):
+            drain(block, self.recv_sem.at[self.group, phase, third, slot])
         self.add(third, phase, 0, high, (2, 5))
-        self.sent[third, phase, 3].wait_recv()
-        self.sent[third, phase, 4].wait_recv()
         self.add(third, phase, 0, low, (3, 4))
 
     def close(self):
-        for copy in self.sent.values():
-            copy.wait_send()
+        for phase in range(3):
+            drain(bulk(self.work, (48, 12, 3)[phase], self.group), self.send_sem.at[self.group, phase])
 
 
 DIRECT = ((1, 2), (2,), (2,))
@@ -514,8 +531,7 @@
 
     def copy(self, phase, step):
         return remote(
-            self.total, self.landed.at[phase, step - 1], self.send_sem.at[phase, step - 1],
-            self.recv_sem.at[phase, step - 1], device(shifted(self.at, "xyz"[phase], step)),
+            self.total, self.landed.at[phase, step - 1], self.send_sem.at[phase], self.recv_sem.at[phase], device(shifted(self.at, "xyz"[phase], step)),
         )
 
     def first(self, phase):
@@ -523,8 +539,8 @@
             self.copy(phase, step).start()
 
     def settle(self, phase):
-        for step in (1, 2, 3):
-            self.copy(phase, step).wait()
+        drain(self.landed.at[phase], self.recv_sem.at[phase])
+        drain(self.landed.at[phase], self.send_sem.at[phase])
         self.total[...] += self.landed[phase, 0] + self.landed[phase, 1] + self.landed[phase, 2]
 
 
@@ -543,7 +559,7 @@
         peer = lax.rem(self.c + d, 8)
         return remote(
             part(self.mixed_grad, peer), self.taken.at[rows_of(self.c)],
-            self.send_sem.at[d - 1], self.recv_sem.at[d - 1], (self.f, peer, self.t),
+            self.send_sem.at[0], self.recv_sem.at[0], (self.f, peer, self.t),
         )
 
     def keep(self):
@@ -555,7 +571,7 @@
         peer = lax.rem(self.c + d, 8)
         return remote(
             self.sources[j].at[rows_of(peer)], part(self.grads.at[j], self.c),
-            self.back_send.at[j, d - 1], self.back_recv.at[j, d - 1], (self.f, peer, self.t),
+            self.back_send.at[j], self.back_recv.at[j, 0], (self.f, peer, self.t),
         )
 
     def keep_back(self, j):
@@ -578,8 +594,7 @@
         query_sum[...] = jnp.zeros_like(query_sum)
         ahead()
         self.keep().wait()
-        for d in range(1, 8):
-            self.push(d).wait_recv()
+        drain(seven(self.taken), self.recv_sem.at[0])
         for block in range(8):
             grad_buf[pl.ds(block * 256, 256), :] = by_head(self.taken[pl.ds(block * ROWS, ROWS), :])
         head_row = lax.broadcasted_iota(jnp.int32, (8, LANES), 0)
@@ -640,14 +655,12 @@
 
     def collect(self, j):
         self.keep_back(j).wait()
-        for d in range(1, 8):
-            self.answer(j, d).wait_recv()
+        drain(seven(self.taken), self.back_recv.at[j, 0])
 
     def close(self):
-        for d in range(1, 8):
-            self.push(d).wait_send()
-            for j in range(3):
-                self.answer(j, d).wait_send()
+        drain(seven(self.taken), self.send_sem.at[0])
+        for j in range(3):
+            drain(seven(self.taken), self.back_send.at[j])
 
 
 def put_quarter(work, quarter, start, value):
@@ -681,7 +694,7 @@
     attn_grad, inner_grad, outer_grad, grads, mixed_grad, taken, grad_buf, query_sum, key_value, query_buf,
     sent, landed, total_land,
     local_sem, gather_send, gather_recv, send_sem, recv_sem, back_send, back_recv, pair_send, pair_recv,
-    turn_local, turn_send, turn_recv, turn_back_send, turn_back_recv, total_send, total_recv,
+    turn_send, turn_recv, total_send, total_recv,
     scatter_send, scatter_recv, *landings,
 ):
     at = place()
@@ -716,17 +729,19 @@
     bias[:, 0:512] = query_bias[...].astype(F32).reshape(1, 512)
     bias[:, 512:1024] = value_bias[...].astype(F32).reshape(1, 512)
     bias[:, 1024:3072] = inner_bias[...].astype(F32).reshape(1, 2048)
+    position = c * ROWS + lax.broadcasted_iota(jnp.int32, (ROWS, 1), 0)
+    rows_by_sequence(cotangent, grad_in, lambda s: jnp.where(position < lengths[s], 1.0, 0.0))
+    trunk[...] = low[0].astype(F32)
+    total_ref[...] = jnp.zeros_like(total_ref)
     one.arrive(1)
     one.first(2)
     two.onward(1)
     three.onward(1)
-    position = c * ROWS + lax.broadcasted_iota(jnp.int32, (ROWS, 1), 0)
-    rows_by_sequence(cotangent, grad_in, lambda s: jnp.where(position < lengths[s], 1.0, 0.0))
-    trunk[...] = low[0].astype(F32)
-    total_ref[...] = jnp.zeros_like(total_ref)
     one.onward(2)
     two.settle(1)
     two.first(2)
+    three.settle(1)
+    three.first(2, (1,))
     one.settle(2)
     length = lengths[c // 4]
     zero = jnp.zeros((1, 1024), F32)
@@ -735,18 +750,20 @@
     for layer in range(LAYERS):
         first = layer == 0
         heads = Heads(
-            own, unit.at[layer], outcome.at[layer], mixed.at[layer], local_sem.at[layer],
-            send_sem.at[layer], recv_sem.at[layer], back_send.at[layer], back_recv.at[layer],
+            own, unit.at[layer], outcome.at[layer], mixed.at[layer], local_sem,
+            send_sem, recv_sem, back_send, back_recv,
         )
         if not first:
             closing.pop().close()
         closing.append(heads)
         heads.project(low[layer], weights, bias)
         if first:
-            three.settle(1)
-            three.first(2)
-            two.onward(2)
-        heads.attend(length, exact.at[layer], logs.at[layer], (lambda: three.onward(2)) if first else (lambda: None))
+            two.onward(2, (0, 2))
+            three.first(2, (0, 2))
+            two.onward(2, (1,))
+        heads.attend(length, exact.at[layer], logs.at[layer])
+        if first:
+            three.onward(2)
         heads.collect()
         if first:
             two.settle(2)
@@ -838,7 +855,7 @@
         Scatter(weights, group, [grouped[group][3 * i : 3 * i + 3] for i in range(3)], scatter_send, scatter_recv)
         for group in range(3)
     )
-    closing += [one, two, three]
+    closing = [one, two, three] + closing
     head_sum = [jnp.zeros((1, 512), F32)] * 2
     each = range(3)
     idle = lambda: None
@@ -851,9 +868,9 @@
         last = layer == 0
         heads = HeadsBack(
             mixed_grad.at[layer], taken.at[layer], key_value.at[layer], query_buf.at[layer], grads.at[layer],
-            turn_local.at[layer], turn_send.at[layer], turn_recv.at[layer], turn_back_send.at[layer],
-            turn_back_recv.at[layer],
-        )
+            local_sem, turn_send, turn_recv, send_sem, recv_sem,
+        )
+        closing.pop().close()
         closing.append(heads)
         if last:
 
@@ -879,9 +896,11 @@
             join.offer(quarter, across(inner_grad[layer], quarter_of(weights, quarter, INNER, 2048)))
         if last:
             weight_grad(weights, OUTER, outer_grad[...].reshape(512, 1024), act, 2048)
-            for third in each:
-                three.first(0, third)
+            for third in (1, 0, 2):
+                three.first(0, third, (0,))
+            three.first(0, 1, (1,))
             weight_grad(weights, INNER, middle[...].reshape(512, 1024), inner_grad, 2048)
+            two.first(0, 1)
         join.wait()
 
         def from_middle(block, total):
@@ -902,19 +921,22 @@
         mixed_grad[layer] = straight(attn_grad[layer], columns_of(weights, OUT, 512)).astype(BF16)
         heads.start()
         if last:
+            for third in (0, 2):
+                three.first(0, third, (1,))
             weight_grad(weights, OUT, attn_grad[...].reshape(512, 1024), mixed, 512)
             columns = jnp.concatenate(sums + [jnp.zeros((LANES - 6, 1024), F32)], 0).T
             weights[:, :, :, :, :, EXTRA : EXTRA + LANES] = columns.astype(BF16).reshape(*SHARDS, 16, LANES)
-            for third in each:
-                two.first(0, third)
+            for third in (0, 2):
+                two.first(0, third, (0,))
         heads.attend(
             length, unit.at[layer], exact.at[layer], logs.at[layer], grad_buf, query_sum,
-            (lambda: onward(three, 0)) if last else idle, (lambda: onward(two, 0)) if last else idle,
+            (lambda: onward(three, 0)) if last else idle, (lambda: two.onward(0, 1)) if last else idle,
         )
         if last:
-            for third in each:
-                three.settle(0, third)
-                three.first(1, third)
+            for third in (0, 2):
+                two.first(0, third, (1,))
+            for third in (0, 2):
+                two.onward(0, third)
         heads.collect(0)
         heads.collect(1)
         head_sum[1] = head_sum[1] + jnp.sum(grads[layer, 1].astype(F32), 0, keepdims=True)
@@ -929,6 +951,9 @@
             one.first(0, 1)
             weight_grad(weights, VALUE, left, grads.at[:, 1], 512)
             one.first(0, 2)
+            for third in each:
+                three.settle(0, third)
+                three.first(1, third)
         heads.collect(2)
         head_sum[0] = head_sum[0] + jnp.sum(grads[layer, 2].astype(F32), 0, keepdims=True)
         join = new_join()
@@ -951,32 +976,33 @@
     for third in each:
         two.settle(0, third)
         two.first(1, third)
+    for third in (1, 2, 0):
+        one.onward(0, third)
     onward(three, 1)
     join.wait()
     for s in range(2):
         rows = pl.ds(s * ROWS, ROWS)
         stream_grad[:, s, :] = trunk[rows, :] + join.total(rows)
-    onward(one, 0)
     totals.settle(0)
     totals.first(1)
+    for third in (1, 2, 0):
+        one.settle(0, third)
+        one.direct(1, third)
+    onward(two, 1)
     for third in each:
         three.settle(1, third)
         three.direct(2, third)
-    onward(two, 1)
     result_ref[...] = jnp.stack([result[s * ROWS : s * ROWS + ROWS, :].astype(F32) for s in range(2)], 1).astype(BF16)
-    for third in (1, 2, 0):
-        one.settle(0, third)
-        one.direct(1, third)
     totals.settle(1)
     totals.first(2)
+    for third in (1, 2, 0):
+        one.arrive(1, third)
+        one.direct(2, third)
     for third in each:
         two.settle(1, third)
         two.direct(2, third)
     for third in each:
         three.arrive(2, third)
-    for third in (1, 2, 0):
-        one.arrive(1, third)
-        one.direct(2, third)
 
     def mine(start, width):
         return weights[x // 2, at["z"], x % 2, at["y"], :, start : start + width].astype(F32)
@@ -1045,24 +1071,21 @@
             vmem(BF16, 2, 2, 256, 512),
             vmem(BF16, 2, 2, 256, 512),
             vmem(F32, 3, 3, 8, 2048),
-            dma((2, 4)),
+            dma((4,)),
+            dma((3, 3)),
+            dma((3, 3, 7)),
+            dma((3,)),
+            dma((3, 7)),
+            dma((1,)),
+            dma((1,)),
+            dma((2,)),
+            dma((2,)),
+            dma((1,)),
+            dma((1,)),
+            dma((3,)),
+            dma((3,)),
+            dma((3, 3)),
             dma((3, 3, 3, 4)),
-            dma((3, 3, 3, 4)),
-            dma((2, 3, 7)),
-            dma((2, 3, 7)),
-            dma((2, 7)),
-            dma((2, 7)),
-            dma((8, 2)),
-            dma((8, 2)),
-            dma((2, 4)),
-            dma((2, 7)),
-            dma((2, 7)),
-            dma((2, 3, 7)),
-            dma((2, 3, 7)),
-            dma((3, 3)),
-            dma((3, 3)),
-            dma((3, 3, 3, 6)),
-            dma((3, 3, 3, 6)),
             *(shape for group in range(3) for shape in landing_shapes(group)),
         ],
         compiler_params=pltpu.CompilerParams(

time: 235 us -> 220 us (0.936); the launches traced: 232 us -> 220 us
  Pallas kernels: 231 us -> 219 us
    pallas_call x1, Pallas kernels: 228 us -> 216 us  [run_layers(): pl.pallas_call(layers_kernel, out_shape=(out(ROWS, 2, 1024), jax.ShapeDty...]
where the time goes in v4:
time: 220 us
  Pallas kernels  219 us (100%)
    pallas_call x1, Pallas kernels, run_layers(): pl.pallas_call(layers_kernel, out_shape=(out(ROWS, 2, 1024), jax.ShapeDty...  216 us

profile of v4, /device:TPU:0, one launch (start us, length us, event | category | flops | bytes accessed | tf_op | source)
XLA Modules:
  0.0 219.8 jit_solution(14803736883744980317)
XLA Ops:
  0.7 216.0 %layers.1 = (f32[128,2,1024]{2,1,0:T(2,128)}, bf16[128,2,1024]{2,1,0:T(2,128)(2,1)}, f32[16,512]{1,0:T(8,128)}, f32[16,512]{1,0:T(8,128)}, f32[16,512]{1,0:T(8,1...) custom-call(bf16[128,2,1024]{2,1,0:T(2,128)(2,1)} %stream.1, ...), custom_call_target="tpu_custom_call" | custom-call | tf_op jit(solution)/shard_map/layers/pallas_call | solution.py:1033
  216.7 2.9 %finish.1 = (bf16[128,2,1024]{2,1,0:T(2,128)(2,1)}, f32[128,2,1024]{2,1,0:T(2,128)}, f32[16,512]{1,0:T(8,128)}, f32[16,512]{1,0:T(8,128)}, f32[16,512]{1,0:T(8,1...) custom-call(f32[128,2,1024]{2,1,0:T(2,128)} %get-tuple-element.47.st, ...), custom_call_target="tpu_custom_call" | custom-call | tf_op jit(solution)/shard_map/finish/pallas_call | solution.py:1123

commit v5 on v4

--- a/solution.py
+++ b/solution.py
@@ -77,8 +77,8 @@
     pltpu.make_async_copy(ref, ref, sem).wait()
 
 
-def bulk(ref, count, group):
-    start, end = GROUPS[group]
+def bulk(ref, count, group, groups=GROUPS):
+    start, end = groups[group]
     picks = {
         3: (0, 0, 0, slice(0, 3)),
         8: (0, slice(0, 2), 0),
@@ -99,10 +99,10 @@
     return ref.at[xh, z, xl, y, :, pl.ds(cols[0], cols[1])]
 
 
-def thirds(group):
-    start = GROUPS[group][0]
+def thirds(group, groups=GROUPS, tiles_of=TILES):
+    start = groups[group][0]
     parts = []
-    for pair in TILES[group]:
+    for pair in tiles_of[group]:
         halves = []
         for tiles in pair:
             halves.append((start, tiles * LANES))
@@ -145,6 +145,10 @@
 
 def part(ref, peer):
     return ref.at[rows_of(peer // 4), rows_of(peer % 4)]
+
+
+GATHER_SLOTS = {(0, 0): 0, (0, 1): 1, (0, 2): 2, (1, 0): 9, (1, 1): 10, (1, 2): 17, (2, 0): 24, (2, 1): 25, (2, 2): 32}
+GATHER_COUNT = 39
 
 
 class Gather:
@@ -158,12 +162,9 @@
     def send(self, third, phase, kind, origin, cols, step):
         order = ORDERS[third]
         block = shards(self.weights, origin, order[:phase], cols)
-        if kind is None or kind > 1:
-            slot = 6
-        else:
-            slot = 2 * third + kind
+        slot = 0 if kind is None or kind > 1 else 1 + 2 * third + kind
         copy = remote(
-            block, block, self.send_sem.at[self.group, phase], self.recv_sem.at[self.group, phase, slot],
+            block, block, self.send_sem.at[self.group, phase], self.recv_sem.at[GATHER_SLOTS[self.group, phase] + slot],
             device(shifted(self.at, order[phase], step)),
         )
         copy.start()
@@ -183,7 +184,7 @@
                 self.send(third, phase, None, self.at, (low[0], low[1] + high[1]), step)
 
     def arrive(self, phase):
-        drain(bulk(self.weights, (3, 12)[phase], self.group), self.recv_sem.at[self.group, phase, 6])
+        drain(bulk(self.weights, (3, 12)[phase], self.group), self.recv_sem.at[GATHER_SLOTS[self.group, phase]])
 
     def onward(self, phase, thirds_now=range(3)):
         for third in thirds_now:
@@ -195,7 +196,7 @@
             self.send(third, phase, 5, shifted(self.at, axis, 1), high, -1)
 
     def settle(self, phase):
-        drain(bulk(self.weights, (2, 8, 32)[phase], self.group), self.recv_sem.at[self.group, phase, 6])
+        drain(bulk(self.weights, (2, 8, 32)[phase], self.group), self.recv_sem.at[GATHER_SLOTS[self.group, phase]])
 
     def close(self):
         for phase in range(3):
@@ -219,7 +220,7 @@
         peer = lax.rem(self.c + d, 8)
         return remote(
             part(self.own.at[j], peer), self.unit.at[j, rows_of(self.c)],
-            self.send_sem.at[j], self.recv_sem.at[j, d - 1 if j == 2 else 0], (self.f, peer, self.t),
+            self.send_sem.at[j], self.recv_sem.at[j + (d - 1 if j == 2 else 0)], (self.f, peer, self.t),
         )
 
     def keep(self, j):
@@ -255,7 +256,7 @@
         c = self.c
         for j in range(2):
             self.keep(j).wait()
-            drain(seven(self.outcome), self.recv_sem.at[j, 0])
+            drain(seven(self.outcome), self.recv_sem.at[j])
         mask = key_mask(length, 0, 8 * ROWS)
         keys = self.unit[0]
         values_across = self.unit[1].T
@@ -356,7 +357,7 @@
     return jnp.where(slot < jnp.where(row < ROWS, lengths[0], lengths[1]), 1.0, 0.0)
 
 
-SLAB = 64
+SLAB = 128
 
 
 def slab_of(block):
@@ -398,13 +399,28 @@
     )
 
 
+SCATTER_GROUPS = ((QUERY, KEY), (KEY, OUT), (OUT, OUTER), (OUTER, WIDTH))
+SCATTER_TILES = (((1, 0), (1, 1), (1, 0)), ((1, 1), (2, 2), (1, 1)), *TILES[1:])
+DIRECT = (((0, 1, 2), (1, 2), (0, 1, 2)), ((1, 2),) * 3, ((2,),) * 3, ((2,),) * 3)
+SCATTER_SLOTS = {}
+SCATTER_COUNT = 0
+for _group in range(4):
+    for _third in range(3):
+        for _phase in range(3):
+            SCATTER_SLOTS[_group, _third, _phase] = SCATTER_COUNT
+            SCATTER_COUNT += 1 if _phase in DIRECT[_group][_third] else 4
+
+
 class Scatter:
     def __init__(self, work, group, landings, send_sem, recv_sem):
         self.at = place()
         self.work, self.group, self.landings = work, group, landings
         self.send_sem, self.recv_sem = send_sem, recv_sem
-        self.parts = thirds(group)
+        self.parts = thirds(group, SCATTER_GROUPS, SCATTER_TILES)
         self.sent = {}
+
+    def slot(self, third, phase, number):
+        return self.recv_sem.at[SCATTER_SLOTS[self.group, third, phase] + number]
 
     def ring(self, third, phase):
         order = ORDERS[third][::-1]
@@ -415,12 +431,12 @@
         land = self.landings[third][phase].at[kind]
         if cols[1] != land.shape[-1]:
             land = land.at[..., pl.ds(0, cols[1])]
-        slot = kind // 2 + 1 if kind > 1 else kind
-        if phase in DIRECT[self.group]:
-            slot = 0
+        number = kind // 2 + 1 if kind > 1 else kind
+        if phase in DIRECT[self.group][third]:
+            number = 0
         copy = remote(
             shards(self.work, shifted(self.at, axis, away), whole, cols), land,
-            self.send_sem.at[self.group, phase], self.recv_sem.at[self.group, phase, third, slot],
+            self.send_sem.at[self.group, phase], self.slot(third, phase, number),
             device(shifted(self.at, axis, step)),
         )
         copy.start()
@@ -462,6 +478,9 @@
             lax.fori_loop(0, 4, turn, 0)
 
     def first(self, phase, third, pieces=(0, 1)):
+        if phase in DIRECT[self.group][third]:
+            self.direct(phase, third)
+            return
         low, high = self.parts[third]
         if 0 in pieces:
             self.send(third, phase, 0, 2, low, 1)
@@ -477,10 +496,12 @@
 
     def arrive(self, phase, third):
         low, high = self.parts[third]
-        drain(self.landings[third][phase], self.recv_sem.at[self.group, phase, third, 0])
+        drain(self.landings[third][phase], self.slot(third, phase, 0))
         self.add(third, phase, 0, (low[0], low[1] + high[1]), (0, 1, 2))
 
     def onward(self, phase, third):
+        if phase in DIRECT[self.group][third]:
+            return
         low, high = self.parts[third]
         self.sent[third, phase, 0].wait_recv()
         self.add(third, phase, 1, low, (0,))
@@ -490,30 +511,30 @@
         self.send(third, phase, 5, -1, high, -1)
 
     def settle(self, phase, third):
+        if phase in DIRECT[self.group][third]:
+            self.arrive(phase, third)
+            return
         low, high = self.parts[third]
         axis, whole = self.ring(third, phase)
         block = shards(self.work, self.at, whole, (low[0], low[1] + high[1]))
         for slot in (2, 3):
-            drain(block, self.recv_sem.at[self.group, phase, third, slot])
+            drain(block, self.slot(third, phase, slot))
         self.add(third, phase, 0, high, (2, 5))
         self.add(third, phase, 0, low, (3, 4))
 
     def close(self):
         for phase in range(3):
-            drain(bulk(self.work, (48, 12, 3)[phase], self.group), self.send_sem.at[self.group, phase])
-
-
-DIRECT = ((1, 2), (2,), (2,))
+            drain(bulk(self.work, (48, 12, 3)[phase], self.group, SCATTER_GROUPS), self.send_sem.at[self.group, phase])
 
 
 def landing_shapes(group):
     shapes = []
     for third in range(3):
         order = ORDERS[third][::-1]
-        low, high = thirds(group)[third]
+        low, high = thirds(group, SCATTER_GROUPS, SCATTER_TILES)[third]
         for phase in range(3):
             whole = order[phase + 1 :]
-            direct = phase in DIRECT[group]
+            direct = phase in DIRECT[group][third]
             shape = [3 if direct else 6]
             shape += [2] if "x" in whole else []
             shape += [4] if "z" in whole else []
@@ -571,7 +592,7 @@
         peer = lax.rem(self.c + d, 8)
         return remote(
             self.sources[j].at[rows_of(peer)], part(self.grads.at[j], self.c),
-            self.back_send.at[j], self.back_recv.at[j, 0], (self.f, peer, self.t),
+            self.back_send.at[j], self.back_recv.at[j], (self.f, peer, self.t),
         )
 
     def keep_back(self, j):
@@ -597,16 +618,11 @@
         drain(seven(self.taken), self.recv_sem.at[0])
         for block in range(8):
             grad_buf[pl.ds(block * 256, 256), :] = by_head(self.taken[pl.ds(block * ROWS, ROWS), :])
-        head_row = lax.broadcasted_iota(jnp.int32, (8, LANES), 0)
-        head_lane = lax.broadcasted_iota(jnp.int32, (8, LANES), 1) // HEAD
-        chosen = jnp.where(head_row == head_lane, 1.0, 0.0)
-        weighted = lax.dot_general(
-            chosen, self.taken[...].astype(F32) * exact[...],
-            (((1,), (1,)), ((), ())), precision=lax.Precision.HIGHEST, preferred_element_type=F32,
-        )
+        turned = (self.taken[...].astype(F32) * exact[...]).T
+        weighted = [jnp.sum(turned[head * HEAD : head * HEAD + HEAD], 0, keepdims=True) for head in range(2)]
         delta = jnp.concatenate(
             [
-                weighted[head : head + 1, block * ROWS : (block + 1) * ROWS]
+                weighted[head][:, block * ROWS : (block + 1) * ROWS]
                 for block in range(8)
                 for head in range(2)
             ],
@@ -655,7 +671,7 @@
 
     def collect(self, j):
         self.keep_back(j).wait()
-        drain(seven(self.taken), self.back_recv.at[j, 0])
+        drain(seven(self.taken), self.back_recv.at[j])
 
     def close(self):
         drain(seven(self.taken), self.send_sem.at[0])
@@ -670,7 +686,7 @@
     )
 
 
-def weight_grad(work, start, left, right, width):
+def weight_grad(work, start, left, right, width, first=0):
     turned = left.T
     tile = 512
 
@@ -681,7 +697,7 @@
             put_quarter(work, quarter, start + offset, straight(turned[quarter * 256 : quarter * 256 + 256], term))
         return carry
 
-    lax.fori_loop(0, width // tile, turn, 0)
+    lax.fori_loop(first // tile, (first + width) // tile, turn, 0)
 
 
 def layers_kernel(
@@ -759,11 +775,11 @@
         heads.project(low[layer], weights, bias)
         if first:
             two.onward(2, (0, 2))
-            three.first(2, (0, 2))
             two.onward(2, (1,))
         heads.attend(length, exact.at[layer], logs.at[layer])
         if first:
-            three.onward(2)
+            three.first(2, (0, 2))
+            three.onward(2, (1,))
         heads.collect()
         if first:
             two.settle(2)
@@ -775,6 +791,8 @@
         join = new_join()
         for quarter in range(4):
             join.offer(quarter, across(mixed[layer], quarter_of(weights, quarter, OUT, 512)))
+        if first:
+            three.onward(2, (0, 2))
         join.wait()
 
         def after_attention(block, total):
@@ -850,12 +868,12 @@
 
     for item in gathers:
         item.close()
-    grouped = [landings[9 * group : 9 * group + 9] for group in range(3)]
-    one, two, three = (
+    grouped = [landings[9 * group : 9 * group + 9] for group in range(4)]
+    last_one, one, two, three = (
         Scatter(weights, group, [grouped[group][3 * i : 3 * i + 3] for i in range(3)], scatter_send, scatter_recv)
-        for group in range(3)
+        for group in range(4)
     )
-    closing = [one, two, three] + closing
+    closing = [last_one, one, two, three] + closing
     head_sum = [jnp.zeros((1, 512), F32)] * 2
     each = range(3)
     idle = lambda: None
@@ -895,10 +913,12 @@
         for quarter in range(4):
             join.offer(quarter, across(inner_grad[layer], quarter_of(weights, quarter, INNER, 2048)))
         if last:
-            weight_grad(weights, OUTER, outer_grad[...].reshape(512, 1024), act, 2048)
-            for third in (1, 0, 2):
-                three.first(0, third, (0,))
-            three.first(0, 1, (1,))
+            left = outer_grad[...].reshape(512, 1024)
+            weight_grad(weights, OUTER, left, act, 1536)
+            three.first(0, 1)
+            three.first(0, 0, (0,))
+            weight_grad(weights, OUTER, left, act, 512, 1536)
+            three.first(0, 2, (0,))
             weight_grad(weights, INNER, middle[...].reshape(512, 1024), inner_grad, 2048)
             two.first(0, 1)
         join.wait()
@@ -948,9 +968,9 @@
         left = low[...].reshape(512, 1024)
         if last:
             weight_grad(weights, KEY, left, grads.at[:, 0], 512)
-            one.first(0, 1)
             weight_grad(weights, VALUE, left, grads.at[:, 1], 512)
-            one.first(0, 2)
+            for third in (1, 0, 2):
+                one.first(0, third)
             for third in each:
                 three.settle(0, third)
                 three.first(1, third)
@@ -963,7 +983,8 @@
             )
         if last:
             weight_grad(weights, QUERY, left, grads.at[:, 2], 512)
-            one.first(0, 0)
+            for third in (1, 0, 2):
+                last_one.first(0, third)
             total_ref[1:2, 0:512] = head_sum[0]
             total_ref[1:2, 512:1024] = head_sum[1]
             count = sum(jnp.clip(lengths[s] - c * ROWS, 0, ROWS) for s in range(2)).astype(F32)
@@ -973,11 +994,16 @@
 
     totals = Totals(total_ref, total_land, total_send, total_recv)
     totals.first(0)
-    for third in each:
-        two.settle(0, third)
-        two.first(1, third)
-    for third in (1, 2, 0):
-        one.onward(0, third)
+
+    def settle(group, phase):
+        for third in (1, 0, 2):
+            group.settle(phase, third)
+            if phase < 2:
+                group.first(phase + 1, third)
+
+    settle(two, 0)
+    onward(one, 0)
+    onward(last_one, 0)
     onward(three, 1)
     join.wait()
     for s in range(2):
@@ -985,31 +1011,23 @@
         stream_grad[:, s, :] = trunk[rows, :] + join.total(rows)
     totals.settle(0)
     totals.first(1)
-    for third in (1, 2, 0):
-        one.settle(0, third)
-        one.direct(1, third)
+    settle(one, 0)
+    settle(last_one, 0)
     onward(two, 1)
-    for third in each:
-        three.settle(1, third)
-        three.direct(2, third)
+    settle(three, 1)
     result_ref[...] = jnp.stack([result[s * ROWS : s * ROWS + ROWS, :].astype(F32) for s in range(2)], 1).astype(BF16)
     totals.settle(1)
     totals.first(2)
-    for third in (1, 2, 0):
-        one.arrive(1, third)
-        one.direct(2, third)
-    for third in each:
-        two.settle(1, third)
-        two.direct(2, third)
-    for third in each:
-        three.arrive(2, third)
+    settle(one, 1)
+    settle(last_one, 1)
+    settle(two, 1)
+    settle(three, 2)
 
     def mine(start, width):
         return weights[x // 2, at["z"], x % 2, at["y"], :, start : start + width].astype(F32)
 
     outer_out[...] = mine(OUTER, 2048)
-    for third in each:
-        two.arrive(2, third)
+    settle(two, 2)
     output_out[...] = mine(OUT, 512)
     inner_out[...] = mine(INNER, 2048)
     vector_out[...] = mine(EXTRA, LANES).T[0:8, :]
@@ -1017,8 +1035,8 @@
     scale = 1.0 / (total_ref[1:2, 1024:1025] * 1024.0)
     square = jnp.sum(total_ref[:, 0:1024], 1, keepdims=True)
     root_ref[...] = jnp.broadcast_to(jnp.sqrt(square * scale + 1e-06), root_ref.shape)
-    for third in (1, 2, 0):
-        one.arrive(2, third)
+    settle(one, 2)
+    settle(last_one, 2)
     query_out[...] = mine(QUERY, 512)
     key_out[...] = mine(KEY, 512)
     value_out[...] = mine(VALUE, 512)
@@ -1073,9 +1091,9 @@
             vmem(F32, 3, 3, 8, 2048),
             dma((4,)),
             dma((3, 3)),
-            dma((3, 3, 7)),
+            dma((GATHER_COUNT,)),
             dma((3,)),
-            dma((3, 7)),
+            dma((9,)),
             dma((1,)),
             dma((1,)),
             dma((2,)),
@@ -1084,9 +1102,9 @@
             dma((1,)),
             dma((3,)),
             dma((3,)),
-            dma((3, 3)),
-            dma((3, 3, 3, 4)),
-            *(shape for group in range(3) for shape in landing_shapes(group)),
+            dma((4, 3)),
+            dma((SCATTER_COUNT,)),
+            *(shape for group in range(4) for shape in landing_shapes(group)),
         ],
         compiler_params=pltpu.CompilerParams(
             collective_id=3, has_side_effects=True, vmem_limit_bytes=LIMIT

time: 220 us -> 213 us (0.968)
  Pallas kernels: 219 us -> 212 us
    pallas_call x1, Pallas kernels: 216 us -> 209 us  [run_layers(): pl.pallas_call(layers_kernel, out_shape=(out(ROWS, 2, 1024), jax.ShapeDty...]
where the time goes in v5:
time: 213 us; the launch traced here: 212 us
  Pallas kernels  212 us (100%)
    pallas_call x1, Pallas kernels, run_layers(): pl.pallas_call(layers_kernel, out_shape=(out(ROWS, 2, 1024), jax.ShapeDty...  209 us

profile of v5, /device:TPU:0, one launch (start us, length us, event | category | flops | bytes accessed | tf_op | source)
XLA Modules:
  0.0 212.4 jit_solution(3261158738009559577)
XLA Ops:
  0.7 208.7 %layers.1 = (f32[128,2,1024]{2,1,0:T(2,128)}, bf16[128,2,1024]{2,1,0:T(2,128)(2,1)}, f32[16,512]{1,0:T(8,128)}, f32[16,512]{1,0:T(8,128)}, f32[16,512]{1,0:T(8,1...) custom-call(bf16[128,2,1024]{2,1,0:T(2,128)(2,1)} %stream.1, ...), custom_call_target="tpu_custom_call" | custom-call | tf_op jit(solution)/shard_map/layers/pallas_call | solution.py:1051
  209.3 2.9 %finish.1 = (bf16[128,2,1024]{2,1,0:T(2,128)(2,1)}, f32[128,2,1024]{2,1,0:T(2,128)}, f32[16,512]{1,0:T(8,128)}, f32[16,512]{1,0:T(8,128)}, f32[16,512]{1,0:T(8,1...) custom-call(f32[128,2,1024]{2,1,0:T(2,128)} %get-tuple-element.47.st, ...), custom_call_target="tpu_custom_call" | custom-call | tf_op jit(solution)/shard_map/finish/pallas_call | solution.py:1141

commit v6 on v5

--- a/solution.py
+++ b/solution.py
@@ -55,11 +55,11 @@
     return [device(shifted(at, axis, step)) for axis in "xyz" for step in steps]
 
 
-def context_peers():
+def far_peers():
     f = lax.axis_index("fsdp")
     c = lax.axis_index("context")
     t = lax.axis_index("tensor")
-    return [(f, lax.rem(c + d, 8), t) for d in range(1, 8)]
+    return [(f, (1 - c // 4) * 4 + y, t) for y in range(4)]
 
 
 def remote(src, dst, send_sem, recv_sem, device_id):
@@ -286,7 +286,7 @@
 
             return carry
 
-        lax.fori_loop(0, 8, step, 0)
+        lax.fori_loop(0, 8, step, 0, unroll=2)
         self.keep_back().start()
 
     def collect(self):
@@ -730,7 +730,7 @@
         weights, (x // 2, at["z"], x % 2, at["y"]), query, key, value, output, inner, outer,
         (bias0, bias1, gain1, shift1, gain2, shift2),
     )
-    greet(neighbours(at, (1, 2, 3)) + context_peers() + [partner])
+    greet(neighbours(at, (1, 2, 3)) + far_peers() + [partner])
     one, two, three = (Gather(weights, group, gather_send, gather_recv) for group in range(3))
     gathers = (one, two, three)
     for group in gathers:

time: 213 us -> 217 us (1.019)
  the two profiles are of different devices: /device:TPU:0 before, /device:TPU:1 now
where the time goes in v6:
time: 217 us; the launch traced here: 214 us
  Pallas kernels  213 us (98%)
    pallas_call x1, Pallas kernels, run_layers(): pl.pallas_call(layers_kernel, out_shape=(out(ROWS, 2, 1024), jax.ShapeDty...  210 us

profile of v6, /device:TPU:1, one launch (start us, length us, event | category | flops | bytes accessed | tf_op | source)
XLA Modules:
  0.0 214.0 jit_solution(52677786117819909)
XLA Ops:
  0.7 210.0 %layers.1 = (f32[128,2,1024]{2,1,0:T(2,128)}, bf16[128,2,1024]{2,1,0:T(2,128)(2,1)}, f32[16,512]{1,0:T(8,128)}, f32[16,512]{1,0:T(8,128)}, f32[16,512]{1,0:T(8,1...) custom-call(bf16[128,2,1024]{2,1,0:T(2,128)(2,1)} %stream.1, ...), custom_call_target="tpu_custom_call" | custom-call | tf_op jit(solution)/shard_map/layers/pallas_call | solution.py:1051
  210.6 2.9 %finish.1 = (bf16[128,2,1024]{2,1,0:T(2,128)(2,1)}, f32[128,2,1024]{2,1,0:T(2,128)}, f32[16,512]{1,0:T(8,128)}, f32[16,512]{1,0:T(8,128)}, f32[16,512]{1,0:T(8,1...) custom-call(f32[128,2,1024]{2,1,0:T(2,128)} %get-tuple-element.47.st, ...), custom_call_target="tpu_custom_call" | custom-call | tf_op jit(solution)/shard_map/finish/pallas_call | solution.py:1141
